TPU v7x, 512 devices: a whole 4x8x8 slice. The times are simulated.
512 devices in a mesh: dp: 64 (over y_hi, z, x), tensor: 8 (over y_lo, core).
Axes of the slice: x: 4, y: 8 (y_hi: 2, y_lo: 4; y = y_hi * 4 + y_lo), z: 8, core: 2. Of those that a mesh axis runs over, the one named last changes fastest.
Arguments:
- train_input: bfloat16 [16384, 5120], P('dp', 'tensor'), may hold values from -40 to 40
- train_preact: bfloat16 [16384, 20480], P('dp', 'tensor'), may hold values from -6 to 6
- train_upstream: bfloat16 [16384, 20480], P('dp', 'tensor'), may hold values from -6 to 6
- valid_input: bfloat16 [512, 5120], P('dp', 'tensor'), may hold values from -40 to 40
- valid_preact: bfloat16 [512, 20480], P('dp', 'tensor'), may hold values from -6 to 6
- valid_upstream: bfloat16 [512, 20480], P('dp', 'tensor'), may hold values from -6 to 6
Outputs:
- first_order: float32 [64, 2], P('dp')
- second_order: float32 [64], P('dp')
All inputs are finite; a program needn't handle non-finite values.
Results may differ from a plain program's by a relative error of at most 0.0044.
Values may be sent and summed in bfloat16 or wider, within the bound.
No kernel may reach another device: no remote copies, remote signals or barrier semaphores. Data moves between devices by JAX's collectives and lax.ppermute only.
A program may use at most 64 MiB of HBM per device.

v0:
```python
import math

import jax
import jax.numpy as jnp
from jax import lax
from jax.sharding import PartitionSpec as P

D = 5120
FF = 20480
SEQ_LEN = 256
VAL_SEQS = 2


inv_root_two = 0.7071067811865476
inv_root_tau = 0.3989422804014327


def output_grad(preact, upstream):
    preact_f = preact.astype(jnp.float32)
    derivative = (
        0.5 * (1.0 + lax.erf(preact_f * inv_root_two))
        + preact_f * jnp.exp(-0.5 * preact_f * preact_f) * inv_root_tau
    )
    return (upstream.astype(jnp.float32) * derivative).astype(jnp.bfloat16)


def cross_dot(left, right):
    return lax.dot_general(
        left, right, (((1,), (1,)), ((), ())), preferred_element_type=jnp.float32
    )


def per_device(
    train_input, train_preact, train_upstream, valid_input, valid_preact, valid_upstream
):
    train_grad = output_grad(train_preact, train_upstream)
    valid_grad = output_grad(valid_preact, valid_upstream)
    input_scale = 1.0 / math.sqrt(D)
    grad_scale = 1.0 / math.sqrt(FF)
    train_full, valid_full = (
        lax.all_gather(train_input, "tensor", axis=1, tiled=True),
        lax.all_gather(valid_input, "tensor", axis=1, tiled=True),
    )
    piece_input, piece_grad = lax.all_gather((valid_full, valid_grad), "dp", axis=0, tiled=True)
    input_part = cross_dot(train_full, piece_input) * input_scale
    grad_part = cross_dot(train_grad, piece_grad) * grad_scale
    stacked = jnp.stack([input_part, grad_part])
    input_kernel = stacked[0]
    grad_part = stacked[1]
    row_count = input_kernel.shape[0]
    grad_kernel = lax.psum(grad_part, "tensor")
    seq_sums = jnp.sum((input_kernel * grad_kernel).reshape(row_count, VAL_SEQS, SEQ_LEN), axis=2)
    first_order = jnp.sum(seq_sums.reshape(row_count // SEQ_LEN, SEQ_LEN, VAL_SEQS), axis=1) * (
        1.0 / SEQ_LEN
    )
    weight = lax.psum(jnp.sum(first_order, axis=0), "dp")
    second_order = jnp.sum(first_order * weight[None, :], axis=1)
    return (first_order, second_order)


def solution(mesh):
    return jax.shard_map(
        per_device,
        mesh=mesh,
        in_specs=(
            P("dp", "tensor"),
            P("dp", "tensor"),
            P("dp", "tensor"),
            P("dp", "tensor"),
            P("dp", "tensor"),
            P("dp", "tensor"),
        ),
        out_specs=(P("dp", None), P("dp")),
        check_vma=False,
    )
```

profile of v0, /device:TPU:32, one launch (start us, length us, event | category | flops | bytes accessed | tf_op | source)
XLA Modules:
  0.0 675.8 jit_solution(3046502768688299123)
XLA Ops:
  7.2 0.0 all-gather.8.cloned.1.call-start
  7.2 1.5 fusion.22
  8.7 0.0 all-gather.8.cloned.1.call-update
  8.7 0.0 all-gather.4.cloned.1.call-start
  8.7 0.7 all-gather.4.cloned.1.call-update
  9.4 0.0 copy-start
  9.4 0.0 all-reduce.2.cloned.1.call-start
  9.5 138.6 %all-gather.8.cloned.1.call-done = bf16[512,2560]{1,0:T(8,128)(2,1)} async-done(((bf16[8,2560]{1,0:T(8,128)(2,1)}), bf16[512,2560]{1,0:T(8,128)(2,1)}) %all-gather.8.cloned.1.call-update) | async-done | bytes 2621456 | tf_op jit(solution)/shard_map/all_gather | solution.py:44
  148.1 4.8 fusion.11
  152.9 0.0 all-reduce.2.cloned.1.call-update
  152.9 0.0 all-gather.6.cloned.1.call-start
  152.9 0.0 copy-done
  153.0 20.4 %all_gather.13 = bf16[8,5120]{1,0:T(8,128)(2,1)} all-gather(bf16[8,640]{1,0:T(8,128)(2,1)S(1)} %copy-done), channel_id=1, replica_groups=mesh['dp'=64,'tensor'=8] {'tensor'}, dimensions={1}, use_global_device_ids=true | all-gather | bytes 92160 | tf_op jit(solution)/shard_map/all_gather | solution.py:42
  173.3 0.0 all-gather.6.cloned.1.call-update
  173.3 22.4 %all-gather.4.cloned.1.call-done = bf16[256,5120]{1,0:T(8,128)(2,1)} async-done(((bf16[256,640]{1,0:T(8,128)(2,1)}), bf16[256,5120]{1,0:T(8,128)(2,1)}) %all-gather.4.cloned.1.call-update) | async-done | bytes 2621456 | tf_op jit(solution)/shard_map/all_gather | solution.py:41
  195.8 79.1 %all-reduce.2.cloned.1.call-done = f32[256,512]{1,0:T(8,128)} async-done(((f32[256,512]{1,0:T(8,128)}), f32[256,512]{1,0:T(8,128)}) %all-reduce.2.cloned.1.call-update) | async-done | bytes 524304 | tf_op jit(solution)/shard_map/psum | solution.py:51
  274.8 156.9 %all-gather.6.cloned.1.call-done = bf16[512,5120]{1,0:T(8,128)(2,1)} async-done(((bf16[8,5120]{1,0:T(8,128)(2,1)}), bf16[512,5120]{1,0:T(8,128)(2,1)}) %all-gather.6.cloned.1.call-update) | async-done | bytes 5242896 | tf_op jit(solution)/shard_map/all_gather | solution.py:44
  431.8 4.9 fusion.14
  436.7 0.1 reduce_sum.37
  436.8 231.3 %psum.15 = f32[2]{0:T(128)S(1)} all-reduce(f32[2]{0:T(128)S(1)} %broadcast_multiply_fusion), channel_id=1, replica_groups=mesh['dp'=64,'tensor'=8] {'dp'}, use_global_device_ids=true, to_apply=%region_3.0 | all-reduce | flops 2 | bytes 16 | tf_op jit(solution)/shard_map/psum | solution.py:56
  668.2 1.1 multiply_reduce_fusion
  (2 shorter events, 0.0 us)
Async XLA Ops:
  7.2 140.9 %all-gather.8.cloned.1.call-start = ((), (), s32[]{:S(2)}) async-start(), calls=%async_computation.2 | async-start | bytes 2662400 | tf_op jit(solution)/shard_map/all_gather | solution.py:44
  8.7 187.1 %all-gather.4.cloned.1.call-start = ((), (), s32[]{:S(2)}) async-start(), calls=%async_computation | async-start | bytes 2949120 | tf_op jit(solution)/shard_map/all_gather | solution.py:41
  9.4 143.5 %copy-start = (bf16[8,640]{1,0:T(8,128)(2,1)S(1)}, bf16[8,640]{1,0:T(8,128)(2,1)}, u32[]{:S(2)}) copy-start(bf16[8,640]{1,0:T(8,128)(2,1)} %param.9) | copy-start | bytes 30724
  9.4 265.4 %all-reduce.2.cloned.1.call-start = ((), (), s32[]{:S(2)}) async-start(), calls=%async_computation.3 | async-start | bytes 1048576 | tf_op jit(solution)/shard_map/psum | solution.py:51
  152.9 278.9 %all-gather.6.cloned.1.call-start = ((), (), s32[]{:S(2)}) async-start(), calls=%async_computation.1 | async-start | bytes 5324800 | tf_op jit(solution)/shard_map/all_gather | solution.py:44
Sparse Core Ops, SparseCore 0:
  12.5 135.5 all-gather.7
  150.2 45.5 all-gather.3
  198.7 76.0 all-reduce.1
  279.8 151.8 all-gather.5
where the time goes:
time: 676 us
  waiting for transfers between devices  398 us (59%)
  blocking collectives  252 us (37%)
  between operations  13.8 us (2%)
  matrix products  9.69 us (1%)
    all_gather x2, waiting for transfers between devices, per_device(): lax.all_gather((valid_full, valid_grad), 'dp', axis=0, tiled=True)  295 us
    psum x1, blocking collectives, per_device(): weight = lax.psum(jnp.sum(first_order, axis=0), 'dp')  231 us
    psum x1, waiting for transfers between devices, per_device(): grad_kernel = lax.psum(grad_part, 'tensor')  79.1 us
    all_gather x1, waiting for transfers between devices, per_device(): lax.all_gather(train_input, 'tensor', axis=1, tiled=True)  22.4 us
    all_gather x1, blocking collectives, per_device(): lax.all_gather(valid_input, 'tensor', axis=1, tiled=True)  20.4 us
  transfers between devices with their start and end apart: 4, of which 4 were waited for; matrix products, arithmetic and copies ran while one was open for 1% of the time, Pallas kernels for 0%

commit v1 on v0

v1 whole, which is shorter than its diff:
```python
import math

import jax
import jax.numpy as jnp
from jax import lax
from jax.sharding import Mesh, PartitionSpec as P

D = 5120
FF = 20480
SEQ_LEN = 256
VAL_SEQS = 2
DP = ("yh", "z", "x")
TENSOR = ("yl", "core")
SIZES = (2, 8, 4, 4, 2)

inv_root_two = 0.7071067811865476
inv_root_tau = 0.3989422804014327


def output_grad(preact, upstream):
    preact_f = preact.astype(jnp.float32)
    derivative = (
        0.5 * (1.0 + lax.erf(preact_f * inv_root_two))
        + preact_f * jnp.exp(-0.5 * preact_f * preact_f) * inv_root_tau
    )
    return (upstream.astype(jnp.float32) * derivative).astype(jnp.bfloat16)


def cross_dot(left, right):
    return lax.dot_general(
        left, right, (((1,), (1,)), ((), ())), preferred_element_type=jnp.float32
    )


def exchange(value, axes):
    return lax.all_to_all(value, axes, 0, 0, tiled=True)


def per_device(
    train_input, train_preact, train_upstream, valid_input, valid_preact, valid_upstream
):
    valid_grad = output_grad(valid_preact, valid_upstream)
    valid = jnp.concatenate([valid_input, valid_grad], axis=1)
    rows, width = valid.shape
    dp = lax.axis_size(DP)
    valid_all = jnp.broadcast_to(valid[None], (dp, rows, width)).reshape(dp * rows, width)
    valid_all = exchange(valid_all, DP)
    train_grad = output_grad(train_preact, train_upstream)
    split = valid_input.shape[1]
    input_part = cross_dot(train_input, valid_all[:, :split]) * (1.0 / math.sqrt(D))
    grad_part = cross_dot(train_grad, valid_all[:, split:]) * (1.0 / math.sqrt(FF))
    parts = jnp.concatenate([input_part, grad_part], axis=1)
    tensor = lax.axis_size(TENSOR)
    count, wide = parts.shape
    parts = exchange(parts, TENSOR).reshape(tensor, count // tensor, wide)
    parts = jnp.sum(parts, axis=0)
    product = parts[:, : wide // 2] * parts[:, wide // 2 :]
    sums = jnp.sum(product.reshape(-1, VAL_SEQS, SEQ_LEN), axis=(0, 2)) * (1.0 / SEQ_LEN)
    lanes = jnp.pad(sums, (0, 128 - VAL_SEQS))[None]
    halves = lax.axis_size("yh")
    column = exchange(jnp.broadcast_to(lanes, (halves * tensor, 128)), ("yh",) + TENSOR)
    by_half = jnp.sum(column.reshape(halves, tensor, 128), axis=1)
    first_order = lax.dynamic_slice(by_half, (lax.axis_index("yh"), 0), (1, VAL_SEQS))
    total = jnp.sum(by_half, axis=0, keepdims=True)
    plane = lax.axis_size(("z", "x"))
    planes = exchange(jnp.broadcast_to(total, (plane, 128)), ("z", "x"))
    weight = jnp.sum(planes, axis=0, keepdims=True)[:, :VAL_SEQS]
    second_order = jnp.sum(first_order * weight, axis=1)
    return (first_order, second_order)


def solution(mesh):
    fine = Mesh(mesh.devices.reshape(SIZES), DP + TENSOR)
    return jax.shard_map(
        per_device,
        mesh=fine,
        in_specs=(P(DP, TENSOR),) * 6,
        out_specs=(P(DP, None), P(DP)),
        check_vma=False,
    )
```

time: 676 us -> 171 us (0.25)
  the two profiles are of different devices: /device:TPU:32 before, /device:TPU:1 now
where the time goes in v1:
time: 171 us; the launch traced here: 170 us
  blocking collectives  131 us (77%)
  starting transfers between devices  16.5 us (10%)
  waiting for transfers between devices  15.6 us (9%)
  other arithmetic  3.06 us (2%)
  matrix products  2.02 us (1%)
  local copies, waits for them, and re-layouts  1.81 us (1%)
    all_to_all x2, blocking collectives, exchange(): return lax.all_to_all(value, axes, 0, 0, tiled=True)  131 us
    all_to_all x2, starting transfers between devices, exchange(): return lax.all_to_all(value, axes, 0, 0, tiled=True)  16.5 us
    all_to_all x2, waiting for transfers between devices, exchange(): return lax.all_to_all(value, axes, 0, 0, tiled=True)  15.6 us
  transfers between devices with their start and end apart: 2, of which 2 were waited for; matrix products, arithmetic and copies ran while one was open for 0% of the time, Pallas kernels for 0%

profile of v1, /device:TPU:1, one launch (start us, length us, event | category | flops | bytes accessed | tf_op | source)
XLA Modules:
  0.0 170.4 jit_solution(9744460925649569777)
XLA Ops:
  0.6 0.0 copy-start
  0.6 0.9 fusion.30
  1.5 0.7 pad_maximum_fusion.1
  2.2 0.2 broadcast_in_dim.8
  2.5 0.0 copy-start.1
  2.5 0.0 copy-start.2
  2.5 91.6 %all_to_all.30 = bf16[64,8,3200]{2,1,0:T(8,128)(2,1)S(1)} all-to-all(bf16[64,8,3200]{2,1,0:T(8,128)(2,1)S(1)} %broadcast_in_dim.8), channel_id=1, replica_groups=mesh['yh'=2,'z'=8,'x'=4,'yl'=4,'core'=2] {'yh','z','x'}, dimensions={0} | all-to-all | bytes 6553600 | tf_op jit(solution)/shard_map/all_to_all | solution.py:36
  94.1 0.0 copy-done
  94.1 0.4 fusion.16
  94.5 0.0 copy-done.1
  94.5 0.0 copy-done.2
  94.6 1.6 fusion.17
  96.2 0.1 pad_maximum_fusion
  96.3 0.3 copy.14
  96.6 39.1 %all_to_all.31 = f32[8,32,1024]{2,1,0:T(8,128)S(1)} all-to-all(f32[8,32,1024]{2,1,0:T(8,128)S(1)} %bitcast.12), channel_id=1, replica_groups=mesh['yh'=2,'z'=8,'x'=4,'yl'=4,'core'=2] {'yl','core'}, dimensions={0} | all-to-all | bytes 2097152 | tf_op jit(solution)/shard_map/all_to_all | solution.py:36
  135.7 0.1 reduce_sum.63
  135.8 0.1 reduce_sum.66
  135.9 0.6 broadcast_in_dim.9
  136.5 6.3 %all-to-all-start.2 = ((f32[16,1,128]{2,1,0:T(1,128)}), f32[16,1,128]{2,1,0:T(1,128)S(1)}, u32[]{:S(2)}, u32[]{:S(2)}) async-start(f32[16,1,128]{2,1,0:T(1,128)} %broadcast_in_dim.9), calls=%async_computation.2 | async-start | bytes 16384 | tf_op jit(solution)/shard_map/all_to_all | solution.py:36
  142.8 7.0 %all-to-all-done.2 = f32[16,1,128]{2,1,0:T(1,128)S(1)} async-done(((f32[16,1,128]{2,1,0:T(1,128)}), f32[16,1,128]{2,1,0:T(1,128)S(1)}, u32[]{:S(2)}, u32[]{:S(2)}) %all-to-all-start.2) | async-done | bytes 8224 | tf_op jit(solution)/shard_map/all_to_all | solution.py:36
  149.8 0.6 broadcast_in_dim.10
  150.4 10.2 %all-to-all-start.3 = ((f32[32,1,128]{2,1,0:T(1,128)}), f32[32,1,128]{2,1,0:T(1,128)S(1)}, u32[]{:S(2)}, u32[]{:S(2)}) async-start(f32[32,1,128]{2,1,0:T(1,128)} %broadcast_in_dim.10), calls=%async_computation.3 | async-start | bytes 32768 | tf_op jit(solution)/shard_map/all_to_all | solution.py:36
  160.7 8.6 %all-to-all-done.3 = f32[32,1,128]{2,1,0:T(1,128)S(1)} async-done(((f32[32,1,128]{2,1,0:T(1,128)}), f32[32,1,128]{2,1,0:T(1,128)S(1)}, u32[]{:S(2)}, u32[]{:S(2)}) %all-to-all-start.3) | async-done | bytes 16416 | tf_op jit(solution)/shard_map/all_to_all | solution.py:36
  169.3 1.1 multiply_reduce_fusion
  (7 shorter events, 0.1 us)
Async XLA Ops:
  0.6 93.5 %copy-start = (bf16[256,640]{1,0:T(8,128)(2,1)S(1)}, bf16[256,640]{1,0:T(8,128)(2,1)}, u32[]{:S(2)}) copy-start(bf16[256,640]{1,0:T(8,128)(2,1)} %param.6) | copy-start | bytes 983044
  2.5 92.1 %copy-start.1 = (bf16[256,2560]{1,0:T(8,128)(2,1)S(1)}, bf16[256,2560]{1,0:T(8,128)(2,1)}, u32[]{:S(2)}) copy-start(bf16[256,2560]{1,0:T(8,128)(2,1)} %param.7) | copy-start | bytes 3932164
  2.5 92.1 %copy-start.2 = (bf16[256,2560]{1,0:T(8,128)(2,1)S(1)}, bf16[256,2560]{1,0:T(8,128)(2,1)}, u32[]{:S(2)}) copy-start(bf16[256,2560]{1,0:T(8,128)(2,1)} %param.8) | copy-start | bytes 3932164
  136.5 13.3 %all-to-all-start.2 = ((f32[16,1,128]{2,1,0:T(1,128)}), f32[16,1,128]{2,1,0:T(1,128)S(1)}, u32[]{:S(2)}, u32[]{:S(2)}) async-start(f32[16,1,128]{2,1,0:T(1,128)} %broadcast_in_dim.9), calls=%async_computation.2 | async-start | bytes 16384 | tf_op jit(solution)/shard_map/all_to_all | solution.py:36
  150.4 18.8 %all-to-all-start.3 = ((f32[32,1,128]{2,1,0:T(1,128)}), f32[32,1,128]{2,1,0:T(1,128)S(1)}, u32[]{:S(2)}, u32[]{:S(2)}) async-start(f32[32,1,128]{2,1,0:T(1,128)} %broadcast_in_dim.10), calls=%async_computation.3 | async-start | bytes 32768 | tf_op jit(solution)/shard_map/all_to_all | solution.py:36

commit v2 on v1

v2 whole, which is shorter than its diff:
```python
import math

import jax
import jax.numpy as jnp
from jax import lax
from jax.sharding import Mesh, PartitionSpec as P

D = 5120
FF = 20480
SEQ_LEN = 256
VAL_SEQS = 2
DP = ("yh", "z", "x")
TENSOR = ("yl", "core")
YH, Z, X, YL, CORE = SIZES = (2, 8, 4, 4, 2)
CLASSES = 4

inv_root_two = 0.7071067811865476
inv_root_tau = 0.3989422804014327


def output_grad(preact, upstream):
    preact_f = preact.astype(jnp.float32)
    derivative = (
        0.5 * (1.0 + lax.erf(preact_f * inv_root_two))
        + preact_f * jnp.exp(-0.5 * preact_f * preact_f) * inv_root_tau
    )
    return (upstream.astype(jnp.float32) * derivative).astype(jnp.bfloat16)


def cross_dot(left, right):
    return lax.dot_general(
        left, right, (((1,), (1,)), ((), ())), preferred_element_type=jnp.float32
    )


def exchange(value, axes, groups=None):
    return lax.all_to_all(value, axes, 0, 0, axis_index_groups=groups, tiled=True)


def place(yh, z, x):
    return (yh * Z + z % Z) * X + x % X


def class_groups():
    return [
        [place(yh, z, kind - 2 * z) for yh in range(YH) for z in range(Z)]
        for kind in range(CLASSES)
    ]


def shift(value, dz, dx):
    pairs = [
        (place(yh, z, x), place(yh, z + dz, x + dx))
        for yh in range(YH)
        for z in range(Z)
        for x in range(X)
    ]
    return lax.ppermute(value, DP, pairs)


def gather_valid(valid):
    rows, width = valid.shape
    members = YH * Z
    own = jnp.broadcast_to(valid[None], (members, rows, width)).reshape(members * rows, width)
    own = exchange(own, DP, class_groups())
    half = own.shape[0] // 2
    return [
        own,
        shift(own, 0, 1),
        shift(own, 0, -1),
        shift(own[:half], 1, 0),
        shift(own[half:], -1, 0),
    ]


def per_device(
    train_input, train_preact, train_upstream, valid_input, valid_preact, valid_upstream
):
    valid_grad = output_grad(valid_preact, valid_upstream)
    blocks = gather_valid(jnp.concatenate([valid_input, valid_grad], axis=1))
    train_grad = lax.optimization_barrier(output_grad(train_preact, train_upstream))
    split = valid_input.shape[1]
    input_parts = [cross_dot(train_input, b[:, :split]) * (1.0 / math.sqrt(D)) for b in blocks]
    grad_parts = [cross_dot(train_grad, b[:, split:]) * (1.0 / math.sqrt(FF)) for b in blocks]
    parts = jnp.concatenate(input_parts + grad_parts, axis=1)
    count, wide = parts.shape
    core = lax.axis_index("core")
    part_rows = count // CORE
    kept = lax.dynamic_slice(parts, (core * part_rows, 0), (part_rows, wide))
    sent = lax.dynamic_slice(parts, ((1 - core) * part_rows, 0), (part_rows, wide))
    parts = kept + lax.ppermute(sent, "core", [(0, 1), (1, 0)])
    parts = exchange(parts, "yl").reshape(YL, part_rows // YL, wide)
    parts = jnp.sum(parts, axis=0)
    product = jnp.sum(parts[:, : wide // 2] * parts[:, wide // 2 :], axis=0)
    edge = blocks[0].shape[0] // 2
    sums = jnp.sum(product.reshape(-1, VAL_SEQS, edge), axis=(0, 2)) * (1.0 / SEQ_LEN)
    lanes = jnp.pad(sums, (0, 128 - VAL_SEQS))[None]
    tensor = YL * CORE
    column = exchange(jnp.broadcast_to(lanes, (YH * tensor, 128)), ("yh",) + TENSOR)
    by_half = jnp.sum(column.reshape(YH, tensor, 128), axis=1)
    first_order = lax.dynamic_slice(by_half, (lax.axis_index("yh"), 0), (1, VAL_SEQS))
    total = jnp.sum(by_half, axis=0, keepdims=True)
    plane = Z * X
    planes = exchange(jnp.broadcast_to(total, (plane, 128)), ("z", "x"))
    weight = jnp.sum(planes, axis=0, keepdims=True)[:, :VAL_SEQS]
    second_order = jnp.sum(first_order * weight, axis=1)
    return (first_order, second_order)


def solution(mesh):
    fine = Mesh(mesh.devices.reshape(SIZES), DP + TENSOR)
    return jax.shard_map(
        per_device,
        mesh=fine,
        in_specs=(P(DP, TENSOR),) * 6,
        out_specs=(P(DP, None), P(DP)),
        check_vma=False,
    )
```

time: 171 us -> 131 us (0.77)
  blocking collectives: 131 us -> 23.5 us
  starting transfers between devices: 16.5 us -> 52.7 us
  waiting for transfers between devices: 15.6 us -> 41.7 us
  other arithmetic: 3.06 us -> 5.59 us
  matrix products: 2.02 us -> 3.84 us
    all_to_all x2 -> x1, blocking collectives: 131 us -> 23.5 us  [exchange(): lax.all_to_all(value, axes, 0, 0, axis_index_groups=groups, tiled=True)]
    ppermute x0 -> x5, starting transfers between devices: none -> 19.9 us  [the longest x4 13 us: shift(): return lax.ppermute(value, DP, pairs)]
    all_to_all x2 -> x3, waiting for transfers between devices: 15.6 us -> 33.8 us  [exchange(): lax.all_to_all(value, axes, 0, 0, axis_index_groups=groups, tiled=True)]
    all_to_all x2 -> x3, starting transfers between devices: 16.5 us -> 32.8 us  [exchange(): lax.all_to_all(value, axes, 0, 0, axis_index_groups=groups, tiled=True)]
    ppermute x0 -> x5, waiting for transfers between devices: none -> 7.89 us  [the longest x4 6.38 us: shift(): return lax.ppermute(value, DP, pairs)]
    convert_element_type x1 -> x2, other arithmetic: 0.89 us -> 3.45 us  [output_grad(): return (upstream.astype(jnp.float32) * derivative).astype(jnp.bfloat16)]
    dot_general x2 -> x10, matrix products: 2.02 us -> 3.84 us  [cross_dot(): lax.dot_general(left, right, (((1,), (1,)), ((), ())), preferred_element_...]
  transfers between devices with their start and end apart: 2 -> 8, of which waited for: 2 -> 6; matrix products, arithmetic and copies ran while one was open for 0% -> 3% of each run, Pallas kernels for 0% -> 0%
where the time goes in v2:
time: 131 us
  starting transfers between devices  52.7 us (40%)
  waiting for transfers between devices  41.7 us (32%)
  blocking collectives  23.5 us (18%)
  other arithmetic  5.59 us (4%)
  matrix products  3.84 us (3%)
  local copies, waits for them, and re-layouts  2.55 us (2%)
    all_to_all x3, waiting for transfers between devices, exchange(): lax.all_to_all(value, axes, 0, 0, axis_index_groups=groups, tiled=True)  33.8 us
    all_to_all x3, starting transfers between devices, exchange(): lax.all_to_all(value, axes, 0, 0, axis_index_groups=groups, tiled=True)  32.8 us
    all_to_all x1, blocking collectives, exchange(): lax.all_to_all(value, axes, 0, 0, axis_index_groups=groups, tiled=True)  23.5 us
    ppermute x4, starting transfers between devices, shift(): return lax.ppermute(value, DP, pairs)  13 us
    ppermute x1, starting transfers between devices, per_device(): parts = kept + lax.ppermute(sent, 'core', [(0, 1), (1, 0)])  6.89 us
    ppermute x4, waiting for transfers between devices, shift(): return lax.ppermute(value, DP, pairs)  6.38 us
    dot_general x10, matrix products, cross_dot(): lax.dot_general(left, right, (((1,), (1,)), ((), ())), preferred_element_...  3.84 us
    convert_element_type x2, other arithmetic, output_grad(): return (upstream.astype(jnp.float32) * derivative).astype(jnp.bfloat16)  3.45 us
  transfers between devices with their start and end apart: 8, of which 6 were waited for; matrix products, arithmetic and copies ran while one was open for 3% of the time, Pallas kernels for 0%

profile of v2, /device:TPU:1, one launch (start us, length us, event | category | flops | bytes accessed | tf_op | source)
XLA Modules:
  0.0 130.7 jit_solution(10476293635160990550)
XLA Ops:
  0.6 0.9 fusion.40
  1.5 0.7 pad_maximum_fusion
  2.2 0.9 broadcast_in_dim.8
  3.2 18.7 %all-to-all-start = ((bf16[16,8,3200]{2,1,0:T(8,128)(2,1)}), bf16[16,8,3200]{2,1,0:T(8,128)(2,1)S(1)}, u32[]{:S(2)}, u32[]{:S(2)}) async-start(bf16[16,8,3200]{2,1,0:T(8,128)(2,1)} %broadcast_in_dim.8), calls=%async_computation | async-start | bytes 1638400 | tf_op jit(solution)/shard_map/all_to_all | solution.py:37
  21.9 2.6 %fusion.7 = bf16[256,2560]{1,0:T(8,128)(2,1)S(1)} fusion(bf16[256,2560]{1,0:T(8,128)(2,1)} %param.7, bf16[256,2560]{1,0:T(8,128)(2,1)} %param.8), kind=kLoop, calls=%fused_computation.11 | loop fusion | flops 7864320 | bytes 3932160 | tf_op jit(solution)/shard_map/convert_element_type | solution.py:27
  24.5 18.1 %all-to-all-done = bf16[16,8,3200]{2,1,0:T(8,128)(2,1)S(1)} async-done(((bf16[16,8,3200]{2,1,0:T(8,128)(2,1)}), bf16[16,8,3200]{2,1,0:T(8,128)(2,1)S(1)}, u32[]{:S(2)}, u32[]{:S(2)}) %all-to-all-start) | async-done | bytes 819232 | tf_op jit(solution)/shard_map/all_to_all | solution.py:37
  42.6 2.2 %collective-permute-start = (bf16[128,3200]{1,0:T(8,128)(2,1)S(1)}, bf16[128,3200]{1,0:T(8,128)(2,1)S(1)}, u32[]{:S(2)}, u32[]{:S(2)}) collective-permute-start(bf16[128,3200]{1,0:T(8,128)(2,1)S(1)} %bitcast.43), channel_id=1, source_target_pairs={{0,8},{8,16},{16,24},{24,0},{32,40},{40,48},{48,56},{56,32},{64,72... | collective-permute-start | bytes 2457608 | tf_op jit(solution)/shard_map/ppermute | solution.py:58
  44.8 4.3 %collective-permute-start.1 = (bf16[128,3200]{1,0:T(8,128)(2,1)S(1)}, bf16[128,3200]{1,0:T(8,128)(2,1)S(1)}, u32[]{:S(2)}, u32[]{:S(2)}) collective-permute-start(bf16[128,3200]{1,0:T(8,128)(2,1)S(1)} %bitcast.44), channel_id=1, source_target_pairs={{0,24},{8,0},{16,8},{24,16},{32,56},{40,32},{48,40},{56,48},{64,88... | collective-permute-start | bytes 2457608 | tf_op jit(solution)/shard_map/ppermute | solution.py:58
  49.2 2.7 %collective-permute-start.2 = (bf16[64,3200]{1,0:T(8,128)(2,1)S(1)}, bf16[64,3200]{1,0:T(8,128)(2,1)S(1)}, u32[]{:S(2)}, u32[]{:S(2)}) collective-permute-start(bf16[64,3200]{1,0:T(8,128)(2,1)S(1)} %get-tuple-element.5), channel_id=1, source_target_pairs={{0,32},{8,40},{16,48},{24,56},{32,64},{40,72},{48,80},{56,88},{64,... | collective-permute-start | bytes 1228808 | tf_op jit(solution)/shard_map/ppermute | solution.py:58
  51.9 3.8 %collective-permute-start.3 = (bf16[64,3200]{1,0:T(8,128)(2,1)S(1)}, bf16[64,3200]{1,0:T(8,128)(2,1)S(1)}, u32[]{:S(2)}, u32[]{:S(2)}) collective-permute-start(bf16[64,3200]{1,0:T(8,128)(2,1)S(1)} %get-tuple-element.4), channel_id=1, source_target_pairs={{0,224},{8,232},{16,240},{24,248},{32,0},{40,8},{48,16},{56,24},{6... | collective-permute-start | bytes 1228808 | tf_op jit(solution)/shard_map/ppermute | solution.py:58
  55.9 5.4 %collective-permute-done = bf16[128,3200]{1,0:T(8,128)(2,1)S(1)} collective-permute-done((bf16[128,3200]{1,0:T(8,128)(2,1)S(1)}, bf16[128,3200]{1,0:T(8,128)(2,1)S(1)}, u32[]{:S(2)}, u32[]{:S(2)}) %collective-permute-start) | collective-permute-done | bytes 819232 | tf_op jit(solution)/shard_map/ppermute | solution.py:58
  61.6 1.0 collective-permute-done.1
  63.3 0.6 fusion.16
  63.8 0.5 fusion.15
  66.0 6.9 %collective-permute-start.4 = (f32[128,1024]{0,1:T(8,128)S(1)}, f32[128,1024]{0,1:T(8,128)S(1)}, u32[]{:S(2)}, u32[]{:S(2)}) collective-permute-start(f32[128,1024]{0,1:T(8,128)S(1)} %constant_dynamic-slice_fusion.1), channel_id=1, source_target_pairs={{0,1},{1,0},{2,3},{3,2},{4,5},{5,4},{6,7},{7,6},{8,9},{9,8},{10,11... | collective-permute-start | bytes 1572872 | tf_op jit(solution)/shard_map/ppermute | solution.py:91
  73.0 1.5 %collective-permute-done.4 = f32[128,1024]{0,1:T(8,128)S(1)} collective-permute-done((f32[128,1024]{0,1:T(8,128)S(1)}, f32[128,1024]{0,1:T(8,128)S(1)}, u32[]{:S(2)}, u32[]{:S(2)}) %collective-permute-start.4) | collective-permute-done | bytes 524320 | tf_op jit(solution)/shard_map/ppermute | solution.py:91
  74.7 23.5 %all_to_all.30 = f32[4,32,1024]{2,1,0:T(8,128)S(1)} all-to-all(f32[4,32,1024]{2,1,0:T(8,128)S(1)} %bitcast.47), channel_id=1, replica_groups=mesh['yh'=2,'z'=8,'x'=4,'yl'=4,'core'=2] {'yl'}, dimensions={0} | all-to-all | bytes 1048576 | tf_op jit(solution)/shard_map/all_to_all | solution.py:37
  98.6 0.6 broadcast_in_dim.9
  99.2 4.7 %all-to-all-start.2 = ((f32[16,1,128]{2,1,0:T(1,128)}), f32[16,1,128]{2,1,0:T(1,128)S(1)}, u32[]{:S(2)}, u32[]{:S(2)}) async-start(f32[16,1,128]{2,1,0:T(1,128)} %broadcast_in_dim.9), calls=%async_computation.2 | async-start | bytes 16384 | tf_op jit(solution)/shard_map/all_to_all | solution.py:37
  103.9 7.1 %all-to-all-done.2 = f32[16,1,128]{2,1,0:T(1,128)S(1)} async-done(((f32[16,1,128]{2,1,0:T(1,128)}), f32[16,1,128]{2,1,0:T(1,128)S(1)}, u32[]{:S(2)}, u32[]{:S(2)}) %all-to-all-start.2) | async-done | bytes 8224 | tf_op jit(solution)/shard_map/all_to_all | solution.py:37
  110.9 0.6 broadcast_in_dim.10
  111.5 9.4 %all-to-all-start.3 = ((f32[32,1,128]{2,1,0:T(1,128)}), f32[32,1,128]{2,1,0:T(1,128)S(1)}, u32[]{:S(2)}, u32[]{:S(2)}) async-start(f32[32,1,128]{2,1,0:T(1,128)} %broadcast_in_dim.10), calls=%async_computation.3 | async-start | bytes 32768 | tf_op jit(solution)/shard_map/all_to_all | solution.py:37
  121.0 8.6 %all-to-all-done.3 = f32[32,1,128]{2,1,0:T(1,128)S(1)} async-done(((f32[32,1,128]{2,1,0:T(1,128)}), f32[32,1,128]{2,1,0:T(1,128)S(1)}, u32[]{:S(2)}, u32[]{:S(2)}) %all-to-all-start.3) | async-done | bytes 16416 | tf_op jit(solution)/shard_map/all_to_all | solution.py:37
  129.6 1.1 multiply_reduce_fusion
  (25 shorter events, 3.5 us)
Async XLA Ops:
  0.6 55.1 %copy-start = (bf16[256,640]{1,0:T(8,128)(2,1)S(1)}, bf16[256,640]{1,0:T(8,128)(2,1)}, u32[]{:S(2)}) copy-start(bf16[256,640]{1,0:T(8,128)(2,1)} %param.6) | copy-start | bytes 983044
  3.2 39.4 %all-to-all-start = ((bf16[16,8,3200]{2,1,0:T(8,128)(2,1)}), bf16[16,8,3200]{2,1,0:T(8,128)(2,1)S(1)}, u32[]{:S(2)}, u32[]{:S(2)}) async-start(bf16[16,8,3200]{2,1,0:T(8,128)(2,1)} %broadcast_in_dim.8), calls=%async_computation | async-start | bytes 1638400 | tf_op jit(solution)/shard_map/all_to_all | solution.py:37
  42.6 18.7 %collective-permute-start = (bf16[128,3200]{1,0:T(8,128)(2,1)S(1)}, bf16[128,3200]{1,0:T(8,128)(2,1)S(1)}, u32[]{:S(2)}, u32[]{:S(2)}) collective-permute-start(bf16[128,3200]{1,0:T(8,128)(2,1)S(1)} %bitcast.43), channel_id=1, source_target_pairs={{0,8},{8,16},{16,24},{24,0},{32,40},{40,48},{48,56},{56,32},{64,72... | collective-permute-start | bytes 2457608 | tf_op jit(solution)/shard_map/ppermute | solution.py:58
  44.8 17.7 %collective-permute-start.1 = (bf16[128,3200]{1,0:T(8,128)(2,1)S(1)}, bf16[128,3200]{1,0:T(8,128)(2,1)S(1)}, u32[]{:S(2)}, u32[]{:S(2)}) collective-permute-start(bf16[128,3200]{1,0:T(8,128)(2,1)S(1)} %bitcast.44), channel_id=1, source_target_pairs={{0,24},{8,0},{16,8},{24,16},{32,56},{40,32},{48,40},{56,48},{64,88... | collective-permute-start | bytes 2457608 | tf_op jit(solution)/shard_map/ppermute | solution.py:58
  49.2 13.6 %collective-permute-start.2 = (bf16[64,3200]{1,0:T(8,128)(2,1)S(1)}, bf16[64,3200]{1,0:T(8,128)(2,1)S(1)}, u32[]{:S(2)}, u32[]{:S(2)}) collective-permute-start(bf16[64,3200]{1,0:T(8,128)(2,1)S(1)} %get-tuple-element.5), channel_id=1, source_target_pairs={{0,32},{8,40},{16,48},{24,56},{32,64},{40,72},{48,80},{56,88},{64,... | collective-permute-start | bytes 1228808 | tf_op jit(solution)/shard_map/ppermute | solution.py:58
  51.9 11.1 %collective-permute-start.3 = (bf16[64,3200]{1,0:T(8,128)(2,1)S(1)}, bf16[64,3200]{1,0:T(8,128)(2,1)S(1)}, u32[]{:S(2)}, u32[]{:S(2)}) collective-permute-start(bf16[64,3200]{1,0:T(8,128)(2,1)S(1)} %get-tuple-element.4), channel_id=1, source_target_pairs={{0,224},{8,232},{16,240},{24,248},{32,0},{40,8},{48,16},{56,24},{6... | collective-permute-start | bytes 1228808 | tf_op jit(solution)/shard_map/ppermute | solution.py:58
  66.0 8.4 %collective-permute-start.4 = (f32[128,1024]{0,1:T(8,128)S(1)}, f32[128,1024]{0,1:T(8,128)S(1)}, u32[]{:S(2)}, u32[]{:S(2)}) collective-permute-start(f32[128,1024]{0,1:T(8,128)S(1)} %constant_dynamic-slice_fusion.1), channel_id=1, source_target_pairs={{0,1},{1,0},{2,3},{3,2},{4,5},{5,4},{6,7},{7,6},{8,9},{9,8},{10,11... | collective-permute-start | bytes 1572872 | tf_op jit(solution)/shard_map/ppermute | solution.py:91
  99.2 11.7 %all-to-all-start.2 = ((f32[16,1,128]{2,1,0:T(1,128)}), f32[16,1,128]{2,1,0:T(1,128)S(1)}, u32[]{:S(2)}, u32[]{:S(2)}) async-start(f32[16,1,128]{2,1,0:T(1,128)} %broadcast_in_dim.9), calls=%async_computation.2 | async-start | bytes 16384 | tf_op jit(solution)/shard_map/all_to_all | solution.py:37
  111.5 18.0 %all-to-all-start.3 = ((f32[32,1,128]{2,1,0:T(1,128)}), f32[32,1,128]{2,1,0:T(1,128)S(1)}, u32[]{:S(2)}, u32[]{:S(2)}) async-start(f32[32,1,128]{2,1,0:T(1,128)} %broadcast_in_dim.10), calls=%async_computation.3 | async-start | bytes 32768 | tf_op jit(solution)/shard_map/all_to_all | solution.py:37

commit v3 on v2

--- a/solution.py
+++ b/solution.py
@@ -58,31 +58,36 @@
     return lax.ppermute(value, DP, pairs)
 
 
-def gather_valid(valid):
+def class_gather(valid):
     rows, width = valid.shape
     members = YH * Z
     own = jnp.broadcast_to(valid[None], (members, rows, width)).reshape(members * rows, width)
-    own = exchange(own, DP, class_groups())
+    return exchange(own, DP, class_groups())
+
+
+def neighbour_blocks(own):
     half = own.shape[0] // 2
-    return [
-        own,
-        shift(own, 0, 1),
-        shift(own, 0, -1),
-        shift(own[:half], 1, 0),
-        shift(own[half:], -1, 0),
-    ]
+    right, left = shift(own, 0, 1), shift(own, 0, -1)
+    above, below = shift(own[:half], 1, 0), shift(own[half:], -1, 0)
+    return [[own], [above, below], [right], [left]]
 
 
 def per_device(
     train_input, train_preact, train_upstream, valid_input, valid_preact, valid_upstream
 ):
     valid_grad = output_grad(valid_preact, valid_upstream)
-    blocks = gather_valid(jnp.concatenate([valid_input, valid_grad], axis=1))
+    own = class_gather(jnp.concatenate([valid_input, valid_grad], axis=1))
+    own, train_preact, train_upstream = lax.optimization_barrier(
+        (own, train_preact, train_upstream)
+    )
+    columns = neighbour_blocks(own)
     train_grad = lax.optimization_barrier(output_grad(train_preact, train_upstream))
     split = valid_input.shape[1]
-    input_parts = [cross_dot(train_input, b[:, :split]) * (1.0 / math.sqrt(D)) for b in blocks]
-    grad_parts = [cross_dot(train_grad, b[:, split:]) * (1.0 / math.sqrt(FF)) for b in blocks]
-    parts = jnp.concatenate(input_parts + grad_parts, axis=1)
+    parts = []
+    for column in columns:
+        parts += [cross_dot(train_input, b[:, :split]) * (1.0 / math.sqrt(D)) for b in column]
+        parts += [cross_dot(train_grad, b[:, split:]) * (1.0 / math.sqrt(FF)) for b in column]
+    parts = jnp.concatenate(parts, axis=1)
     count, wide = parts.shape
     core = lax.axis_index("core")
     part_rows = count // CORE
@@ -91,15 +96,16 @@
     parts = kept + lax.ppermute(sent, "core", [(0, 1), (1, 0)])
     parts = exchange(parts, "yl").reshape(YL, part_rows // YL, wide)
     parts = jnp.sum(parts, axis=0)
-    product = jnp.sum(parts[:, : wide // 2] * parts[:, wide // 2 :], axis=0)
-    edge = blocks[0].shape[0] // 2
-    sums = jnp.sum(product.reshape(-1, VAL_SEQS, edge), axis=(0, 2)) * (1.0 / SEQ_LEN)
+    pairs = parts.reshape(-1, CLASSES, 2, VAL_SEQS, wide // (4 * CLASSES))
+    sums = jnp.sum(pairs[:, :, 0] * pairs[:, :, 1], axis=(0, 1, 3)) * (1.0 / SEQ_LEN)
     lanes = jnp.pad(sums, (0, 128 - VAL_SEQS))[None]
     tensor = YL * CORE
+    lanes, yh = lax.optimization_barrier((lanes, lax.axis_index("yh")))
     column = exchange(jnp.broadcast_to(lanes, (YH * tensor, 128)), ("yh",) + TENSOR)
     by_half = jnp.sum(column.reshape(YH, tensor, 128), axis=1)
-    first_order = lax.dynamic_slice(by_half, (lax.axis_index("yh"), 0), (1, VAL_SEQS))
+    first_order = lax.dynamic_slice(by_half, (yh, 0), (1, VAL_SEQS))
     total = jnp.sum(by_half, axis=0, keepdims=True)
+    first_order, total = lax.optimization_barrier((first_order, total))
     plane = Z * X
     planes = exchange(jnp.broadcast_to(total, (plane, 128)), ("z", "x"))
     weight = jnp.sum(planes, axis=0, keepdims=True)[:, :VAL_SEQS]

time: 131 us -> 129 us (0.985)
  blocking collectives: 23.5 us -> 16.7 us
  waiting for transfers between devices: 41.7 us -> 47.5 us
  other arithmetic: 5.59 us -> 3.9 us
    all_to_all x3, waiting for transfers between devices: 33.8 us -> 41.8 us  [exchange(): lax.all_to_all(value, axes, 0, 0, axis_index_groups=groups, tiled=True)]
    all_to_all x1, blocking collectives: 23.5 us -> 16.7 us  [exchange(): lax.all_to_all(value, axes, 0, 0, axis_index_groups=groups, tiled=True)]
    ppermute x4, waiting for transfers between devices: 6.38 us -> 4.22 us  [shift(): return lax.ppermute(value, DP, pairs)]
    ppermute x1, starting transfers between devices: 6.89 us -> 8.62 us  [per_device(): parts = kept + lax.ppermute(sent, 'core', [(0, 1), (1, 0)])]
    all_to_all x3, starting transfers between devices: 32.8 us -> 31.1 us  [exchange(): lax.all_to_all(value, axes, 0, 0, axis_index_groups=groups, tiled=True)]
where the time goes in v3:
time: 129 us; the launch traced here: 128 us
  starting transfers between devices  52.8 us (41%)
  waiting for transfers between devices  47.5 us (37%)
  blocking collectives  16.7 us (13%)
  other arithmetic  3.9 us (3%)
  matrix products  3.84 us (3%)
  local copies, waits for them, and re-layouts  2.88 us (2%)
    all_to_all x3, waiting for transfers between devices, exchange(): lax.all_to_all(value, axes, 0, 0, axis_index_groups=groups, tiled=True)  41.8 us
    all_to_all x3, starting transfers between devices, exchange(): lax.all_to_all(value, axes, 0, 0, axis_index_groups=groups, tiled=True)  31.1 us
    all_to_all x1, blocking collectives, exchange(): lax.all_to_all(value, axes, 0, 0, axis_index_groups=groups, tiled=True)  16.7 us
    ppermute x4, starting transfers between devices, shift(): return lax.ppermute(value, DP, pairs)  13.1 us
    ppermute x1, starting transfers between devices, per_device(): parts = kept + lax.ppermute(sent, 'core', [(0, 1), (1, 0)])  8.62 us
    ppermute x4, waiting for transfers between devices, shift(): return lax.ppermute(value, DP, pairs)  4.22 us
    dot_general x10, matrix products, cross_dot(): lax.dot_general(left, right, (((1,), (1,)), ((), ())), preferred_element_...  3.84 us
  transfers between devices with their start and end apart: 8, of which 6 were waited for; matrix products, arithmetic and copies ran while one was open for 3% of the time, Pallas kernels for 0%

profile of v3, /device:TPU:1, one launch (start us, length us, event | category | flops | bytes accessed | tf_op | source)
XLA Modules:
  0.0 128.5 jit_solution(6331104996836409246)
XLA Ops:
  0.6 0.9 fusion.41
  1.5 0.7 pad_maximum_fusion
  2.2 0.9 broadcast_in_dim.12
  3.2 18.8 %all-to-all-start = ((bf16[16,8,3200]{2,1,0:T(8,128)(2,1)}), bf16[16,8,3200]{2,1,0:T(8,128)(2,1)S(1)}, u32[]{:S(2)}, u32[]{:S(2)}) async-start(bf16[16,8,3200]{2,1,0:T(8,128)(2,1)} %broadcast_in_dim.12), calls=%async_computation | async-start | bytes 1638400 | tf_op jit(solution)/shard_map/all_to_all | solution.py:37
  22.0 20.7 %all-to-all-done = bf16[16,8,3200]{2,1,0:T(8,128)(2,1)S(1)} async-done(((bf16[16,8,3200]{2,1,0:T(8,128)(2,1)}), bf16[16,8,3200]{2,1,0:T(8,128)(2,1)S(1)}, u32[]{:S(2)}, u32[]{:S(2)}) %all-to-all-start) | async-done | bytes 819232 | tf_op jit(solution)/shard_map/all_to_all | solution.py:37
  42.8 2.4 %collective-permute-start.2 = (bf16[128,3200]{1,0:T(8,128)(2,1)S(1)}, bf16[128,3200]{1,0:T(8,128)(2,1)S(1)}, u32[]{:S(2)}, u32[]{:S(2)}) collective-permute-start(bf16[128,3200]{1,0:T(8,128)(2,1)S(1)} %bitcast.45), channel_id=1, source_target_pairs={{0,8},{8,16},{16,24},{24,0},{32,40},{40,48},{48,56},{56,32},{64,72... | collective-permute-start | bytes 2457608 | tf_op jit(solution)/shard_map/ppermute | solution.py:58
  45.2 4.3 %collective-permute-start.3 = (bf16[128,3200]{1,0:T(8,128)(2,1)S(1)}, bf16[128,3200]{1,0:T(8,128)(2,1)S(1)}, u32[]{:S(2)}, u32[]{:S(2)}) collective-permute-start(bf16[128,3200]{1,0:T(8,128)(2,1)S(1)} %bitcast.46), channel_id=1, source_target_pairs={{0,24},{8,0},{16,8},{24,16},{32,56},{40,32},{48,40},{56,48},{64,88... | collective-permute-start | bytes 2457608 | tf_op jit(solution)/shard_map/ppermute | solution.py:58
  49.5 1.3 fusion.7
  50.8 2.7 %collective-permute-start = (bf16[64,3200]{1,0:T(8,128)(2,1)S(1)}, bf16[64,3200]{1,0:T(8,128)(2,1)S(1)}, u32[]{:S(2)}, u32[]{:S(2)}) collective-permute-start(bf16[64,3200]{1,0:T(8,128)(2,1)S(1)} %get-tuple-element.17), channel_id=1, source_target_pairs={{0,32},{8,40},{16,48},{24,56},{32,64},{40,72},{48,80},{56,88},{64,... | collective-permute-start | bytes 1228808 | tf_op jit(solution)/shard_map/ppermute | solution.py:58
  53.5 3.8 %collective-permute-start.1 = (bf16[64,3200]{1,0:T(8,128)(2,1)S(1)}, bf16[64,3200]{1,0:T(8,128)(2,1)S(1)}, u32[]{:S(2)}, u32[]{:S(2)}) collective-permute-start(bf16[64,3200]{1,0:T(8,128)(2,1)S(1)} %get-tuple-element.16), channel_id=1, source_target_pairs={{0,224},{8,232},{16,240},{24,248},{32,0},{40,8},{48,16},{56,24},{6... | collective-permute-start | bytes 1228808 | tf_op jit(solution)/shard_map/ppermute | solution.py:58
  57.5 0.5 fusion.16
  58.1 2.9 %collective-permute-done = bf16[64,3200]{1,0:T(8,128)(2,1)S(1)} collective-permute-done((bf16[64,3200]{1,0:T(8,128)(2,1)S(1)}, bf16[64,3200]{1,0:T(8,128)(2,1)S(1)}, u32[]{:S(2)}, u32[]{:S(2)}) %collective-permute-start) | collective-permute-done | bytes 409632 | tf_op jit(solution)/shard_map/ppermute | solution.py:58
  61.2 1.3 %collective-permute-done.1 = bf16[64,3200]{1,0:T(8,128)(2,1)S(1)} collective-permute-done((bf16[64,3200]{1,0:T(8,128)(2,1)S(1)}, bf16[64,3200]{1,0:T(8,128)(2,1)S(1)}, u32[]{:S(2)}, u32[]{:S(2)}) %collective-permute-start.1) | collective-permute-done | bytes 409632 | tf_op jit(solution)/shard_map/ppermute | solution.py:58
  64.0 0.5 fusion.15
  65.5 8.6 %collective-permute-start.4 = (f32[128,1024]{0,1:T(8,128)S(1)}, f32[128,1024]{0,1:T(8,128)S(1)}, u32[]{:S(2)}, u32[]{:S(2)}) collective-permute-start(f32[128,1024]{0,1:T(8,128)S(1)} %constant_dynamic-slice_fusion.1), channel_id=1, source_target_pairs={{0,1},{1,0},{2,3},{3,2},{4,5},{5,4},{6,7},{7,6},{8,9},{9,8},{10,11... | collective-permute-start | bytes 1572872 | tf_op jit(solution)/shard_map/ppermute | solution.py:96
  74.1 1.5 %collective-permute-done.4 = f32[128,1024]{0,1:T(8,128)S(1)} collective-permute-done((f32[128,1024]{0,1:T(8,128)S(1)}, f32[128,1024]{0,1:T(8,128)S(1)}, u32[]{:S(2)}, u32[]{:S(2)}) %collective-permute-start.4) | collective-permute-done | bytes 524320 | tf_op jit(solution)/shard_map/ppermute | solution.py:96
  75.7 1.0 copy.12
  76.7 7.4 %all-to-all-start.1 = ((f32[4,32,1024]{2,1,0:T(8,128)}), f32[4,32,1024]{2,1,0:T(8,128)S(1)}, u32[]{:S(2)}, u32[]{:S(2)}) async-start(f32[4,32,1024]{2,1,0:T(8,128)} %bitcast.6), calls=%async_computation.1 | async-start | bytes 1048576 | tf_op jit(solution)/shard_map/all_to_all | solution.py:37
  84.1 14.0 %all-to-all-done.1 = f32[4,32,1024]{2,1,0:T(8,128)S(1)} async-done(((f32[4,32,1024]{2,1,0:T(8,128)}), f32[4,32,1024]{2,1,0:T(8,128)S(1)}, u32[]{:S(2)}, u32[]{:S(2)}) %all-to-all-start.1) | async-done | bytes 524320 | tf_op jit(solution)/shard_map/all_to_all | solution.py:37
  98.6 0.6 broadcast_in_dim.27
  99.2 4.9 %all-to-all-start.2 = ((f32[16,1,128]{2,1,0:T(1,128)}), f32[16,1,128]{2,1,0:T(1,128)S(1)}, u32[]{:S(2)}, u32[]{:S(2)}) async-start(f32[16,1,128]{2,1,0:T(1,128)} %broadcast_in_dim.27), calls=%async_computation.2 | async-start | bytes 16384 | tf_op jit(solution)/shard_map/all_to_all | solution.py:37
  104.1 7.0 %all-to-all-done.2 = f32[16,1,128]{2,1,0:T(1,128)S(1)} async-done(((f32[16,1,128]{2,1,0:T(1,128)}), f32[16,1,128]{2,1,0:T(1,128)S(1)}, u32[]{:S(2)}, u32[]{:S(2)}) %all-to-all-start.2) | async-done | bytes 8224 | tf_op jit(solution)/shard_map/all_to_all | solution.py:37
  111.2 16.7 %all_to_all.30 = f32[32,1,128]{2,1,0:T(1,128)S(1)} all-to-all(f32[32,1,128]{2,1,0:T(1,128)S(1)} %broadcast_in_dim.29), channel_id=1, replica_groups=mesh['yh'=2,'z'=8,'x'=4,'yl'=4,'core'=2] {'z','x'}, dimensions={0} | all-to-all | bytes 32768 | tf_op jit(solution)/shard_map/all_to_all | solution.py:37
  127.9 0.6 multiply_reduce_fusion
  (31 shorter events, 3.5 us)
Async XLA Ops:
  0.6 56.6 %copy-start = (bf16[256,640]{1,0:T(8,128)(2,1)S(1)}, bf16[256,640]{1,0:T(8,128)(2,1)}, u32[]{:S(2)}) copy-start(bf16[256,640]{1,0:T(8,128)(2,1)} %param.6) | copy-start | bytes 983044
  3.2 46.3 %copy-start.1 = (bf16[256,2560]{1,0:T(8,128)(2,1)S(1)}, bf16[256,2560]{1,0:T(8,128)(2,1)}, u32[]{:S(2)}) copy-start(bf16[256,2560]{1,0:T(8,128)(2,1)} %param.7) | copy-start | bytes 3932164
  3.2 39.5 %all-to-all-start = ((bf16[16,8,3200]{2,1,0:T(8,128)(2,1)}), bf16[16,8,3200]{2,1,0:T(8,128)(2,1)S(1)}, u32[]{:S(2)}, u32[]{:S(2)}) async-start(bf16[16,8,3200]{2,1,0:T(8,128)(2,1)} %broadcast_in_dim.12), calls=%async_computation | async-start | bytes 1638400 | tf_op jit(solution)/shard_map/all_to_all | solution.py:37
  42.7 6.7 %copy-start.2 = (bf16[256,2560]{1,0:T(8,128)(2,1)S(1)}, bf16[256,2560]{1,0:T(8,128)(2,1)}, u32[]{:S(2)}) copy-start(bf16[256,2560]{1,0:T(8,128)(2,1)} %param.8) | copy-start | bytes 3932164
  42.8 21.0 %collective-permute-start.2 = (bf16[128,3200]{1,0:T(8,128)(2,1)S(1)}, bf16[128,3200]{1,0:T(8,128)(2,1)S(1)}, u32[]{:S(2)}, u32[]{:S(2)}) collective-permute-start(bf16[128,3200]{1,0:T(8,128)(2,1)S(1)} %bitcast.45), channel_id=1, source_target_pairs={{0,8},{8,16},{16,24},{24,0},{32,40},{40,48},{48,56},{56,32},{64,72... | collective-permute-start | bytes 2457608 | tf_op jit(solution)/shard_map/ppermute | solution.py:58
  45.2 19.4 %collective-permute-start.3 = (bf16[128,3200]{1,0:T(8,128)(2,1)S(1)}, bf16[128,3200]{1,0:T(8,128)(2,1)S(1)}, u32[]{:S(2)}, u32[]{:S(2)}) collective-permute-start(bf16[128,3200]{1,0:T(8,128)(2,1)S(1)} %bitcast.46), channel_id=1, source_target_pairs={{0,24},{8,0},{16,8},{24,16},{32,56},{40,32},{48,40},{56,48},{64,88... | collective-permute-start | bytes 2457608 | tf_op jit(solution)/shard_map/ppermute | solution.py:58
  50.8 10.2 %collective-permute-start = (bf16[64,3200]{1,0:T(8,128)(2,1)S(1)}, bf16[64,3200]{1,0:T(8,128)(2,1)S(1)}, u32[]{:S(2)}, u32[]{:S(2)}) collective-permute-start(bf16[64,3200]{1,0:T(8,128)(2,1)S(1)} %get-tuple-element.17), channel_id=1, source_target_pairs={{0,32},{8,40},{16,48},{24,56},{32,64},{40,72},{48,80},{56,88},{64,... | collective-permute-start | bytes 1228808 | tf_op jit(solution)/shard_map/ppermute | solution.py:58
  53.5 9.0 %collective-permute-start.1 = (bf16[64,3200]{1,0:T(8,128)(2,1)S(1)}, bf16[64,3200]{1,0:T(8,128)(2,1)S(1)}, u32[]{:S(2)}, u32[]{:S(2)}) collective-permute-start(bf16[64,3200]{1,0:T(8,128)(2,1)S(1)} %get-tuple-element.16), channel_id=1, source_target_pairs={{0,224},{8,232},{16,240},{24,248},{32,0},{40,8},{48,16},{56,24},{6... | collective-permute-start | bytes 1228808 | tf_op jit(solution)/shard_map/ppermute | solution.py:58
  65.5 10.1 %collective-permute-start.4 = (f32[128,1024]{0,1:T(8,128)S(1)}, f32[128,1024]{0,1:T(8,128)S(1)}, u32[]{:S(2)}, u32[]{:S(2)}) collective-permute-start(f32[128,1024]{0,1:T(8,128)S(1)} %constant_dynamic-slice_fusion.1), channel_id=1, source_target_pairs={{0,1},{1,0},{2,3},{3,2},{4,5},{5,4},{6,7},{7,6},{8,9},{9,8},{10,11... | collective-permute-start | bytes 1572872 | tf_op jit(solution)/shard_map/ppermute | solution.py:96
  76.7 21.4 %all-to-all-start.1 = ((f32[4,32,1024]{2,1,0:T(8,128)}), f32[4,32,1024]{2,1,0:T(8,128)S(1)}, u32[]{:S(2)}, u32[]{:S(2)}) async-start(f32[4,32,1024]{2,1,0:T(8,128)} %bitcast.6), calls=%async_computation.1 | async-start | bytes 1048576 | tf_op jit(solution)/shard_map/all_to_all | solution.py:37
  99.2 11.9 %all-to-all-start.2 = ((f32[16,1,128]{2,1,0:T(1,128)}), f32[16,1,128]{2,1,0:T(1,128)S(1)}, u32[]{:S(2)}, u32[]{:S(2)}) async-start(f32[16,1,128]{2,1,0:T(1,128)} %broadcast_in_dim.27), calls=%async_computation.2 | async-start | bytes 16384 | tf_op jit(solution)/shard_map/all_to_all | solution.py:37
  111.2 17.3 %copy-start.3 = (f32[1,2]{1,0:T(1,128)}, f32[1,2]{1,0:T(1,128)S(1)}, u32[]{:S(2)}) copy-start(f32[1,2]{1,0:T(1,128)S(1)} %constant_dynamic-slice_fusion) | copy-start | bytes 28

commit v4 on v3

v4 whole, which is shorter than its diff:
```python
import math

import jax
import jax.numpy as jnp
from jax import lax
from jax.experimental import pallas as pl
from jax.sharding import Mesh, PartitionSpec as P

D = 5120
FF = 20480
SEQ_LEN = 256
VAL_SEQS = 2
DP = ("yh", "z", "x")
TENSOR = ("yl", "core")
YH, Z, X, YL, CORE = SIZES = (2, 8, 4, 4, 2)
CLASSES = 4
LANES = 128
LOW, HIGH = -126.0, 30.0

inv_root_two = 0.7071067811865476
inv_root_tau = 0.3989422804014327


def output_grad(preact, upstream):
    preact_f = preact.astype(jnp.float32)
    derivative = (
        0.5 * (1.0 + lax.erf(preact_f * inv_root_two))
        + preact_f * jnp.exp(-0.5 * preact_f * preact_f) * inv_root_tau
    )
    return (upstream.astype(jnp.float32) * derivative).astype(jnp.bfloat16)


def cross_dot(left, right):
    return lax.dot_general(
        left, right, (((1,), (1,)), ((), ())), preferred_element_type=jnp.float32
    )


def exchange(value, axes, groups=None):
    return lax.all_to_all(value, axes, 0, 0, axis_index_groups=groups, tiled=True)


def place(yh, z, x):
    return (yh * Z + z % Z) * X + x % X


def class_groups():
    return [
        [place(yh, z, kind - 2 * z) for yh in range(YH) for z in range(Z)]
        for kind in range(CLASSES)
    ]


def shift(value, dz, dx):
    pairs = [
        (place(yh, z, x), place(yh, z + dz, x + dx))
        for yh in range(YH)
        for z in range(Z)
        for x in range(X)
    ]
    return lax.ppermute(value, DP, pairs)


def valid_copies_kernel(input_ref, preact_ref, upstream_ref, out_ref):
    split = input_ref.shape[1]
    joined = output_grad(preact_ref[...], upstream_ref[...])
    for member in range(out_ref.shape[0]):
        out_ref[member, :, :split] = input_ref[...]
        out_ref[member, :, split:] = joined


def class_gather(valid_input, valid_preact, valid_upstream):
    rows, split = valid_input.shape
    width = split + valid_preact.shape[1]
    members = YH * Z
    copies = pl.pallas_call(
        valid_copies_kernel,
        out_shape=jax.ShapeDtypeStruct((members, rows, width), jnp.bfloat16),
    )(valid_input, valid_preact, valid_upstream)
    return exchange(copies.reshape(members * rows, width), DP, class_groups())


def neighbour_blocks(own):
    half = own.shape[0] // 2
    right, left = shift(own, 0, 1), shift(own, 0, -1)
    above, below = shift(own[:half], 1, 0), shift(own[half:], -1, 0)
    return [[own], [above, below], [right], [left]]


def encode(parts):
    kinds = [parts[0::2], parts[1::2]]
    largest = jnp.stack(
        [jnp.max(jnp.stack([jnp.max(jnp.abs(p), axis=1) for p in kind]), axis=0) for kind in kinds],
        axis=1,
    )
    exponents = jnp.clip(jnp.ceil(jnp.log2(jnp.maximum(largest, 2.0**LOW))), LOW, HIGH)
    scale = jnp.exp2(-exponents)
    scaled = [(p * scale[:, i % 2, None]).astype(jnp.float16) for i, p in enumerate(parts)]
    tail = jnp.pad(exponents, ((0, 0), (0, LANES - 2))).astype(jnp.float16)
    return jnp.concatenate(scaled + [tail], axis=1)


def decode(coded):
    blocks = 2 * CLASSES
    scale = jnp.exp2(coded[:, :, blocks * LANES : blocks * LANES + 2].astype(jnp.float32))
    return [
        jnp.sum(
            coded[:, :, i * LANES : (i + 1) * LANES].astype(jnp.float32)
            * scale[:, :, i % 2, None],
            axis=0,
        )
        for i in range(blocks)
    ]


def finish_kernel(column_ref, planes_ref, first_ref, second_ref):
    tensor = YL * CORE
    start = pl.multiple_of(lax.axis_index("yh") * tensor, tensor)
    first = jnp.sum(column_ref[pl.ds(start, tensor), :], axis=0, keepdims=True)
    weight = jnp.sum(planes_ref[...], axis=0, keepdims=True)
    first_ref[...] = first[:, :VAL_SEQS]
    second_ref[...] = jnp.sum(first * weight, axis=1, keepdims=True)


def per_device(
    train_input, train_preact, train_upstream, valid_input, valid_preact, valid_upstream
):
    own = class_gather(valid_input, valid_preact, valid_upstream)
    own, train_preact, train_upstream = lax.optimization_barrier(
        (own, train_preact, train_upstream)
    )
    columns = neighbour_blocks(own)
    train_grad = lax.optimization_barrier(output_grad(train_preact, train_upstream))
    split = valid_input.shape[1]
    parts = []
    for column in columns:
        inputs = [cross_dot(train_input, b[:, :split]) * (1.0 / math.sqrt(D)) for b in column]
        grads = [cross_dot(train_grad, b[:, split:]) * (1.0 / math.sqrt(FF)) for b in column]
        parts += [jnp.concatenate(inputs, axis=1), jnp.concatenate(grads, axis=1)]
    coded = encode(parts)
    tensor = YL * CORE
    coded = exchange(coded, TENSOR).reshape(tensor, -1, coded.shape[1])
    summed = decode(coded)
    product = sum(summed[2 * i] * summed[2 * i + 1] for i in range(CLASSES))
    product = jnp.sum(product, axis=0).reshape(VAL_SEQS, LANES // VAL_SEQS)
    sums = jnp.sum(product, axis=1) * (1.0 / SEQ_LEN)
    lanes = jnp.pad(sums, (0, LANES - VAL_SEQS))[None]
    column = exchange(jnp.broadcast_to(lanes, (YH * tensor, LANES)), ("yh",) + TENSOR)
    total = jnp.sum(column, axis=0, keepdims=True)
    planes = exchange(jnp.broadcast_to(total, (Z * X, LANES)), ("z", "x"))
    first_order, second_order = pl.pallas_call(
        finish_kernel,
        out_shape=(
            jax.ShapeDtypeStruct((1, VAL_SEQS), jnp.float32),
            jax.ShapeDtypeStruct((1, 1), jnp.float32),
        ),
    )(column, planes)
    return (first_order, second_order.reshape(1))


def solution(mesh):
    fine = Mesh(mesh.devices.reshape(SIZES), DP + TENSOR)
    return jax.shard_map(
        per_device,
        mesh=fine,
        in_specs=(P(DP, TENSOR),) * 6,
        out_specs=(P(DP, None), P(DP)),
        check_vma=False,
    )
```

time: 129 us -> 124 us (0.961)
  blocking collectives: 16.7 us -> 92.8 us
  starting transfers between devices: 52.8 us -> 12.2 us
  waiting for transfers between devices: 47.5 us -> 7.42 us
  Pallas kernels: 0 us -> 3.15 us
  other arithmetic: 3.9 us -> 1.92 us
  local copies, waits for them, and re-layouts: 2.88 us -> 0.93 us
    all_to_all x1 -> x4, blocking collectives: 16.7 us -> 92.8 us  [exchange(): lax.all_to_all(value, axes, 0, 0, axis_index_groups=groups, tiled=True)]
    all_to_all x3 -> x0, waiting for transfers between devices: 41.8 us -> none  [exchange(): lax.all_to_all(value, axes, 0, 0, axis_index_groups=groups, tiled=True)]
    all_to_all x3 -> x0, starting transfers between devices: 31.1 us -> none  [exchange(): lax.all_to_all(value, axes, 0, 0, axis_index_groups=groups, tiled=True)]
    ppermute x1 -> x0, starting transfers between devices: 8.62 us -> none  [per_device(): parts = kept + lax.ppermute(sent, 'core', [(0, 1), (1, 0)])]
    ppermute x4, waiting for transfers between devices: 4.22 us -> 7.42 us  [shift(): return lax.ppermute(value, DP, pairs)]
    pallas_call x0 -> x2, Pallas kernels: none -> 3.15 us  [the longest x1 1.81 us: class_gather(): pl.pallas_call(valid_copies_kernel, out_shape=jax.ShapeDtypeStruct((membe...]
    broadcast_in_dim x4 -> x2, local copies, waits for them, and re-layouts: 1.56 us -> 0.02 us  [the longest x1 0.01 us: per_device(): planes = exchange(jnp.broadcast_to(total, (Z * X, LANES)), ('z', 'x'))]
    ppermute x1 -> x0, waiting for transfers between devices: 1.51 us -> none  [per_device(): parts = kept + lax.ppermute(sent, 'core', [(0, 1), (1, 0)])]
  transfers between devices with their start and end apart: 8 -> 4, of which waited for: 6 -> 2; matrix products, arithmetic and copies ran while one was open for 3% -> 3% of each run, Pallas kernels for 0% -> 0%
where the time goes in v4:
time: 124 us; the launch traced here: 123 us
  blocking collectives  92.8 us (75%)
  starting transfers between devices  12.2 us (10%)
  waiting for transfers between devices  7.42 us (6%)
  matrix products  3.92 us (3%)
  Pallas kernels  3.15 us (3%)
  other arithmetic  1.92 us (2%)
    all_to_all x4, blocking collectives, exchange(): lax.all_to_all(value, axes, 0, 0, axis_index_groups=groups, tiled=True)  92.8 us
    ppermute x4, starting transfers between devices, shift(): return lax.ppermute(value, DP, pairs)  12.2 us
    ppermute x4, waiting for transfers between devices, shift(): return lax.ppermute(value, DP, pairs)  7.42 us
    dot_general x10, matrix products, cross_dot(): lax.dot_general(left, right, (((1,), (1,)), ((), ())), preferred_element_...  3.92 us
  transfers between devices with their start and end apart: 4, of which 2 were waited for; matrix products, arithmetic and copies ran while one was open for 3% of the time, Pallas kernels for 0%

profile of v4, /device:TPU:1, one launch (start us, length us, event | category | flops | bytes accessed | tf_op | source)
XLA Modules:
  0.0 123.3 jit_solution(4134579134037320093)
XLA Ops:
  0.6 1.8 %shard_map.77 = bf16[16,8,3200]{2,1,0:T(8,128)(2,1)} custom-call(bf16[8,640]{1,0:T(8,128)(2,1)} %input_ref.1, bf16[8,2560]{1,0:T(8,128)(2,1)} %preact_ref.1, bf16[8,2560]{1,0:T(8,128)(2,1)} %upstream_ref.1), custom_call_target="tpu_custom_call" | custom-call | tf_op jit(solution)/shard_map/pallas_call | solution.py:76
  2.5 40.1 %all_to_all.34 = bf16[16,8,3200]{2,1,0:T(8,128)(2,1)S(1)} all-to-all(bf16[16,8,3200]{2,1,0:T(8,128)(2,1)} %shard_map.77), channel_id=1, replica_groups={{0,48,64,112,128,176,192,240,256,304,320,368,384,432,448,496},{8,56,72,..., dimensions={0} | all-to-all | bytes 1638400 | tf_op jit(solution)/shard_map/all_to_all | solution.py:40
  42.6 2.9 %collective-permute-start.2 = (bf16[128,3200]{1,0:T(8,128)(2,1)S(1)}, bf16[128,3200]{1,0:T(8,128)(2,1)S(1)}, u32[]{:S(2)}, u32[]{:S(2)}) collective-permute-start(bf16[128,3200]{1,0:T(8,128)(2,1)S(1)} %bitcast.36), channel_id=1, source_target_pairs={{0,8},{8,16},{16,24},{24,0},{32,40},{40,48},{48,56},{56,32},{64,72... | collective-permute-start | bytes 2457608 | tf_op jit(solution)/shard_map/ppermute | solution.py:61
  45.5 3.6 %collective-permute-start.3 = (bf16[128,3200]{1,0:T(8,128)(2,1)S(1)}, bf16[128,3200]{1,0:T(8,128)(2,1)S(1)}, u32[]{:S(2)}, u32[]{:S(2)}) collective-permute-start(bf16[128,3200]{1,0:T(8,128)(2,1)S(1)} %bitcast.37), channel_id=1, source_target_pairs={{0,24},{8,0},{16,8},{24,16},{32,56},{40,32},{48,40},{56,48},{64,88... | collective-permute-start | bytes 2457608 | tf_op jit(solution)/shard_map/ppermute | solution.py:61
  49.2 1.3 %fusion.7 = bf16[256,2560]{1,0:T(8,128)(2,1)S(1)} fusion(bf16[256,2560]{1,0:T(8,128)(2,1)S(1)} %copy-done.1, bf16[256,2560]{1,0:T(8,128)(2,1)S(1)} %copy-done.2), kind=kLoop, calls=%fused_computation.11 | loop fusion | flops 7864320 | bytes 3932160 | tf_op jit(solution)/shard_map/convert_element_type | solution.py:30
  50.5 3.8 %collective-permute-start.1 = (bf16[64,3200]{1,0:T(8,128)(2,1)S(1)}, bf16[64,3200]{1,0:T(8,128)(2,1)S(1)}, u32[]{:S(2)}, u32[]{:S(2)}) collective-permute-start(bf16[64,3200]{1,0:T(8,128)(2,1)S(1)} %get-tuple-element.29), channel_id=1, source_target_pairs={{0,224},{8,232},{16,240},{24,248},{32,0},{40,8},{48,16},{56,24},{6... | collective-permute-start | bytes 1228808 | tf_op jit(solution)/shard_map/ppermute | solution.py:61
  54.2 1.9 %collective-permute-start = (bf16[64,3200]{1,0:T(8,128)(2,1)S(1)}, bf16[64,3200]{1,0:T(8,128)(2,1)S(1)}, u32[]{:S(2)}, u32[]{:S(2)}) collective-permute-start(bf16[64,3200]{1,0:T(8,128)(2,1)S(1)} %get-tuple-element.28), channel_id=1, source_target_pairs={{0,32},{8,40},{16,48},{24,56},{32,64},{40,72},{48,80},{56,88},{64,... | collective-permute-start | bytes 1228808 | tf_op jit(solution)/shard_map/ppermute | solution.py:61
  56.2 0.6 abs_reduce_fusion.3
  56.7 0.3 abs_reduce_fusion.7
  57.0 2.9 %collective-permute-done.1 = bf16[64,3200]{1,0:T(8,128)(2,1)S(1)} collective-permute-done((bf16[64,3200]{1,0:T(8,128)(2,1)S(1)}, bf16[64,3200]{1,0:T(8,128)(2,1)S(1)}, u32[]{:S(2)}, u32[]{:S(2)}) %collective-permute-start.1) | collective-permute-done | bytes 409632 | tf_op jit(solution)/shard_map/ppermute | solution.py:61
  59.9 0.5 convolution_multiply_fusion
  60.4 4.5 %collective-permute-done = bf16[64,3200]{1,0:T(8,128)(2,1)S(1)} collective-permute-done((bf16[64,3200]{1,0:T(8,128)(2,1)S(1)}, bf16[64,3200]{1,0:T(8,128)(2,1)S(1)}, u32[]{:S(2)}, u32[]{:S(2)}) %collective-permute-start) | collective-permute-done | bytes 409632 | tf_op jit(solution)/shard_map/ppermute | solution.py:61
  64.9 0.5 convolution_multiply_fusion.1
  65.7 0.2 fusion.9
  66.0 0.6 abs_reduce_fusion.1
  66.6 0.6 abs_reduce_fusion
  67.2 0.3 abs_reduce_fusion.4
  67.4 0.3 abs_reduce_fusion.5
  68.0 0.5 copy.11
  68.5 28.6 %all_to_all.35 = f16[8,32,1152]{2,1,0:T(8,128)(2,1)S(1)} all-to-all(f16[8,32,1152]{2,1,0:T(8,128)(2,1)S(1)} %bitcast.40), channel_id=1, replica_groups=mesh['yh'=2,'z'=8,'x'=4,'yl'=4,'core'=2] {'yl','core'}, dimensions={0} | all-to-all | bytes 1179648 | tf_op jit(solution)/shard_map/all_to_all | solution.py:40
  97.1 0.2 slice_reduce_fusion
  97.8 10.2 %all_to_all.36 = f32[16,1,128]{2,1,0:T(1,128)S(1)} all-to-all(f32[16,1,128]{2,1,0:T(1,128)S(1)} %broadcast_in_dim.4), channel_id=1, replica_groups=mesh['yh'=2,'z'=8,'x'=4,'yl'=4,'core'=2] {'yh','yl','core'}, dimensions={0} | all-to-all | bytes 16384 | tf_op jit(solution)/shard_map/all_to_all | solution.py:40
  108.0 13.9 %all_to_all.37 = f32[32,1,128]{2,1,0:T(1,128)} all-to-all(f32[32,1,128]{2,1,0:T(1,128)S(1)} %broadcast_in_dim.5), channel_id=1, replica_groups=mesh['yh'=2,'z'=8,'x'=4,'yl'=4,'core'=2] {'z','x'}, dimensions={0} | all-to-all | bytes 32768 | tf_op jit(solution)/shard_map/all_to_all | solution.py:40
  121.9 1.3 %shard_map.78 = (f32[1,2]{1,0:T(1,128)}, f32[1,1]{1,0:T(1,128)}) custom-call(f32[16,128]{1,0:T(8,128)} %bitcast.41, f32[32,128]{1,0:T(8,128)} %bitcast.42), custom_call_target="tpu_custom_call" | custom-call | tf_op jit(solution)/shard_map/pallas_call | solution.py:151
  (40 shorter events, 1.1 us)
Async XLA Ops:
  0.6 56.1 %copy-start = (bf16[256,640]{1,0:T(8,128)(2,1)S(1)}, bf16[256,640]{1,0:T(8,128)(2,1)}, u32[]{:S(2)}) copy-start(bf16[256,640]{1,0:T(8,128)(2,1)} %param.6) | copy-start | bytes 983044
  2.5 46.7 %copy-start.1 = (bf16[256,2560]{1,0:T(8,128)(2,1)S(1)}, bf16[256,2560]{1,0:T(8,128)(2,1)}, u32[]{:S(2)}) copy-start(bf16[256,2560]{1,0:T(8,128)(2,1)} %param.7) | copy-start | bytes 3932164
  2.5 46.7 %copy-start.2 = (bf16[256,2560]{1,0:T(8,128)(2,1)S(1)}, bf16[256,2560]{1,0:T(8,128)(2,1)}, u32[]{:S(2)}) copy-start(bf16[256,2560]{1,0:T(8,128)(2,1)} %param.8) | copy-start | bytes 3932164
  42.6 23.3 %collective-permute-start.2 = (bf16[128,3200]{1,0:T(8,128)(2,1)S(1)}, bf16[128,3200]{1,0:T(8,128)(2,1)S(1)}, u32[]{:S(2)}, u32[]{:S(2)}) collective-permute-start(bf16[128,3200]{1,0:T(8,128)(2,1)S(1)} %bitcast.36), channel_id=1, source_target_pairs={{0,8},{8,16},{16,24},{24,0},{32,40},{40,48},{48,56},{56,32},{64,72... | collective-permute-start | bytes 2457608 | tf_op jit(solution)/shard_map/ppermute | solution.py:61
  45.5 21.0 %collective-permute-start.3 = (bf16[128,3200]{1,0:T(8,128)(2,1)S(1)}, bf16[128,3200]{1,0:T(8,128)(2,1)S(1)}, u32[]{:S(2)}, u32[]{:S(2)}) collective-permute-start(bf16[128,3200]{1,0:T(8,128)(2,1)S(1)} %bitcast.37), channel_id=1, source_target_pairs={{0,24},{8,0},{16,8},{24,16},{32,56},{40,32},{48,40},{56,48},{64,88... | collective-permute-start | bytes 2457608 | tf_op jit(solution)/shard_map/ppermute | solution.py:61
  50.5 9.4 %collective-permute-start.1 = (bf16[64,3200]{1,0:T(8,128)(2,1)S(1)}, bf16[64,3200]{1,0:T(8,128)(2,1)S(1)}, u32[]{:S(2)}, u32[]{:S(2)}) collective-permute-start(bf16[64,3200]{1,0:T(8,128)(2,1)S(1)} %get-tuple-element.29), channel_id=1, source_target_pairs={{0,224},{8,232},{16,240},{24,248},{32,0},{40,8},{48,16},{56,24},{6... | collective-permute-start | bytes 1228808 | tf_op jit(solution)/shard_map/ppermute | solution.py:61
  54.2 10.7 %collective-permute-start = (bf16[64,3200]{1,0:T(8,128)(2,1)S(1)}, bf16[64,3200]{1,0:T(8,128)(2,1)S(1)}, u32[]{:S(2)}, u32[]{:S(2)}) collective-permute-start(bf16[64,3200]{1,0:T(8,128)(2,1)S(1)} %get-tuple-element.28), channel_id=1, source_target_pairs={{0,32},{8,40},{16,48},{24,56},{32,64},{40,72},{48,80},{56,88},{64,... | collective-permute-start | bytes 1228808 | tf_op jit(solution)/shard_map/ppermute | solution.py:61
  108.0 13.9 %copy-start.3 = (f32[16,1,128]{2,1,0:T(1,128)}, f32[16,1,128]{2,1,0:T(1,128)S(1)}, u32[]{:S(2)}) copy-start(f32[16,1,128]{2,1,0:T(1,128)S(1)} %all_to_all.36) | copy-start | bytes 24580

commit v5 on v4

--- a/solution.py
+++ b/solution.py
@@ -61,7 +61,10 @@
     return lax.ppermute(value, DP, pairs)
 
 
-def valid_copies_kernel(input_ref, preact_ref, upstream_ref, out_ref):
+def valid_copies_kernel(input_ref, preact_ref, upstream_ref, out_ref, mine_ref):
+    tensor = YL * CORE
+    member = lax.broadcasted_iota(jnp.int32, mine_ref.shape, 0)
+    mine_ref[...] = (member // tensor == lax.axis_index("yh")).astype(jnp.float32)
     split = input_ref.shape[1]
     joined = output_grad(preact_ref[...], upstream_ref[...])
     for member in range(out_ref.shape[0]):
@@ -73,11 +76,14 @@
     rows, split = valid_input.shape
     width = split + valid_preact.shape[1]
     members = YH * Z
-    copies = pl.pallas_call(
+    copies, mine = pl.pallas_call(
         valid_copies_kernel,
-        out_shape=jax.ShapeDtypeStruct((members, rows, width), jnp.bfloat16),
+        out_shape=(
+            jax.ShapeDtypeStruct((members, rows, width), jnp.bfloat16),
+            jax.ShapeDtypeStruct((YH * YL * CORE, LANES), jnp.float32),
+        ),
     )(valid_input, valid_preact, valid_upstream)
-    return exchange(copies.reshape(members * rows, width), DP, class_groups())
+    return exchange(copies.reshape(members * rows, width), DP, class_groups()), mine
 
 
 def neighbour_blocks(own):
@@ -113,19 +119,10 @@
     ]
 
 
-def finish_kernel(column_ref, planes_ref, first_ref, second_ref):
-    tensor = YL * CORE
-    start = pl.multiple_of(lax.axis_index("yh") * tensor, tensor)
-    first = jnp.sum(column_ref[pl.ds(start, tensor), :], axis=0, keepdims=True)
-    weight = jnp.sum(planes_ref[...], axis=0, keepdims=True)
-    first_ref[...] = first[:, :VAL_SEQS]
-    second_ref[...] = jnp.sum(first * weight, axis=1, keepdims=True)
-
-
 def per_device(
     train_input, train_preact, train_upstream, valid_input, valid_preact, valid_upstream
 ):
-    own = class_gather(valid_input, valid_preact, valid_upstream)
+    own, mine = class_gather(valid_input, valid_preact, valid_upstream)
     own, train_preact, train_upstream = lax.optimization_barrier(
         (own, train_preact, train_upstream)
     )
@@ -134,28 +131,25 @@
     split = valid_input.shape[1]
     parts = []
     for column in columns:
-        inputs = [cross_dot(train_input, b[:, :split]) * (1.0 / math.sqrt(D)) for b in column]
-        grads = [cross_dot(train_grad, b[:, split:]) * (1.0 / math.sqrt(FF)) for b in column]
-        parts += [jnp.concatenate(inputs, axis=1), jnp.concatenate(grads, axis=1)]
-    coded = encode(parts)
-    tensor = YL * CORE
-    coded = exchange(coded, TENSOR).reshape(tensor, -1, coded.shape[1])
+        parts += [cross_dot(train_input, b[:, :split]) * (1.0 / math.sqrt(D)) for b in column]
+        parts += [cross_dot(train_grad, b[:, split:]) * (1.0 / math.sqrt(FF)) for b in column]
+    parts = jnp.concatenate(parts, axis=1)
+    wide = parts.shape[1]
+    parts = jnp.sum(exchange(parts, "core").reshape(CORE, -1, wide), axis=0)
+    blocks = [parts[:, i : i + LANES] for i in range(0, wide, LANES)]
+    coded = encode(blocks)
+    coded = exchange(coded, "yl").reshape(YL, -1, coded.shape[1])
     summed = decode(coded)
     product = sum(summed[2 * i] * summed[2 * i + 1] for i in range(CLASSES))
     product = jnp.sum(product, axis=0).reshape(VAL_SEQS, LANES // VAL_SEQS)
     sums = jnp.sum(product, axis=1) * (1.0 / SEQ_LEN)
     lanes = jnp.pad(sums, (0, LANES - VAL_SEQS))[None]
-    column = exchange(jnp.broadcast_to(lanes, (YH * tensor, LANES)), ("yh",) + TENSOR)
-    total = jnp.sum(column, axis=0, keepdims=True)
+    column = exchange(jnp.broadcast_to(lanes, mine.shape), ("yh",) + TENSOR)
+    first = jnp.sum(column * mine, axis=0, keepdims=True)
+    total = first + jnp.sum(column * (1.0 - mine), axis=0, keepdims=True)
     planes = exchange(jnp.broadcast_to(total, (Z * X, LANES)), ("z", "x"))
-    first_order, second_order = pl.pallas_call(
-        finish_kernel,
-        out_shape=(
-            jax.ShapeDtypeStruct((1, VAL_SEQS), jnp.float32),
-            jax.ShapeDtypeStruct((1, 1), jnp.float32),
-        ),
-    )(column, planes)
-    return (first_order, second_order.reshape(1))
+    weight = jnp.sum(planes, axis=0, keepdims=True)
+    return (first[:, :VAL_SEQS], jnp.sum(first * weight, axis=1))
 
 
 def solution(mesh):

time: 124 us -> 120 us (0.968)
  waiting for transfers between devices: 7.42 us -> 3.85 us
  Pallas kernels: 3.15 us -> 1.81 us
    ppermute x4, waiting for transfers between devices: 7.42 us -> 3.85 us  [shift(): return lax.ppermute(value, DP, pairs)]
    pallas_call x2 -> x1, Pallas kernels: 3.15 us -> 1.81 us  [class_gather(): pl.pallas_call(valid_copies_kernel, out_shape=(jax.ShapeDtypeStruct((memb...]
    all_to_all x4 -> x5, blocking collectives: 92.8 us -> 93.1 us  [exchange(): lax.all_to_all(value, axes, 0, 0, axis_index_groups=groups, tiled=True)]
  transfers between devices with their start and end apart: 4 -> 4, of which waited for: 2 -> 2; matrix products, arithmetic and copies ran while one was open for 3% -> 4% of each run, Pallas kernels for 0% -> 0%
where the time goes in v5:
time: 120 us
  blocking collectives  93.1 us (78%)
  starting transfers between devices  13 us (11%)
  waiting for transfers between devices  3.85 us (3%)
  matrix products  3.83 us (3%)
  other arithmetic  2.55 us (2%)
  Pallas kernels  1.81 us (2%)
    all_to_all x5, blocking collectives, exchange(): lax.all_to_all(value, axes, 0, 0, axis_index_groups=groups, tiled=True)  93.1 us
    ppermute x4, starting transfers between devices, shift(): return lax.ppermute(value, DP, pairs)  13 us
    ppermute x4, waiting for transfers between devices, shift(): return lax.ppermute(value, DP, pairs)  3.85 us
    dot_general x10, matrix products, cross_dot(): lax.dot_general(left, right, (((1,), (1,)), ((), ())), preferred_element_...  3.83 us
  transfers between devices with their start and end apart: 4, of which 2 were waited for; matrix products, arithmetic and copies ran while one was open for 4% of the time, Pallas kernels for 0%

profile of v5, /device:TPU:1, one launch (start us, length us, event | category | flops | bytes accessed | tf_op | source)
XLA Modules:
  0.0 119.8 jit_solution(44565801032454253)
XLA Ops:
  0.6 1.8 %shard_map.77 = (bf16[16,8,3200]{2,1,0:T(8,128)(2,1)}, f32[16,128]{1,0:T(8,128)}) custom-call(bf16[8,640]{1,0:T(8,128)(2,1)} %input_ref.1, bf16[8,2560]{1,0:T(8,128)(2,1)} %preact_ref.1, bf16[8,2560]{1,0:T(8,128)(2,1)} %upstream_ref.1), custom_call_target="tpu_custom_call" | custom-call | tf_op jit(solution)/shard_map/pallas_call | solution.py:79
  2.5 40.1 %all_to_all.42 = bf16[16,8,3200]{2,1,0:T(8,128)(2,1)S(1)} all-to-all(bf16[16,8,3200]{2,1,0:T(8,128)(2,1)} %get-tuple-element.7), channel_id=1, replica_groups={{0,48,64,112,128,176,192,240,256,304,320,368,384,432,448,496},{8,56,72,..., dimensions={0} | all-to-all | bytes 1638400 | tf_op jit(solution)/shard_map/all_to_all | solution.py:40
  42.7 2.9 %collective-permute-start.2 = (bf16[128,3200]{1,0:T(8,128)(2,1)S(1)}, bf16[128,3200]{1,0:T(8,128)(2,1)S(1)}, u32[]{:S(2)}, u32[]{:S(2)}) collective-permute-start(bf16[128,3200]{1,0:T(8,128)(2,1)S(1)} %bitcast.51), channel_id=1, source_target_pairs={{0,8},{8,16},{16,24},{24,0},{32,40},{40,48},{48,56},{56,32},{64,72... | collective-permute-start | bytes 2457608 | tf_op jit(solution)/shard_map/ppermute | solution.py:61
  45.5 3.6 %collective-permute-start.3 = (bf16[128,3200]{1,0:T(8,128)(2,1)S(1)}, bf16[128,3200]{1,0:T(8,128)(2,1)S(1)}, u32[]{:S(2)}, u32[]{:S(2)}) collective-permute-start(bf16[128,3200]{1,0:T(8,128)(2,1)S(1)} %bitcast.52), channel_id=1, source_target_pairs={{0,24},{8,0},{16,8},{24,16},{32,56},{40,32},{48,40},{56,48},{64,88... | collective-permute-start | bytes 2457608 | tf_op jit(solution)/shard_map/ppermute | solution.py:61
  49.2 1.3 %fusion.7 = bf16[256,2560]{1,0:T(8,128)(2,1)S(1)} fusion(bf16[256,2560]{1,0:T(8,128)(2,1)S(1)} %copy-done.1, bf16[256,2560]{1,0:T(8,128)(2,1)S(1)} %copy-done.2), kind=kLoop, calls=%fused_computation.11 | loop fusion | flops 7864320 | bytes 3932160 | tf_op jit(solution)/shard_map/convert_element_type | solution.py:30
  50.5 1.9 %collective-permute-start = (bf16[64,3200]{1,0:T(8,128)(2,1)S(1)}, bf16[64,3200]{1,0:T(8,128)(2,1)S(1)}, u32[]{:S(2)}, u32[]{:S(2)}) collective-permute-start(bf16[64,3200]{1,0:T(8,128)(2,1)S(1)} %get-tuple-element.37), channel_id=1, source_target_pairs={{0,32},{8,40},{16,48},{24,56},{32,64},{40,72},{48,80},{56,88},{64,... | collective-permute-start | bytes 1228808 | tf_op jit(solution)/shard_map/ppermute | solution.py:61
  52.4 4.6 %collective-permute-start.1 = (bf16[64,3200]{1,0:T(8,128)(2,1)S(1)}, bf16[64,3200]{1,0:T(8,128)(2,1)S(1)}, u32[]{:S(2)}, u32[]{:S(2)}) collective-permute-start(bf16[64,3200]{1,0:T(8,128)(2,1)S(1)} %get-tuple-element.36), channel_id=1, source_target_pairs={{0,224},{8,232},{16,240},{24,248},{32,0},{40,8},{48,16},{56,24},{6... | collective-permute-start | bytes 1228808 | tf_op jit(solution)/shard_map/ppermute | solution.py:61
  57.0 0.2 fusion.13
  57.2 0.5 fusion.16
  57.8 2.9 %collective-permute-done = bf16[64,3200]{1,0:T(8,128)(2,1)S(1)} collective-permute-done((bf16[64,3200]{1,0:T(8,128)(2,1)S(1)}, bf16[64,3200]{1,0:T(8,128)(2,1)S(1)}, u32[]{:S(2)}, u32[]{:S(2)}) %collective-permute-start) | collective-permute-done | bytes 409632 | tf_op jit(solution)/shard_map/ppermute | solution.py:61
  60.9 1.0 collective-permute-done.1
  61.9 0.2 fusion.20
  62.1 0.5 fusion.18
  62.6 0.5 fusion.17
  63.1 0.2 fusion.11
  63.4 0.5 fusion.15
  64.0 0.2 fusion.9
  64.2 0.5 fusion.14
  64.8 10.3 %all_to_all.43 = f32[2,128,1024]{1,2,0:T(8,128)S(1)} all-to-all(f32[2,128,1024]{1,2,0:T(8,128)S(1)} %copy_bitcast_fusion), channel_id=1, replica_groups=mesh['yh'=2,'z'=8,'x'=4,'yl'=4,'core'=2] {'core'}, dimensions={0} | all-to-all | bytes 2097152 | tf_op jit(solution)/shard_map/all_to_all | solution.py:40
  75.6 0.3 copy.15
  75.9 17.1 %all_to_all.44 = f16[4,32,1152]{2,1,0:T(8,128)(2,1)S(1)} all-to-all(f16[4,32,1152]{2,1,0:T(8,128)(2,1)S(1)} %bitcast.55), channel_id=1, replica_groups=mesh['yh'=2,'z'=8,'x'=4,'yl'=4,'core'=2] {'yl'}, dimensions={0} | all-to-all | bytes 589824 | tf_op jit(solution)/shard_map/all_to_all | solution.py:40
  93.5 11.5 %all_to_all.45 = f32[16,1,128]{2,1,0:T(1,128)S(1)} all-to-all(f32[16,1,128]{2,1,0:T(1,128)S(1)} %broadcast_in_dim.6), channel_id=1, replica_groups=mesh['yh'=2,'z'=8,'x'=4,'yl'=4,'core'=2] {'yh','yl','core'}, dimensions={0} | all-to-all | bytes 16384 | tf_op jit(solution)/shard_map/all_to_all | solution.py:40
  105.1 14.1 %all_to_all.46 = f32[32,1,128]{2,1,0:T(1,128)S(1)} all-to-all(f32[32,1,128]{2,1,0:T(1,128)S(1)} %broadcast_in_dim.8), channel_id=1, replica_groups=mesh['yh'=2,'z'=8,'x'=4,'yl'=4,'core'=2] {'z','x'}, dimensions={0} | all-to-all | bytes 32768 | tf_op jit(solution)/shard_map/all_to_all | solution.py:40
  119.2 0.6 multiply_reduce_fusion.10
  (42 shorter events, 1.3 us)
Async XLA Ops:
  0.6 56.4 %copy-start = (bf16[256,640]{1,0:T(8,128)(2,1)S(1)}, bf16[256,640]{1,0:T(8,128)(2,1)}, u32[]{:S(2)}) copy-start(bf16[256,640]{1,0:T(8,128)(2,1)} %param.6) | copy-start | bytes 983044
  2.5 46.7 %copy-start.1 = (bf16[256,2560]{1,0:T(8,128)(2,1)S(1)}, bf16[256,2560]{1,0:T(8,128)(2,1)}, u32[]{:S(2)}) copy-start(bf16[256,2560]{1,0:T(8,128)(2,1)} %param.7) | copy-start | bytes 3932164
  2.5 46.7 %copy-start.2 = (bf16[256,2560]{1,0:T(8,128)(2,1)S(1)}, bf16[256,2560]{1,0:T(8,128)(2,1)}, u32[]{:S(2)}) copy-start(bf16[256,2560]{1,0:T(8,128)(2,1)} %param.8) | copy-start | bytes 3932164
  42.7 20.5 %collective-permute-start.2 = (bf16[128,3200]{1,0:T(8,128)(2,1)S(1)}, bf16[128,3200]{1,0:T(8,128)(2,1)S(1)}, u32[]{:S(2)}, u32[]{:S(2)}) collective-permute-start(bf16[128,3200]{1,0:T(8,128)(2,1)S(1)} %bitcast.51), channel_id=1, source_target_pairs={{0,8},{8,16},{16,24},{24,0},{32,40},{40,48},{48,56},{56,32},{64,72... | collective-permute-start | bytes 2457608 | tf_op jit(solution)/shard_map/ppermute | solution.py:61
  45.5 18.4 %collective-permute-start.3 = (bf16[128,3200]{1,0:T(8,128)(2,1)S(1)}, bf16[128,3200]{1,0:T(8,128)(2,1)S(1)}, u32[]{:S(2)}, u32[]{:S(2)}) collective-permute-start(bf16[128,3200]{1,0:T(8,128)(2,1)S(1)} %bitcast.52), channel_id=1, source_target_pairs={{0,24},{8,0},{16,8},{24,16},{32,56},{40,32},{48,40},{56,48},{64,88... | collective-permute-start | bytes 2457608 | tf_op jit(solution)/shard_map/ppermute | solution.py:61
  50.5 10.2 %collective-permute-start = (bf16[64,3200]{1,0:T(8,128)(2,1)S(1)}, bf16[64,3200]{1,0:T(8,128)(2,1)S(1)}, u32[]{:S(2)}, u32[]{:S(2)}) collective-permute-start(bf16[64,3200]{1,0:T(8,128)(2,1)S(1)} %get-tuple-element.37), channel_id=1, source_target_pairs={{0,32},{8,40},{16,48},{24,56},{32,64},{40,72},{48,80},{56,88},{64,... | collective-permute-start | bytes 1228808 | tf_op jit(solution)/shard_map/ppermute | solution.py:61
  52.4 9.5 %collective-permute-start.1 = (bf16[64,3200]{1,0:T(8,128)(2,1)S(1)}, bf16[64,3200]{1,0:T(8,128)(2,1)S(1)}, u32[]{:S(2)}, u32[]{:S(2)}) collective-permute-start(bf16[64,3200]{1,0:T(8,128)(2,1)S(1)} %get-tuple-element.36), channel_id=1, source_target_pairs={{0,224},{8,232},{16,240},{24,248},{32,0},{40,8},{48,16},{56,24},{6... | collective-permute-start | bytes 1228808 | tf_op jit(solution)/shard_map/ppermute | solution.py:61
  75.4 29.6 %copy-start.3 = (f32[16,128]{1,0:T(8,128)S(1)}, f32[16,128]{1,0:T(8,128)}, u32[]{:S(2)}) copy-start(f32[16,128]{1,0:T(8,128)} %get-tuple-element.11) | copy-start | bytes 24580
  105.0 14.8 %copy-start.4 = (f32[128]{0:T(128)}, f32[128]{0:T(128)S(1)}, u32[]{:S(2)}) copy-start(f32[128]{0:T(128)S(1)} %get-tuple-element.35) | copy-start | bytes 1540

commit v6 on v5

v6 whole, which is shorter than its diff:
```python
import math

import jax
import jax.numpy as jnp
from jax import lax
from jax.experimental import pallas as pl
from jax.sharding import Mesh, PartitionSpec as P

D = 5120
FF = 20480
SEQ_LEN = 256
VAL_SEQS = 2
DP = ("yh", "z", "x")
TENSOR = ("yl", "core")
YH, Z, X, YL, CORE = SIZES = (2, 8, 4, 4, 2)
CLASSES = 4
LANES = 128
TAIL = 8
LOW, HIGH = -126.0, 30.0

inv_root_two = 0.7071067811865476
inv_root_tau = 0.3989422804014327


def output_grad(preact, upstream):
    preact_f = preact.astype(jnp.float32)
    derivative = (
        0.5 * (1.0 + lax.erf(preact_f * inv_root_two))
        + preact_f * jnp.exp(-0.5 * preact_f * preact_f) * inv_root_tau
    )
    return (upstream.astype(jnp.float32) * derivative).astype(jnp.bfloat16)


def cross_dot(left, right):
    return lax.dot_general(
        left, right, (((1,), (1,)), ((), ())), preferred_element_type=jnp.float32
    )


def exchange(value, axes, groups=None):
    return lax.all_to_all(value, axes, 0, 0, axis_index_groups=groups, tiled=True)


def place(yh, z, x):
    return (yh * Z + z % Z) * X + x % X


def device(yh, z, x, yl, core):
    return (((yh * Z + z % Z) * X + x % X) * YL + yl) * CORE + core


def class_groups():
    groups = []
    for kind in range(CLASSES):
        for yl in range(YL):
            groups.append(
                [device(yh, z, kind - 2 * z, yl, 0) for yh in range(YH) for z in range(Z)]
            )
            groups.append(
                [
                    device(yh, (kind - 2 * x) % 4 + 4 * far, x, yl, 1)
                    for yh in range(YH)
                    for x in range(X)
                    for far in range(2)
                ]
            )
    return groups


def shift(value, major, minor):
    pairs = []
    for yh in range(YH):
        for z in range(Z):
            for x in range(X):
                for yl in range(YL):
                    pairs.append(
                        (device(yh, z, x, yl, 0), device(yh, z + minor, x + major, yl, 0))
                    )
                    pairs.append(
                        (device(yh, z, x, yl, 1), device(yh, z + major, x + minor, yl, 1))
                    )
    return lax.ppermute(value, DP + TENSOR, pairs)


def valid_copies_kernel(input_ref, preact_ref, upstream_ref, out_ref, mine_ref):
    tensor = YL * CORE
    member = lax.broadcasted_iota(jnp.int32, mine_ref.shape, 0)
    mine_ref[...] = (member // tensor == lax.axis_index("yh")).astype(jnp.float32)
    split = input_ref.shape[1]
    joined = output_grad(preact_ref[...], upstream_ref[...])
    for member in range(out_ref.shape[0]):
        out_ref[member, :, :split] = input_ref[...]
        out_ref[member, :, split:] = joined


def class_gather(valid_input, valid_preact, valid_upstream):
    rows, split = valid_input.shape
    width = split + valid_preact.shape[1]
    members = YH * Z
    copies, mine = pl.pallas_call(
        valid_copies_kernel,
        out_shape=(
            jax.ShapeDtypeStruct((members, rows, width), jnp.bfloat16),
            jax.ShapeDtypeStruct((YH * YL * CORE, LANES), jnp.float32),
        ),
    )(valid_input, valid_preact, valid_upstream)
    return exchange(
        copies.reshape(members * rows, width), DP + TENSOR, class_groups()
    ), mine


def neighbour_blocks(own):
    half = own.shape[0] // 2
    back, on = shift(own, 1, 0), shift(own, -1, 0)
    across = [shift(own[:half], 0, 1), shift(own[half:], 0, -1)]
    return [own, jnp.concatenate(across), back, on]


def align_kernel(pieces_ref, out_ref):
    z, x = lax.axis_index("z"), lax.axis_index("x")
    tile = out_ref.shape[0] // (CLASSES * 2 * YH * Z)
    for place0, step in enumerate((0, 2, 3, 1)):
        for source_z in range(Z):
            source_x = (x + 2 * z + step - 2 * source_z + 16) & 3
            turn = (2 * source_x + source_z - 2 * x - z + 16) & 3
            place1 = jnp.where(turn == 1, 3, jnp.where(turn == 2, 1, jnp.where(turn == 3, 2, 0)))
            other = place1 * (2 * YH * Z) + 2 * source_x + source_z // 4
            for part in range(2 * YH):
                here = (place0 * 2 * YH * Z + part * Z + source_z) * tile
                there = pl.multiple_of((other + part * Z) * tile, tile)
                out_ref[here : here + tile, :] = (
                    pieces_ref[0, here : here + tile, :] + pieces_ref[1, pl.ds(there, tile), :]
                )


def encode(parts):
    largest = jnp.max(jnp.abs(parts), axis=2)
    exponents = jnp.clip(jnp.ceil(jnp.log2(jnp.maximum(largest, 2.0**LOW))), LOW, HIGH)
    scaled = (parts * jnp.exp2(-exponents)[:, :, None]).astype(jnp.float16)
    blocks, kinds, rows, lanes = parts.shape
    tail = jnp.pad(exponents, ((0, 0), (0, TAIL - kinds), (0, 0))).astype(jnp.float16)
    return jnp.concatenate([scaled.reshape(blocks, kinds * rows, lanes), tail], axis=1)


def decode(coded, kinds):
    count, rows, lanes = coded.shape
    rows -= TAIL
    scale = jnp.exp2(coded[:, rows : rows + kinds].astype(jnp.float32))
    values = coded[:, :rows].astype(jnp.float32).reshape(count, kinds, rows // kinds, lanes)
    return jnp.sum(values * scale[:, :, None], axis=0)


def per_device(
    train_input, train_preact, train_upstream, valid_input, valid_preact, valid_upstream
):
    own, mine = class_gather(valid_input, valid_preact, valid_upstream)
    own, train_preact, train_upstream = lax.optimization_barrier(
        (own, train_preact, train_upstream)
    )
    blocks = neighbour_blocks(own)
    train_grad = lax.optimization_barrier(output_grad(train_preact, train_upstream))
    split = valid_input.shape[1]
    parts = []
    for block in blocks:
        parts.append(cross_dot(block[:, :split], train_input) * (1.0 / math.sqrt(D)))
        parts.append(cross_dot(block[:, split:], train_grad) * (1.0 / math.sqrt(FF)))
    parts = jnp.concatenate(parts)
    rows = parts.shape[0]
    pieces = jnp.stack(jnp.split(parts, CORE, axis=1))
    pieces = exchange(pieces, "core")
    parts = pl.pallas_call(
        align_kernel,
        out_shape=jax.ShapeDtypeStruct(pieces.shape[1:], jnp.float32),
    )(pieces)
    coded = encode(parts.reshape(CLASSES, 2, rows // (2 * CLASSES), -1))
    input_kernel, grad_kernel = decode(exchange(coded, "yl"), 2)
    product = (input_kernel * grad_kernel).reshape(VAL_SEQS, -1, input_kernel.shape[1])
    sums = jnp.sum(product, axis=(1, 2)) * (1.0 / SEQ_LEN)
    lanes = jnp.pad(sums, (0, LANES - VAL_SEQS))[None]
    column = exchange(jnp.broadcast_to(lanes, mine.shape), ("yh",) + TENSOR)
    first = jnp.sum(column * mine, axis=0, keepdims=True)
    total = first + jnp.sum(column * (1.0 - mine), axis=0, keepdims=True)
    planes = exchange(jnp.broadcast_to(total, (Z * X, LANES)), ("z", "x"))
    weight = jnp.sum(planes, axis=0, keepdims=True)
    return (first[:, :VAL_SEQS], jnp.sum(first * weight, axis=1))


def solution(mesh):
    fine = Mesh(mesh.devices.reshape(SIZES), DP + TENSOR)
    return jax.shard_map(
        per_device,
        mesh=fine,
        in_specs=(P(DP, TENSOR),) * 6,
        out_specs=(P(DP, None), P(DP)),
        check_vma=False,
    )
```

time: 120 us -> 124 us (1.033)
  blocking collectives: 93.1 us -> 90.1 us
  Pallas kernels: 1.81 us -> 4 us
  other arithmetic: 2.55 us -> 4.55 us
  starting transfers between devices: 13 us -> 14.8 us
  waiting for transfers between devices: 3.85 us -> 5.31 us
    all_to_all x5, blocking collectives: 93.1 us -> 90.1 us  [exchange(): lax.all_to_all(value, axes, 0, 0, axis_index_groups=groups, tiled=True)]
    pallas_call x0 -> x1, Pallas kernels: none -> 2.19 us  [per_device(): pl.pallas_call(align_kernel, out_shape=jax.ShapeDtypeStruct(pieces.shape[...]
    ppermute x4, starting transfers between devices: 13 us -> 14.8 us  [shift(): return lax.ppermute(value, DP + TENSOR, pairs)]
    ppermute x4, waiting for transfers between devices: 3.85 us -> 5.31 us  [shift(): return lax.ppermute(value, DP + TENSOR, pairs)]
    dot_general x10 -> x8, matrix products: 3.83 us -> 3.17 us  [cross_dot(): lax.dot_general(left, right, (((1,), (1,)), ((), ())), preferred_element_...]
  transfers between devices with their start and end apart: 4 -> 4, of which waited for: 2 -> 2; matrix products, arithmetic and copies ran while one was open for 4% -> 3% of each run, Pallas kernels for 0% -> 0%
where the time goes in v6:
time: 124 us; the launch traced here: 123 us
  blocking collectives  90.1 us (73%)
  starting transfers between devices  14.8 us (12%)
  waiting for transfers between devices  5.31 us (4%)
  other arithmetic  4.55 us (4%)
  Pallas kernels  4 us (3%)
  matrix products  3.17 us (3%)
    all_to_all x5, blocking collectives, exchange(): lax.all_to_all(value, axes, 0, 0, axis_index_groups=groups, tiled=True)  90.1 us
    ppermute x4, starting transfers between devices, shift(): return lax.ppermute(value, DP + TENSOR, pairs)  14.8 us
    ppermute x4, waiting for transfers between devices, shift(): return lax.ppermute(value, DP + TENSOR, pairs)  5.31 us
    dot_general x8, matrix products, cross_dot(): lax.dot_general(left, right, (((1,), (1,)), ((), ())), preferred_element_...  3.17 us
  transfers between devices with their start and end apart: 4, of which 2 were waited for; matrix products, arithmetic and copies ran while one was open for 3% of the time, Pallas kernels for 0%

profile of v6, /device:TPU:1, one launch (start us, length us, event | category | flops | bytes accessed | tf_op | source)
XLA Modules:
  0.0 123.2 jit_solution(13202793326006999424)
XLA Ops:
  0.6 1.8 %shard_map.77 = (bf16[16,8,3200]{2,1,0:T(8,128)(2,1)}, f32[16,128]{1,0:T(8,128)}) custom-call(bf16[8,640]{1,0:T(8,128)(2,1)} %input_ref.1, bf16[8,2560]{1,0:T(8,128)(2,1)} %preact_ref.1, bf16[8,2560]{1,0:T(8,128)(2,1)} %upstream_ref.1), custom_call_target="tpu_custom_call" | custom-call | tf_op jit(solution)/shard_map/pallas_call | solution.py:100
  2.5 43.9 %all_to_all.34 = bf16[16,8,3200]{2,1,0:T(8,128)(2,1)S(1)} all-to-all(bf16[16,8,3200]{2,1,0:T(8,128)(2,1)} %get-tuple-element.7), channel_id=1, replica_groups={{0,48,64,112,128,176,192,240,256,304,320,368,384,432,448,496},{1,129,73..., dimensions={0} | all-to-all | bytes 1638400 | tf_op jit(solution)/shard_map/all_to_all | solution.py:41
  46.4 2.7 %collective-permute-start.2 = (bf16[128,3200]{1,0:T(8,128)(2,1)S(1)}, bf16[128,3200]{1,0:T(8,128)(2,1)S(1)}, u32[]{:S(2)}, u32[]{:S(2)}) collective-permute-start(bf16[128,3200]{1,0:T(8,128)(2,1)S(1)} %bitcast.30), channel_id=1, source_target_pairs={{0,8},{1,33},{2,10},{3,35},{4,12},{5,37},{6,14},{7,39},{8,16},{9,4... | collective-permute-start | bytes 2457608 | tf_op jit(solution)/shard_map/ppermute | solution.py:82
  49.2 3.7 %collective-permute-start.3 = (bf16[128,3200]{1,0:T(8,128)(2,1)S(1)}, bf16[128,3200]{1,0:T(8,128)(2,1)S(1)}, u32[]{:S(2)}, u32[]{:S(2)}) collective-permute-start(bf16[128,3200]{1,0:T(8,128)(2,1)S(1)} %bitcast.31), channel_id=1, source_target_pairs={{0,24},{1,225},{2,26},{3,227},{4,28},{5,229},{6,30},{7,231},{8,0},... | collective-permute-start | bytes 2457608 | tf_op jit(solution)/shard_map/ppermute | solution.py:82
  53.0 1.3 %fusion.7 = bf16[256,2560]{1,0:T(8,128)(2,1)S(1)} fusion(bf16[256,2560]{1,0:T(8,128)(2,1)S(1)} %copy-done.1, bf16[256,2560]{1,0:T(8,128)(2,1)S(1)} %copy-done.2), kind=kLoop, calls=%fused_computation.11 | loop fusion | flops 7864320 | bytes 3932160 | tf_op jit(solution)/shard_map/convert_element_type | solution.py:31
  54.3 2.3 %collective-permute-start = (bf16[64,3200]{1,0:T(8,128)(2,1)S(1)}, bf16[64,3200]{1,0:T(8,128)(2,1)S(1)}, u32[]{:S(2)}, u32[]{:S(2)}) collective-permute-start(bf16[64,3200]{1,0:T(8,128)(2,1)S(1)} %get-tuple-element.17), channel_id=1, source_target_pairs={{0,32},{1,9},{2,34},{3,11},{4,36},{5,13},{6,38},{7,15},{8,40},{9,1... | collective-permute-start | bytes 1228808 | tf_op jit(solution)/shard_map/ppermute | solution.py:82
  56.6 6.0 %collective-permute-start.1 = (bf16[64,3200]{1,0:T(8,128)(2,1)S(1)}, bf16[64,3200]{1,0:T(8,128)(2,1)S(1)}, u32[]{:S(2)}, u32[]{:S(2)}) collective-permute-start(bf16[64,3200]{1,0:T(8,128)(2,1)S(1)} %get-tuple-element.16), channel_id=1, source_target_pairs={{0,224},{1,25},{2,226},{3,27},{4,228},{5,29},{6,230},{7,31},{8,232... | collective-permute-start | bytes 1228808 | tf_op jit(solution)/shard_map/ppermute | solution.py:82
  62.6 0.2 fusion.11
  62.9 0.5 fusion.15
  63.4 3.6 %collective-permute-done = bf16[64,3200]{1,0:T(8,128)(2,1)S(1)} collective-permute-done((bf16[64,3200]{1,0:T(8,128)(2,1)S(1)}, bf16[64,3200]{1,0:T(8,128)(2,1)S(1)}, u32[]{:S(2)}, u32[]{:S(2)}) %collective-permute-start) | collective-permute-done | bytes 409632 | tf_op jit(solution)/shard_map/ppermute | solution.py:82
  67.0 1.7 %collective-permute-done.1 = bf16[64,3200]{1,0:T(8,128)(2,1)S(1)} collective-permute-done((bf16[64,3200]{1,0:T(8,128)(2,1)S(1)}, bf16[64,3200]{1,0:T(8,128)(2,1)S(1)}, u32[]{:S(2)}, u32[]{:S(2)}) %collective-permute-start.1) | collective-permute-done | bytes 409632 | tf_op jit(solution)/shard_map/ppermute | solution.py:82
  68.8 0.2 fusion.10
  69.0 0.5 fusion.14
  69.6 0.2 fusion.9
  69.9 0.5 fusion.13
  70.7 0.5 fusion.12
  71.4 5.0 %all_to_all.35.pieces_ref = f32[2,1024,128]{2,1,0:T(8,128)} all-to-all(f32[2,1024,128]{2,1,0:T(8,128)S(1)} %pad_maximum_fusion), channel_id=1, replica_groups=mesh['yh'=2,'z'=8,'x'=4,'yl'=4,'core'=2] {'core'}, dimensions={0} | all-to-all | bytes 2097152 | tf_op jit(solution)/shard_map/all_to_all | solution.py:41
  76.4 2.2 %shard_map.78 = f32[1024,128]{1,0:T(8,128)} custom-call(f32[2,1024,128]{2,1,0:T(8,128)} %all_to_all.35.pieces_ref), custom_call_target="tpu_custom_call" | custom-call | tf_op jit(solution)/shard_map/pallas_call | solution.py:171
  78.6 1.1 bitcast_reduce_fusion
  79.7 1.1 fusion.22
  80.9 14.6 %all_to_all.36 = f16[4,264,128]{2,1,0:T(8,128)(2,1)S(1)} all-to-all(f16[4,264,128]{2,1,0:T(8,128)(2,1)S(1)} %fusion.23), channel_id=1, replica_groups=mesh['yh'=2,'z'=8,'x'=4,'yl'=4,'core'=2] {'yl'}, dimensions={0} | all-to-all | bytes 540672 | tf_op jit(solution)/shard_map/all_to_all | solution.py:41
  95.9 11.9 %all_to_all.37 = f32[16,1,128]{2,1,0:T(1,128)S(1)} all-to-all(f32[16,1,128]{2,1,0:T(1,128)S(1)} %broadcast_in_dim.6), channel_id=1, replica_groups=mesh['yh'=2,'z'=8,'x'=4,'yl'=4,'core'=2] {'yh','yl','core'}, dimensions={0} | all-to-all | bytes 16384 | tf_op jit(solution)/shard_map/all_to_all | solution.py:41
  107.9 14.7 %all_to_all.38 = f32[32,1,128]{2,1,0:T(1,128)S(1)} all-to-all(f32[32,1,128]{2,1,0:T(1,128)S(1)} %broadcast_in_dim.8), channel_id=1, replica_groups=mesh['yh'=2,'z'=8,'x'=4,'yl'=4,'core'=2] {'z','x'}, dimensions={0} | all-to-all | bytes 32768 | tf_op jit(solution)/shard_map/all_to_all | solution.py:41
  122.6 0.6 multiply_reduce_fusion.2
  (32 shorter events, 1.0 us)
Async XLA Ops:
  0.6 62.0 %copy-start = (bf16[256,640]{1,0:T(8,128)(2,1)S(1)}, bf16[256,640]{1,0:T(8,128)(2,1)}, u32[]{:S(2)}) copy-start(bf16[256,640]{1,0:T(8,128)(2,1)} %param.6) | copy-start | bytes 983044
  2.5 50.5 %copy-start.1 = (bf16[256,2560]{1,0:T(8,128)(2,1)S(1)}, bf16[256,2560]{1,0:T(8,128)(2,1)}, u32[]{:S(2)}) copy-start(bf16[256,2560]{1,0:T(8,128)(2,1)} %param.7) | copy-start | bytes 3932164
  2.5 50.5 %copy-start.2 = (bf16[256,2560]{1,0:T(8,128)(2,1)S(1)}, bf16[256,2560]{1,0:T(8,128)(2,1)}, u32[]{:S(2)}) copy-start(bf16[256,2560]{1,0:T(8,128)(2,1)} %param.8) | copy-start | bytes 3932164
  46.4 23.2 %collective-permute-start.2 = (bf16[128,3200]{1,0:T(8,128)(2,1)S(1)}, bf16[128,3200]{1,0:T(8,128)(2,1)S(1)}, u32[]{:S(2)}, u32[]{:S(2)}) collective-permute-start(bf16[128,3200]{1,0:T(8,128)(2,1)S(1)} %bitcast.30), channel_id=1, source_target_pairs={{0,8},{1,33},{2,10},{3,35},{4,12},{5,37},{6,14},{7,39},{8,16},{9,4... | collective-permute-start | bytes 2457608 | tf_op jit(solution)/shard_map/ppermute | solution.py:82
  49.2 21.2 %collective-permute-start.3 = (bf16[128,3200]{1,0:T(8,128)(2,1)S(1)}, bf16[128,3200]{1,0:T(8,128)(2,1)S(1)}, u32[]{:S(2)}, u32[]{:S(2)}) collective-permute-start(bf16[128,3200]{1,0:T(8,128)(2,1)S(1)} %bitcast.31), channel_id=1, source_target_pairs={{0,24},{1,225},{2,26},{3,227},{4,28},{5,229},{6,30},{7,231},{8,0},... | collective-permute-start | bytes 2457608 | tf_op jit(solution)/shard_map/ppermute | solution.py:82
  54.3 12.7 %collective-permute-start = (bf16[64,3200]{1,0:T(8,128)(2,1)S(1)}, bf16[64,3200]{1,0:T(8,128)(2,1)S(1)}, u32[]{:S(2)}, u32[]{:S(2)}) collective-permute-start(bf16[64,3200]{1,0:T(8,128)(2,1)S(1)} %get-tuple-element.17), channel_id=1, source_target_pairs={{0,32},{1,9},{2,34},{3,11},{4,36},{5,13},{6,38},{7,15},{8,40},{9,1... | collective-permute-start | bytes 1228808 | tf_op jit(solution)/shard_map/ppermute | solution.py:82
  56.6 12.1 %collective-permute-start.1 = (bf16[64,3200]{1,0:T(8,128)(2,1)S(1)}, bf16[64,3200]{1,0:T(8,128)(2,1)S(1)}, u32[]{:S(2)}, u32[]{:S(2)}) collective-permute-start(bf16[64,3200]{1,0:T(8,128)(2,1)S(1)} %get-tuple-element.16), channel_id=1, source_target_pairs={{0,224},{1,25},{2,226},{3,27},{4,228},{5,29},{6,230},{7,31},{8,232... | collective-permute-start | bytes 1228808 | tf_op jit(solution)/shard_map/ppermute | solution.py:82
  79.7 28.2 %copy-start.3 = (f32[16,128]{1,0:T(8,128)S(1)}, f32[16,128]{1,0:T(8,128)}, u32[]{:S(2)}) copy-start(f32[16,128]{1,0:T(8,128)} %get-tuple-element.11) | copy-start | bytes 24580
  107.9 15.3 %copy-start.4 = (f32[128]{0:T(128)}, f32[128]{0:T(128)S(1)}, u32[]{:S(2)}) copy-start(f32[128]{0:T(128)S(1)} %get-tuple-element.13) | copy-start | bytes 1540

commit v7 on v5

--- a/solution.py
+++ b/solution.py
@@ -15,6 +15,7 @@
 YH, Z, X, YL, CORE = SIZES = (2, 8, 4, 4, 2)
 CLASSES = 4
 LANES = 128
+TAIL = 8
 LOW, HIGH = -126.0, 30.0
 
 inv_root_two = 0.7071067811865476
@@ -86,37 +87,29 @@
     return exchange(copies.reshape(members * rows, width), DP, class_groups()), mine
 
 
-def neighbour_blocks(own):
+def neighbour_rows(own):
     half = own.shape[0] // 2
     right, left = shift(own, 0, 1), shift(own, 0, -1)
     above, below = shift(own[:half], 1, 0), shift(own[half:], -1, 0)
-    return [[own], [above, below], [right], [left]]
+    return jnp.concatenate([above, below, right, left])
 
 
 def encode(parts):
-    kinds = [parts[0::2], parts[1::2]]
-    largest = jnp.stack(
-        [jnp.max(jnp.stack([jnp.max(jnp.abs(p), axis=1) for p in kind]), axis=0) for kind in kinds],
-        axis=1,
-    )
+    kinds, blocks, rows, lanes = parts.shape
+    largest = jnp.max(jnp.abs(parts), axis=2)
     exponents = jnp.clip(jnp.ceil(jnp.log2(jnp.maximum(largest, 2.0**LOW))), LOW, HIGH)
-    scale = jnp.exp2(-exponents)
-    scaled = [(p * scale[:, i % 2, None]).astype(jnp.float16) for i, p in enumerate(parts)]
-    tail = jnp.pad(exponents, ((0, 0), (0, LANES - 2))).astype(jnp.float16)
-    return jnp.concatenate(scaled + [tail], axis=1)
+    scale = jnp.exp2(-exponents)[:, :, None]
+    scaled = [(parts[kind] * scale[kind]).astype(jnp.float16) for kind in range(kinds)]
+    tail = jnp.pad(exponents.transpose(1, 0, 2), ((0, 0), (0, TAIL - kinds), (0, 0)))
+    return jnp.concatenate(scaled + [tail.astype(jnp.float16)], axis=1)
 
 
-def decode(coded):
-    blocks = 2 * CLASSES
-    scale = jnp.exp2(coded[:, :, blocks * LANES : blocks * LANES + 2].astype(jnp.float32))
-    return [
-        jnp.sum(
-            coded[:, :, i * LANES : (i + 1) * LANES].astype(jnp.float32)
-            * scale[:, :, i % 2, None],
-            axis=0,
-        )
-        for i in range(blocks)
-    ]
+def decode(coded, kinds):
+    count, rows, lanes = coded.shape
+    rows -= TAIL
+    scale = jnp.exp2(coded[:, rows : rows + kinds].astype(jnp.float32))
+    values = coded[:, :rows].astype(jnp.float32).reshape(count, kinds, rows // kinds, lanes)
+    return jnp.sum(values * scale[:, :, None], axis=0)
 
 
 def per_device(
@@ -126,23 +119,18 @@
     own, train_preact, train_upstream = lax.optimization_barrier(
         (own, train_preact, train_upstream)
     )
-    columns = neighbour_blocks(own)
+    foreign = neighbour_rows(own)
     train_grad = lax.optimization_barrier(output_grad(train_preact, train_upstream))
     split = valid_input.shape[1]
-    parts = []
-    for column in columns:
-        parts += [cross_dot(train_input, b[:, :split]) * (1.0 / math.sqrt(D)) for b in column]
-        parts += [cross_dot(train_grad, b[:, split:]) * (1.0 / math.sqrt(FF)) for b in column]
-    parts = jnp.concatenate(parts, axis=1)
-    wide = parts.shape[1]
-    parts = jnp.sum(exchange(parts, "core").reshape(CORE, -1, wide), axis=0)
-    blocks = [parts[:, i : i + LANES] for i in range(0, wide, LANES)]
-    coded = encode(blocks)
-    coded = exchange(coded, "yl").reshape(YL, -1, coded.shape[1])
-    summed = decode(coded)
-    product = sum(summed[2 * i] * summed[2 * i + 1] for i in range(CLASSES))
-    product = jnp.sum(product, axis=0).reshape(VAL_SEQS, LANES // VAL_SEQS)
-    sums = jnp.sum(product, axis=1) * (1.0 / SEQ_LEN)
+    input_scale, grad_scale = 1.0 / math.sqrt(D), 1.0 / math.sqrt(FF)
+    parts = [cross_dot(rows[:, :split], train_input) * input_scale for rows in (own, foreign)]
+    parts += [cross_dot(rows[:, split:], train_grad) * grad_scale for rows in (own, foreign)]
+    pieces = jnp.stack(jnp.split(jnp.concatenate(parts), CORE, axis=1))
+    parts = jnp.sum(exchange(pieces, "core"), axis=0)
+    coded = encode(parts.reshape(2, CLASSES, -1, parts.shape[1]))
+    input_kernel, grad_kernel = decode(exchange(coded, "yl"), 2)
+    product = (input_kernel * grad_kernel).reshape(VAL_SEQS, -1, input_kernel.shape[1])
+    sums = jnp.sum(product, axis=(1, 2)) * (1.0 / SEQ_LEN)
     lanes = jnp.pad(sums, (0, LANES - VAL_SEQS))[None]
     column = exchange(jnp.broadcast_to(lanes, mine.shape), ("yh",) + TENSOR)
     first = jnp.sum(column * mine, axis=0, keepdims=True)

time: 120 us -> 120 us (level)
  matrix products: 3.83 us -> 1.85 us
  waiting for transfers between devices: 3.85 us -> 5.17 us
    dot_general x10 -> x4, matrix products: 3.83 us -> 1.85 us  [cross_dot(): lax.dot_general(left, right, (((1,), (1,)), ((), ())), preferred_element_...]
    ppermute x4, waiting for transfers between devices: 3.85 us -> 5.17 us  [shift(): return lax.ppermute(value, DP, pairs)]
  transfers between devices with their start and end apart: 4 -> 4, of which waited for: 2 -> 4; matrix products, arithmetic and copies ran while one was open for 4% -> 2% of each run, Pallas kernels for 0% -> 0%
where the time goes in v7:
time: 120 us; the launch traced here: 119 us
  blocking collectives  93.1 us (78%)
  starting transfers between devices  13 us (11%)
  waiting for transfers between devices  5.17 us (4%)
  other arithmetic  2.67 us (2%)
  Pallas kernels  1.92 us (2%)
  matrix products  1.85 us (2%)
    all_to_all x5, blocking collectives, exchange(): lax.all_to_all(value, axes, 0, 0, axis_index_groups=groups, tiled=True)  93.1 us
    ppermute x4, starting transfers between devices, shift(): return lax.ppermute(value, DP, pairs)  13 us
    ppermute x4, waiting for transfers between devices, shift(): return lax.ppermute(value, DP, pairs)  5.17 us
  transfers between devices with their start and end apart: 4, of which 4 were waited for; matrix products, arithmetic and copies ran while one was open for 2% of the time, Pallas kernels for 0%

profile of v7, /device:TPU:1, one launch (start us, length us, event | category | flops | bytes accessed | tf_op | source)
XLA Modules:
  0.0 119.2 jit_solution(4660541020463652458)
XLA Ops:
  0.7 1.9 %shard_map.77 = (bf16[16,8,3200]{2,1,0:T(8,128)(2,1)}, f32[16,128]{1,0:T(8,128)}) custom-call(bf16[8,640]{1,0:T(8,128)(2,1)} %input_ref.1, bf16[8,2560]{1,0:T(8,128)(2,1)} %preact_ref.1, bf16[8,2560]{1,0:T(8,128)(2,1)} %upstream_ref.1), custom_call_target="tpu_custom_call" | custom-call | tf_op jit(solution)/shard_map/pallas_call | solution.py:80
  2.6 39.9 %all_to_all.34 = bf16[16,8,3200]{2,1,0:T(8,128)(2,1)S(1)} all-to-all(bf16[16,8,3200]{2,1,0:T(8,128)(2,1)} %get-tuple-element.7), channel_id=1, replica_groups={{0,48,64,112,128,176,192,240,256,304,320,368,384,432,448,496},{8,56,72,..., dimensions={0} | all-to-all | bytes 1638400 | tf_op jit(solution)/shard_map/all_to_all | solution.py:41
  42.5 2.9 %collective-permute-start.2 = (bf16[128,3200]{1,0:T(8,128)(2,1)S(1)}, bf16[128,3200]{1,0:T(8,128)(2,1)S(1)}, u32[]{:S(2)}, u32[]{:S(2)}) collective-permute-start(bf16[128,3200]{1,0:T(8,128)(2,1)S(1)} %bitcast.29), channel_id=1, source_target_pairs={{0,8},{8,16},{16,24},{24,0},{32,40},{40,48},{48,56},{56,32},{64,72... | collective-permute-start | bytes 2457608 | tf_op jit(solution)/shard_map/ppermute | solution.py:62
  45.4 3.6 %collective-permute-start.3 = (bf16[128,3200]{1,0:T(8,128)(2,1)S(1)}, bf16[128,3200]{1,0:T(8,128)(2,1)S(1)}, u32[]{:S(2)}, u32[]{:S(2)}) collective-permute-start(bf16[128,3200]{1,0:T(8,128)(2,1)S(1)} %bitcast.30), channel_id=1, source_target_pairs={{0,24},{8,0},{16,8},{24,16},{32,56},{40,32},{48,40},{56,48},{64,88... | collective-permute-start | bytes 2457608 | tf_op jit(solution)/shard_map/ppermute | solution.py:62
  49.0 1.9 %collective-permute-start = (bf16[64,3200]{1,0:T(8,128)(2,1)S(1)}, bf16[64,3200]{1,0:T(8,128)(2,1)S(1)}, u32[]{:S(2)}, u32[]{:S(2)}) collective-permute-start(bf16[64,3200]{1,0:T(8,128)(2,1)S(1)} %get-tuple-element.17), channel_id=1, source_target_pairs={{0,32},{8,40},{16,48},{24,56},{32,64},{40,72},{48,80},{56,88},{64,... | collective-permute-start | bytes 1228808 | tf_op jit(solution)/shard_map/ppermute | solution.py:62
  50.9 4.6 %collective-permute-start.1 = (bf16[64,3200]{1,0:T(8,128)(2,1)S(1)}, bf16[64,3200]{1,0:T(8,128)(2,1)S(1)}, u32[]{:S(2)}, u32[]{:S(2)}) collective-permute-start(bf16[64,3200]{1,0:T(8,128)(2,1)S(1)} %get-tuple-element.16), channel_id=1, source_target_pairs={{0,224},{8,232},{16,240},{24,248},{32,0},{40,8},{48,16},{56,24},{6... | collective-permute-start | bytes 1228808 | tf_op jit(solution)/shard_map/ppermute | solution.py:62
  55.5 1.3 %fusion.7 = bf16[256,2560]{1,0:T(8,128)(2,1)S(1)} fusion(bf16[256,2560]{1,0:T(8,128)(2,1)S(1)} %copy-done.1, bf16[256,2560]{1,0:T(8,128)(2,1)S(1)} %copy-done.2), kind=kLoop, calls=%fused_computation.11 | loop fusion | flops 7864320 | bytes 3932160 | tf_op jit(solution)/shard_map/convert_element_type | solution.py:31
  56.8 0.2 convolution_multiply_fusion.1
  57.1 0.5 convolution_multiply_fusion.2
  57.7 1.6 %collective-permute-done = bf16[64,3200]{1,0:T(8,128)(2,1)S(1)} collective-permute-done((bf16[64,3200]{1,0:T(8,128)(2,1)S(1)}, bf16[64,3200]{1,0:T(8,128)(2,1)S(1)}, u32[]{:S(2)}, u32[]{:S(2)}) %collective-permute-start) | collective-permute-done | bytes 409632 | tf_op jit(solution)/shard_map/ppermute | solution.py:62
  59.3 1.1 collective-permute-done.1
  60.4 0.5 collective-permute-done.2
  61.0 0.1 constant_dynamic-update-slice_fusion.1
  61.1 1.9 %collective-permute-done.3 = bf16[128,3200]{1,0:T(8,128)(2,1)S(1)} collective-permute-done((bf16[128,3200]{1,0:T(8,128)(2,1)S(1)}, bf16[128,3200]{1,0:T(8,128)(2,1)S(1)}, u32[]{:S(2)}, u32[]{:S(2)}) %collective-permute-start.3) | collective-permute-done | bytes 819232 | tf_op jit(solution)/shard_map/ppermute | solution.py:62
  63.1 0.7 fusion.10
  63.8 0.4 convolution_multiply_fusion
  64.4 9.2 %all_to_all.35 = f32[2,1024,128]{2,1,0:T(8,128)S(1)} all-to-all(f32[2,1024,128]{2,1,0:T(8,128)S(1)} %pad_maximum_fusion.1), channel_id=1, replica_groups=mesh['yh'=2,'z'=8,'x'=4,'yl'=4,'core'=2] {'core'}, dimensions={0} | all-to-all | bytes 2097152 | tf_op jit(solution)/shard_map/all_to_all | solution.py:41
  73.6 0.1 reduce_sum.72
  74.0 17.0 %all_to_all.36 = f16[4,264,128]{2,1,0:T(8,128)(2,1)S(1)} all-to-all(f16[4,264,128]{2,1,0:T(8,128)(2,1)S(1)} %fusion.17), channel_id=1, replica_groups=mesh['yh'=2,'z'=8,'x'=4,'yl'=4,'core'=2] {'yl'}, dimensions={0} | all-to-all | bytes 540672 | tf_op jit(solution)/shard_map/all_to_all | solution.py:41
  91.0 0.1 fusion.19
  91.2 0.1 reduce_sum.76
  91.3 11.9 %all_to_all.37 = f32[16,1,128]{2,1,0:T(1,128)S(1)} all-to-all(f32[16,1,128]{2,1,0:T(1,128)S(1)} %broadcast_in_dim.6), channel_id=1, replica_groups=mesh['yh'=2,'z'=8,'x'=4,'yl'=4,'core'=2] {'yh','yl','core'}, dimensions={0} | all-to-all | bytes 16384 | tf_op jit(solution)/shard_map/all_to_all | solution.py:41
  103.3 15.3 %all_to_all.38 = f32[32,1,128]{2,1,0:T(1,128)S(1)} all-to-all(f32[32,1,128]{2,1,0:T(1,128)S(1)} %broadcast_in_dim.8), channel_id=1, replica_groups=mesh['yh'=2,'z'=8,'x'=4,'yl'=4,'core'=2] {'z','x'}, dimensions={0} | all-to-all | bytes 32768 | tf_op jit(solution)/shard_map/all_to_all | solution.py:41
  118.6 0.6 multiply_reduce_fusion.2
  (34 shorter events, 0.9 us)
Async XLA Ops:
  0.6 56.2 %copy-start = (bf16[256,640]{1,0:T(8,128)(2,1)S(1)}, bf16[256,640]{1,0:T(8,128)(2,1)}, u32[]{:S(2)}) copy-start(bf16[256,640]{1,0:T(8,128)(2,1)} %param.6) | copy-start | bytes 983044
  0.6 54.9 %copy-start.1 = (bf16[256,2560]{1,0:T(8,128)(2,1)S(1)}, bf16[256,2560]{1,0:T(8,128)(2,1)}, u32[]{:S(2)}) copy-start(bf16[256,2560]{1,0:T(8,128)(2,1)} %param.7) | copy-start | bytes 3932164
  0.7 54.9 %copy-start.2 = (bf16[256,2560]{1,0:T(8,128)(2,1)S(1)}, bf16[256,2560]{1,0:T(8,128)(2,1)}, u32[]{:S(2)}) copy-start(bf16[256,2560]{1,0:T(8,128)(2,1)} %param.8) | copy-start | bytes 3932164
  42.5 18.5 %collective-permute-start.2 = (bf16[128,3200]{1,0:T(8,128)(2,1)S(1)}, bf16[128,3200]{1,0:T(8,128)(2,1)S(1)}, u32[]{:S(2)}, u32[]{:S(2)}) collective-permute-start(bf16[128,3200]{1,0:T(8,128)(2,1)S(1)} %bitcast.29), channel_id=1, source_target_pairs={{0,8},{8,16},{16,24},{24,0},{32,40},{40,48},{48,56},{56,32},{64,72... | collective-permute-start | bytes 2457608 | tf_op jit(solution)/shard_map/ppermute | solution.py:62
  45.4 17.6 %collective-permute-start.3 = (bf16[128,3200]{1,0:T(8,128)(2,1)S(1)}, bf16[128,3200]{1,0:T(8,128)(2,1)S(1)}, u32[]{:S(2)}, u32[]{:S(2)}) collective-permute-start(bf16[128,3200]{1,0:T(8,128)(2,1)S(1)} %bitcast.30), channel_id=1, source_target_pairs={{0,24},{8,0},{16,8},{24,16},{32,56},{40,32},{48,40},{56,48},{64,88... | collective-permute-start | bytes 2457608 | tf_op jit(solution)/shard_map/ppermute | solution.py:62
  49.0 10.2 %collective-permute-start = (bf16[64,3200]{1,0:T(8,128)(2,1)S(1)}, bf16[64,3200]{1,0:T(8,128)(2,1)S(1)}, u32[]{:S(2)}, u32[]{:S(2)}) collective-permute-start(bf16[64,3200]{1,0:T(8,128)(2,1)S(1)} %get-tuple-element.17), channel_id=1, source_target_pairs={{0,32},{8,40},{16,48},{24,56},{32,64},{40,72},{48,80},{56,88},{64,... | collective-permute-start | bytes 1228808 | tf_op jit(solution)/shard_map/ppermute | solution.py:62
  50.9 9.5 %collective-permute-start.1 = (bf16[64,3200]{1,0:T(8,128)(2,1)S(1)}, bf16[64,3200]{1,0:T(8,128)(2,1)S(1)}, u32[]{:S(2)}, u32[]{:S(2)}) collective-permute-start(bf16[64,3200]{1,0:T(8,128)(2,1)S(1)} %get-tuple-element.16), channel_id=1, source_target_pairs={{0,224},{8,232},{16,240},{24,248},{32,0},{40,8},{48,16},{56,24},{6... | collective-permute-start | bytes 1228808 | tf_op jit(solution)/shard_map/ppermute | solution.py:62
  73.6 29.7 %copy-start.3 = (f32[16,128]{1,0:T(8,128)S(1)}, f32[16,128]{1,0:T(8,128)}, u32[]{:S(2)}) copy-start(f32[16,128]{1,0:T(8,128)} %get-tuple-element.11) | copy-start | bytes 24580
  103.3 15.9 %copy-start.4 = (f32[128]{0:T(128)}, f32[128]{0:T(128)S(1)}, u32[]{:S(2)}) copy-start(f32[128]{0:T(128)S(1)} %get-tuple-element.13) | copy-start | bytes 1540

commit v8 on v7

--- a/solution.py
+++ b/solution.py
@@ -52,14 +52,20 @@
     ]
 
 
+def device(yh, z, x, yl, core):
+    return (place(yh, z, x) * YL + yl) * CORE + core
+
+
 def shift(value, dz, dx):
     pairs = [
-        (place(yh, z, x), place(yh, z + dz, x + dx))
+        (device(yh, z, x, yl, core), device(yh, z + turn * dz, x + turn * dx, yl, core))
         for yh in range(YH)
         for z in range(Z)
         for x in range(X)
+        for yl in range(YL)
+        for core, turn in enumerate((1, -1))
     ]
-    return lax.ppermute(value, DP, pairs)
+    return lax.ppermute(value, DP + TENSOR, pairs)
 
 
 def valid_copies_kernel(input_ref, preact_ref, upstream_ref, out_ref, mine_ref):
@@ -89,9 +95,9 @@
 
 def neighbour_rows(own):
     half = own.shape[0] // 2
-    right, left = shift(own, 0, 1), shift(own, 0, -1)
-    above, below = shift(own[:half], 1, 0), shift(own[half:], -1, 0)
-    return jnp.concatenate([above, below, right, left])
+    first, second = shift(own, 0, 1), shift(own, 0, -1)
+    across = [shift(own[:half], 1, 0), shift(own[half:], -1, 0)]
+    return jnp.concatenate(across + [first, second])
 
 
 def encode(parts):
@@ -126,8 +132,9 @@
     parts = [cross_dot(rows[:, :split], train_input) * input_scale for rows in (own, foreign)]
     parts += [cross_dot(rows[:, split:], train_grad) * grad_scale for rows in (own, foreign)]
     pieces = jnp.stack(jnp.split(jnp.concatenate(parts), CORE, axis=1))
-    parts = jnp.sum(exchange(pieces, "core"), axis=0)
-    coded = encode(parts.reshape(2, CLASSES, -1, parts.shape[1]))
+    lower, upper = exchange(pieces, "core").reshape(CORE, 2, CLASSES, -1, pieces.shape[2])
+    upper = jnp.concatenate([upper[:, :2], upper[:, 3:], upper[:, 2:3]], axis=1)
+    coded = encode(lower + upper)
     input_kernel, grad_kernel = decode(exchange(coded, "yl"), 2)
     product = (input_kernel * grad_kernel).reshape(VAL_SEQS, -1, input_kernel.shape[1])
     sums = jnp.sum(product, axis=(1, 2)) * (1.0 / SEQ_LEN)

time: 120 us -> 117 us (0.975)
  blocking collectives: 93.1 us -> 85.5 us
  waiting for transfers between devices: 5.17 us -> 11.2 us
    all_to_all x5, blocking collectives: 93.1 us -> 85.5 us  [exchange(): lax.all_to_all(value, axes, 0, 0, axis_index_groups=groups, tiled=True)]
    ppermute x4, waiting for transfers between devices: 5.17 us -> 11.2 us  [shift(): return lax.ppermute(value, DP + TENSOR, pairs)]
  transfers between devices with their start and end apart: 4 -> 4, of which waited for: 4 -> 3; matrix products, arithmetic and copies ran while one was open for 2% -> 2% of each run, Pallas kernels for 0% -> 0%
where the time goes in v8:
time: 117 us; the launch traced here: 116 us
  blocking collectives  85.5 us (73%)
  starting transfers between devices  11.8 us (10%)
  waiting for transfers between devices  11.2 us (10%)
  other arithmetic  2.59 us (2%)
  Pallas kernels  1.92 us (2%)
  matrix products  1.86 us (2%)
    all_to_all x5, blocking collectives, exchange(): lax.all_to_all(value, axes, 0, 0, axis_index_groups=groups, tiled=True)  85.5 us
    ppermute x4, starting transfers between devices, shift(): return lax.ppermute(value, DP + TENSOR, pairs)  11.8 us
    ppermute x4, waiting for transfers between devices, shift(): return lax.ppermute(value, DP + TENSOR, pairs)  11.2 us
  transfers between devices with their start and end apart: 4, of which 3 were waited for; matrix products, arithmetic and copies ran while one was open for 2% of the time, Pallas kernels for 0%

profile of v8, /device:TPU:1, one launch (start us, length us, event | category | flops | bytes accessed | tf_op | source)
XLA Modules:
  0.0 116.5 jit_solution(2534438032660220324)
XLA Ops:
  0.7 1.9 %shard_map.77 = (bf16[16,8,3200]{2,1,0:T(8,128)(2,1)}, f32[16,128]{1,0:T(8,128)}) custom-call(bf16[8,640]{1,0:T(8,128)(2,1)} %input_ref.1, bf16[8,2560]{1,0:T(8,128)(2,1)} %preact_ref.1, bf16[8,2560]{1,0:T(8,128)(2,1)} %upstream_ref.1), custom_call_target="tpu_custom_call" | custom-call | tf_op jit(solution)/shard_map/pallas_call | solution.py:86
  2.6 39.9 %all_to_all.34 = bf16[16,8,3200]{2,1,0:T(8,128)(2,1)S(1)} all-to-all(bf16[16,8,3200]{2,1,0:T(8,128)(2,1)} %get-tuple-element.7), channel_id=1, replica_groups={{0,48,64,112,128,176,192,240,256,304,320,368,384,432,448,496},{8,56,72,..., dimensions={0} | all-to-all | bytes 1638400 | tf_op jit(solution)/shard_map/all_to_all | solution.py:41
  42.5 3.4 %collective-permute-start.2 = (bf16[128,3200]{1,0:T(8,128)(2,1)S(1)}, bf16[128,3200]{1,0:T(8,128)(2,1)S(1)}, u32[]{:S(2)}, u32[]{:S(2)}) collective-permute-start(bf16[128,3200]{1,0:T(8,128)(2,1)S(1)} %bitcast.39), channel_id=1, source_target_pairs={{0,8},{1,25},{2,10},{3,27},{4,12},{5,29},{6,14},{7,31},{8,16},{9,1... | collective-permute-start | bytes 2457608 | tf_op jit(solution)/shard_map/ppermute | solution.py:68
  46.0 1.9 %collective-permute-start.3 = (bf16[128,3200]{1,0:T(8,128)(2,1)S(1)}, bf16[128,3200]{1,0:T(8,128)(2,1)S(1)}, u32[]{:S(2)}, u32[]{:S(2)}) collective-permute-start(bf16[128,3200]{1,0:T(8,128)(2,1)S(1)} %bitcast.40), channel_id=1, source_target_pairs={{0,24},{1,9},{2,26},{3,11},{4,28},{5,13},{6,30},{7,15},{8,0},{9,17... | collective-permute-start | bytes 2457608 | tf_op jit(solution)/shard_map/ppermute | solution.py:68
  47.9 4.6 %collective-permute-start = (bf16[64,3200]{1,0:T(8,128)(2,1)S(1)}, bf16[64,3200]{1,0:T(8,128)(2,1)S(1)}, u32[]{:S(2)}, u32[]{:S(2)}) collective-permute-start(bf16[64,3200]{1,0:T(8,128)(2,1)S(1)} %get-tuple-element.21), channel_id=1, source_target_pairs={{0,32},{1,225},{2,34},{3,227},{4,36},{5,229},{6,38},{7,231},{8,40}... | collective-permute-start | bytes 1228808 | tf_op jit(solution)/shard_map/ppermute | solution.py:68
  52.5 1.9 %collective-permute-start.1 = (bf16[64,3200]{1,0:T(8,128)(2,1)S(1)}, bf16[64,3200]{1,0:T(8,128)(2,1)S(1)}, u32[]{:S(2)}, u32[]{:S(2)}) collective-permute-start(bf16[64,3200]{1,0:T(8,128)(2,1)S(1)} %get-tuple-element.20), channel_id=1, source_target_pairs={{0,224},{1,33},{2,226},{3,35},{4,228},{5,37},{6,230},{7,39},{8,232... | collective-permute-start | bytes 1228808 | tf_op jit(solution)/shard_map/ppermute | solution.py:68
  54.4 1.3 %fusion.7 = bf16[256,2560]{1,0:T(8,128)(2,1)S(1)} fusion(bf16[256,2560]{1,0:T(8,128)(2,1)S(1)} %copy-done.1, bf16[256,2560]{1,0:T(8,128)(2,1)S(1)} %copy-done.2), kind=kLoop, calls=%fused_computation.11 | loop fusion | flops 7864320 | bytes 3932160 | tf_op jit(solution)/shard_map/convert_element_type | solution.py:31
  55.7 0.2 convolution_multiply_fusion.1
  56.0 0.5 convolution_multiply_fusion.2
  56.5 0.8 collective-permute-done
  57.4 7.7 %collective-permute-done.1 = bf16[64,3200]{1,0:T(8,128)(2,1)S(1)} collective-permute-done((bf16[64,3200]{1,0:T(8,128)(2,1)S(1)}, bf16[64,3200]{1,0:T(8,128)(2,1)S(1)}, u32[]{:S(2)}, u32[]{:S(2)}) %collective-permute-start.1) | collective-permute-done | bytes 409632 | tf_op jit(solution)/shard_map/ppermute | solution.py:68
  65.1 0.1 constant_dynamic-update-slice_fusion.1
  65.2 2.7 %collective-permute-done.3 = bf16[128,3200]{1,0:T(8,128)(2,1)S(1)} collective-permute-done((bf16[128,3200]{1,0:T(8,128)(2,1)S(1)}, bf16[128,3200]{1,0:T(8,128)(2,1)S(1)}, u32[]{:S(2)}, u32[]{:S(2)}) %collective-permute-start.3) | collective-permute-done | bytes 819232 | tf_op jit(solution)/shard_map/ppermute | solution.py:68
  67.9 0.1 constant_dynamic-update-slice_fusion
  68.0 0.7 fusion.10
  68.7 0.4 convolution_multiply_fusion
  69.3 6.1 %all_to_all.35 = f32[2,1024,128]{2,1,0:T(8,128)S(1)} all-to-all(f32[2,1024,128]{2,1,0:T(8,128)S(1)} %pad_maximum_fusion.1), channel_id=1, replica_groups=mesh['yh'=2,'z'=8,'x'=4,'yl'=4,'core'=2] {'core'}, dimensions={0} | all-to-all | bytes 2097152 | tf_op jit(solution)/shard_map/all_to_all | solution.py:41
  75.9 15.3 %all_to_all.36 = f16[4,264,128]{2,1,0:T(8,128)(2,1)S(1)} all-to-all(f16[4,264,128]{2,1,0:T(8,128)(2,1)S(1)} %fusion.17), channel_id=1, replica_groups=mesh['yh'=2,'z'=8,'x'=4,'yl'=4,'core'=2] {'yl'}, dimensions={0} | all-to-all | bytes 540672 | tf_op jit(solution)/shard_map/all_to_all | solution.py:41
  91.2 0.1 fusion.23
  91.3 0.1 reduce_sum.65
  91.4 0.1 reduce_sum.66
  91.6 11.9 %all_to_all.37 = f32[16,1,128]{2,1,0:T(1,128)S(1)} all-to-all(f32[16,1,128]{2,1,0:T(1,128)S(1)} %broadcast_in_dim.6), channel_id=1, replica_groups=mesh['yh'=2,'z'=8,'x'=4,'yl'=4,'core'=2] {'yh','yl','core'}, dimensions={0} | all-to-all | bytes 16384 | tf_op jit(solution)/shard_map/all_to_all | solution.py:41
  103.6 12.3 %all_to_all.38 = f32[32,1,128]{2,1,0:T(1,128)S(1)} all-to-all(f32[32,1,128]{2,1,0:T(1,128)S(1)} %broadcast_in_dim.8), channel_id=1, replica_groups=mesh['yh'=2,'z'=8,'x'=4,'yl'=4,'core'=2] {'z','x'}, dimensions={0} | all-to-all | bytes 32768 | tf_op jit(solution)/shard_map/all_to_all | solution.py:41
  115.8 0.6 multiply_reduce_fusion.2
  (35 shorter events, 0.8 us)
Async XLA Ops:
  0.6 55.1 %copy-start = (bf16[256,640]{1,0:T(8,128)(2,1)S(1)}, bf16[256,640]{1,0:T(8,128)(2,1)}, u32[]{:S(2)}) copy-start(bf16[256,640]{1,0:T(8,128)(2,1)} %param.6) | copy-start | bytes 983044
  0.6 53.7 %copy-start.1 = (bf16[256,2560]{1,0:T(8,128)(2,1)S(1)}, bf16[256,2560]{1,0:T(8,128)(2,1)}, u32[]{:S(2)}) copy-start(bf16[256,2560]{1,0:T(8,128)(2,1)} %param.7) | copy-start | bytes 3932164
  0.7 53.7 %copy-start.2 = (bf16[256,2560]{1,0:T(8,128)(2,1)S(1)}, bf16[256,2560]{1,0:T(8,128)(2,1)}, u32[]{:S(2)}) copy-start(bf16[256,2560]{1,0:T(8,128)(2,1)} %param.8) | copy-start | bytes 3932164
  42.5 22.6 %collective-permute-start.2 = (bf16[128,3200]{1,0:T(8,128)(2,1)S(1)}, bf16[128,3200]{1,0:T(8,128)(2,1)S(1)}, u32[]{:S(2)}, u32[]{:S(2)}) collective-permute-start(bf16[128,3200]{1,0:T(8,128)(2,1)S(1)} %bitcast.39), channel_id=1, source_target_pairs={{0,8},{1,25},{2,10},{3,27},{4,12},{5,29},{6,14},{7,31},{8,16},{9,1... | collective-permute-start | bytes 2457608 | tf_op jit(solution)/shard_map/ppermute | solution.py:68
  46.0 21.9 %collective-permute-start.3 = (bf16[128,3200]{1,0:T(8,128)(2,1)S(1)}, bf16[128,3200]{1,0:T(8,128)(2,1)S(1)}, u32[]{:S(2)}, u32[]{:S(2)}) collective-permute-start(bf16[128,3200]{1,0:T(8,128)(2,1)S(1)} %bitcast.40), channel_id=1, source_target_pairs={{0,24},{1,9},{2,26},{3,11},{4,28},{5,13},{6,30},{7,15},{8,0},{9,17... | collective-permute-start | bytes 2457608 | tf_op jit(solution)/shard_map/ppermute | solution.py:68
  47.9 9.4 %collective-permute-start = (bf16[64,3200]{1,0:T(8,128)(2,1)S(1)}, bf16[64,3200]{1,0:T(8,128)(2,1)S(1)}, u32[]{:S(2)}, u32[]{:S(2)}) collective-permute-start(bf16[64,3200]{1,0:T(8,128)(2,1)S(1)} %get-tuple-element.21), channel_id=1, source_target_pairs={{0,32},{1,225},{2,34},{3,227},{4,36},{5,229},{6,38},{7,231},{8,40}... | collective-permute-start | bytes 1228808 | tf_op jit(solution)/shard_map/ppermute | solution.py:68
  52.5 12.6 %collective-permute-start.1 = (bf16[64,3200]{1,0:T(8,128)(2,1)S(1)}, bf16[64,3200]{1,0:T(8,128)(2,1)S(1)}, u32[]{:S(2)}, u32[]{:S(2)}) collective-permute-start(bf16[64,3200]{1,0:T(8,128)(2,1)S(1)} %get-tuple-element.20), channel_id=1, source_target_pairs={{0,224},{1,33},{2,226},{3,35},{4,228},{5,37},{6,230},{7,39},{8,232... | collective-permute-start | bytes 1228808 | tf_op jit(solution)/shard_map/ppermute | solution.py:68
  75.5 28.0 %copy-start.3 = (f32[16,128]{1,0:T(8,128)S(1)}, f32[16,128]{1,0:T(8,128)}, u32[]{:S(2)}) copy-start(f32[16,128]{1,0:T(8,128)} %get-tuple-element.11) | copy-start | bytes 24580
  103.5 12.9 %copy-start.4 = (f32[128]{0:T(128)}, f32[128]{0:T(128)S(1)}, u32[]{:S(2)}) copy-start(f32[128]{0:T(128)S(1)} %get-tuple-element.13) | copy-start | bytes 1540

commit v9 on v8

--- a/solution.py
+++ b/solution.py
@@ -94,10 +94,9 @@
 
 
 def neighbour_rows(own):
-    half = own.shape[0] // 2
     first, second = shift(own, 0, 1), shift(own, 0, -1)
-    across = [shift(own[:half], 1, 0), shift(own[half:], -1, 0)]
-    return jnp.concatenate(across + [first, second])
+    across = shift(own, 1, 0)
+    return jnp.concatenate([across, first, second])
 
 
 def encode(parts):

time: 117 us -> 120 us (1.026)
  waiting for transfers between devices: 11.2 us -> 17.3 us
  blocking collectives: 85.5 us -> 83.3 us
  starting transfers between devices: 11.8 us -> 9.91 us
    ppermute x4 -> x3, waiting for transfers between devices: 11.2 us -> 17.3 us  [shift(): return lax.ppermute(value, DP + TENSOR, pairs)]
    all_to_all x5, blocking collectives: 85.5 us -> 83.3 us  [exchange(): lax.all_to_all(value, axes, 0, 0, axis_index_groups=groups, tiled=True)]
    ppermute x4 -> x3, starting transfers between devices: 11.8 us -> 9.91 us  [shift(): return lax.ppermute(value, DP + TENSOR, pairs)]
  transfers between devices with their start and end apart: 4 -> 3, of which waited for: 3 -> 3; matrix products, arithmetic and copies ran while one was open for 2% -> 3% of each run, Pallas kernels for 0% -> 0%
where the time goes in v9:
time: 120 us; the launch traced here: 119 us
  blocking collectives  83.3 us (69%)
  waiting for transfers between devices  17.3 us (14%)
  starting transfers between devices  9.91 us (8%)
  other arithmetic  3.66 us (3%)
  Pallas kernels  1.89 us (2%)
  matrix products  1.85 us (2%)
    all_to_all x5, blocking collectives, exchange(): lax.all_to_all(value, axes, 0, 0, axis_index_groups=groups, tiled=True)  83.3 us
    ppermute x3, waiting for transfers between devices, shift(): return lax.ppermute(value, DP + TENSOR, pairs)  17.3 us
    ppermute x3, starting transfers between devices, shift(): return lax.ppermute(value, DP + TENSOR, pairs)  9.91 us
  transfers between devices with their start and end apart: 3, of which 3 were waited for; matrix products, arithmetic and copies ran while one was open for 3% of the time, Pallas kernels for 0%

profile of v9, /device:TPU:1, one launch (start us, length us, event | category | flops | bytes accessed | tf_op | source)
XLA Modules:
  0.0 119.4 jit_solution(3175429328404594800)
XLA Ops:
  0.7 1.9 %shard_map.77 = (bf16[16,8,3200]{2,1,0:T(8,128)(2,1)}, f32[16,128]{1,0:T(8,128)}) custom-call(bf16[8,640]{1,0:T(8,128)(2,1)} %input_ref.1, bf16[8,2560]{1,0:T(8,128)(2,1)} %preact_ref.1, bf16[8,2560]{1,0:T(8,128)(2,1)} %upstream_ref.1), custom_call_target="tpu_custom_call" | custom-call | tf_op jit(solution)/shard_map/pallas_call | solution.py:86
  2.5 39.9 %all_to_all.34 = bf16[16,8,3200]{2,1,0:T(8,128)(2,1)S(1)} all-to-all(bf16[16,8,3200]{2,1,0:T(8,128)(2,1)} %get-tuple-element.7), channel_id=1, replica_groups={{0,48,64,112,128,176,192,240,256,304,320,368,384,432,448,496},{8,56,72,..., dimensions={0} | all-to-all | bytes 1638400 | tf_op jit(solution)/shard_map/all_to_all | solution.py:41
  42.4 3.7 %collective-permute-start = (bf16[128,3200]{1,0:T(8,128)(2,1)S(1)}, bf16[128,3200]{1,0:T(8,128)(2,1)S(1)}, u32[]{:S(2)}, u32[]{:S(2)}) collective-permute-start(bf16[128,3200]{1,0:T(8,128)(2,1)S(1)} %bitcast.38), channel_id=1, source_target_pairs={{0,32},{1,225},{2,34},{3,227},{4,36},{5,229},{6,38},{7,231},{8,40}... | collective-permute-start | bytes 2457608 | tf_op jit(solution)/shard_map/ppermute | solution.py:68
  46.2 4.2 %collective-permute-start.1 = (bf16[128,3200]{1,0:T(8,128)(2,1)S(1)}, bf16[128,3200]{1,0:T(8,128)(2,1)S(1)}, u32[]{:S(2)}, u32[]{:S(2)}) collective-permute-start(bf16[128,3200]{1,0:T(8,128)(2,1)S(1)} %bitcast.39), channel_id=1, source_target_pairs={{0,8},{1,25},{2,10},{3,27},{4,12},{5,29},{6,14},{7,31},{8,16},{9,1... | collective-permute-start | bytes 2457608 | tf_op jit(solution)/shard_map/ppermute | solution.py:68
  50.4 1.9 %collective-permute-start.2 = (bf16[128,3200]{1,0:T(8,128)(2,1)S(1)}, bf16[128,3200]{1,0:T(8,128)(2,1)S(1)}, u32[]{:S(2)}, u32[]{:S(2)}) collective-permute-start(bf16[128,3200]{1,0:T(8,128)(2,1)S(1)} %bitcast.40), channel_id=1, source_target_pairs={{0,24},{1,9},{2,26},{3,11},{4,28},{5,13},{6,30},{7,15},{8,0},{9,17... | collective-permute-start | bytes 2457608 | tf_op jit(solution)/shard_map/ppermute | solution.py:68
  52.4 2.4 %fusion.7 = bf16[256,2560]{1,0:T(8,128)(2,1)S(1)} fusion(bf16[256,2560]{1,0:T(8,128)(2,1)S(1)} %copy-done.1, bf16[256,2560]{1,0:T(8,128)(2,1)} %param.8), kind=kLoop, calls=%fused_computation.11 | loop fusion | flops 7864320 | bytes 3932160 | tf_op jit(solution)/shard_map/convert_element_type | solution.py:31
  54.7 0.2 convolution_multiply_fusion.1
  55.0 0.5 convolution_multiply_fusion.2
  55.5 0.2 collective-permute-done
  55.8 6.9 %collective-permute-done.1 = bf16[128,3200]{1,0:T(8,128)(2,1)S(1)} collective-permute-done((bf16[128,3200]{1,0:T(8,128)(2,1)S(1)}, bf16[128,3200]{1,0:T(8,128)(2,1)S(1)}, u32[]{:S(2)}, u32[]{:S(2)}) %collective-permute-start.1) | collective-permute-done | bytes 819232 | tf_op jit(solution)/shard_map/ppermute | solution.py:68
  62.7 0.1 constant_dynamic-update-slice_fusion.1
  62.8 10.2 %collective-permute-done.2 = bf16[128,3200]{1,0:T(8,128)(2,1)S(1)} collective-permute-done((bf16[128,3200]{1,0:T(8,128)(2,1)S(1)}, bf16[128,3200]{1,0:T(8,128)(2,1)S(1)}, u32[]{:S(2)}, u32[]{:S(2)}) %collective-permute-start.2) | collective-permute-done | bytes 819232 | tf_op jit(solution)/shard_map/ppermute | solution.py:68
  73.0 0.1 constant_dynamic-update-slice_fusion
  73.1 0.7 fusion.10
  73.8 0.4 convolution_multiply_fusion
  74.4 4.6 %all_to_all.35 = f32[2,1024,128]{2,1,0:T(8,128)S(1)} all-to-all(f32[2,1024,128]{2,1,0:T(8,128)S(1)} %pad_maximum_fusion.1), channel_id=1, replica_groups=mesh['yh'=2,'z'=8,'x'=4,'yl'=4,'core'=2] {'core'}, dimensions={0} | all-to-all | bytes 2097152 | tf_op jit(solution)/shard_map/all_to_all | solution.py:41
  79.4 0.1 fusion.17
  79.5 13.2 %all_to_all.36 = f16[4,264,128]{2,1,0:T(8,128)(2,1)S(1)} all-to-all(f16[4,264,128]{2,1,0:T(8,128)(2,1)S(1)} %fusion.17), channel_id=1, replica_groups=mesh['yh'=2,'z'=8,'x'=4,'yl'=4,'core'=2] {'yl'}, dimensions={0} | all-to-all | bytes 540672 | tf_op jit(solution)/shard_map/all_to_all | solution.py:41
  92.7 0.1 fusion.23
  92.9 0.1 reduce_sum.65
  92.9 0.1 reduce_sum.66
  93.1 11.9 %all_to_all.37 = f32[16,1,128]{2,1,0:T(1,128)S(1)} all-to-all(f32[16,1,128]{2,1,0:T(1,128)S(1)} %broadcast_in_dim.6), channel_id=1, replica_groups=mesh['yh'=2,'z'=8,'x'=4,'yl'=4,'core'=2] {'yh','yl','core'}, dimensions={0} | all-to-all | bytes 16384 | tf_op jit(solution)/shard_map/all_to_all | solution.py:41
  105.1 13.7 %all_to_all.38 = f32[32,1,128]{2,1,0:T(1,128)S(1)} all-to-all(f32[32,1,128]{2,1,0:T(1,128)S(1)} %broadcast_in_dim.8), channel_id=1, replica_groups=mesh['yh'=2,'z'=8,'x'=4,'yl'=4,'core'=2] {'z','x'}, dimensions={0} | all-to-all | bytes 32768 | tf_op jit(solution)/shard_map/all_to_all | solution.py:41
  118.8 0.6 multiply_reduce_fusion.2
  (29 shorter events, 0.7 us)
Async XLA Ops:
  0.6 54.1 %copy-start = (bf16[256,640]{1,0:T(8,128)(2,1)S(1)}, bf16[256,640]{1,0:T(8,128)(2,1)}, u32[]{:S(2)}) copy-start(bf16[256,640]{1,0:T(8,128)(2,1)} %param.6) | copy-start | bytes 983044
  0.6 51.7 %copy-start.1 = (bf16[256,2560]{1,0:T(8,128)(2,1)S(1)}, bf16[256,2560]{1,0:T(8,128)(2,1)}, u32[]{:S(2)}) copy-start(bf16[256,2560]{1,0:T(8,128)(2,1)} %param.7) | copy-start | bytes 3932164
  42.4 13.4 %collective-permute-start = (bf16[128,3200]{1,0:T(8,128)(2,1)S(1)}, bf16[128,3200]{1,0:T(8,128)(2,1)S(1)}, u32[]{:S(2)}, u32[]{:S(2)}) collective-permute-start(bf16[128,3200]{1,0:T(8,128)(2,1)S(1)} %bitcast.38), channel_id=1, source_target_pairs={{0,32},{1,225},{2,34},{3,227},{4,36},{5,229},{6,38},{7,231},{8,40}... | collective-permute-start | bytes 2457608 | tf_op jit(solution)/shard_map/ppermute | solution.py:68
  46.2 16.6 %collective-permute-start.1 = (bf16[128,3200]{1,0:T(8,128)(2,1)S(1)}, bf16[128,3200]{1,0:T(8,128)(2,1)S(1)}, u32[]{:S(2)}, u32[]{:S(2)}) collective-permute-start(bf16[128,3200]{1,0:T(8,128)(2,1)S(1)} %bitcast.39), channel_id=1, source_target_pairs={{0,8},{1,25},{2,10},{3,27},{4,12},{5,29},{6,14},{7,31},{8,16},{9,1... | collective-permute-start | bytes 2457608 | tf_op jit(solution)/shard_map/ppermute | solution.py:68
  50.4 22.6 %collective-permute-start.2 = (bf16[128,3200]{1,0:T(8,128)(2,1)S(1)}, bf16[128,3200]{1,0:T(8,128)(2,1)S(1)}, u32[]{:S(2)}, u32[]{:S(2)}) collective-permute-start(bf16[128,3200]{1,0:T(8,128)(2,1)S(1)} %bitcast.40), channel_id=1, source_target_pairs={{0,24},{1,9},{2,26},{3,11},{4,28},{5,13},{6,30},{7,15},{8,0},{9,17... | collective-permute-start | bytes 2457608 | tf_op jit(solution)/shard_map/ppermute | solution.py:68
  79.1 25.9 %copy-start.2 = (f32[16,128]{1,0:T(8,128)S(1)}, f32[16,128]{1,0:T(8,128)}, u32[]{:S(2)}) copy-start(f32[16,128]{1,0:T(8,128)} %get-tuple-element.11) | copy-start | bytes 24580
  105.0 14.3 %copy-start.3 = (f32[128]{0:T(128)}, f32[128]{0:T(128)S(1)}, u32[]{:S(2)}) copy-start(f32[128]{0:T(128)S(1)} %get-tuple-element.13) | copy-start | bytes 1540

commit v10 on v8

--- a/solution.py
+++ b/solution.py
@@ -16,7 +16,7 @@
 CLASSES = 4
 LANES = 128
 TAIL = 8
-LOW, HIGH = -126.0, 30.0
+LOW, HIGH, TOP = -110.0, 30.0, 15.0
 
 inv_root_two = 0.7071067811865476
 inv_root_tau = 0.3989422804014327
@@ -68,29 +68,27 @@
     return lax.ppermute(value, DP + TENSOR, pairs)
 
 
-def valid_copies_kernel(input_ref, preact_ref, upstream_ref, out_ref, mine_ref):
-    tensor = YL * CORE
+def valid_rows_kernel(input_ref, preact_ref, upstream_ref, out_ref, mine_ref):
     member = lax.broadcasted_iota(jnp.int32, mine_ref.shape, 0)
-    mine_ref[...] = (member // tensor == lax.axis_index("yh")).astype(jnp.float32)
+    mine_ref[...] = (member // (YL * CORE) == lax.axis_index("yh")).astype(jnp.float32)
     split = input_ref.shape[1]
-    joined = output_grad(preact_ref[...], upstream_ref[...])
-    for member in range(out_ref.shape[0]):
-        out_ref[member, :, :split] = input_ref[...]
-        out_ref[member, :, split:] = joined
+    out_ref[:, :split] = input_ref[...]
+    out_ref[:, split:] = output_grad(preact_ref[...], upstream_ref[...])
 
 
 def class_gather(valid_input, valid_preact, valid_upstream):
     rows, split = valid_input.shape
     width = split + valid_preact.shape[1]
     members = YH * Z
-    copies, mine = pl.pallas_call(
-        valid_copies_kernel,
+    valid, mine = pl.pallas_call(
+        valid_rows_kernel,
         out_shape=(
-            jax.ShapeDtypeStruct((members, rows, width), jnp.bfloat16),
+            jax.ShapeDtypeStruct((rows, width), jnp.bfloat16),
             jax.ShapeDtypeStruct((YH * YL * CORE, LANES), jnp.float32),
         ),
     )(valid_input, valid_preact, valid_upstream)
-    return exchange(copies.reshape(members * rows, width), DP, class_groups()), mine
+    copies = jnp.broadcast_to(valid[None], (members, rows, width)).reshape(members * rows, width)
+    return exchange(copies, DP, class_groups()), mine
 
 
 def neighbour_rows(own):
@@ -103,7 +101,7 @@
 def encode(parts):
     kinds, blocks, rows, lanes = parts.shape
     largest = jnp.max(jnp.abs(parts), axis=2)
-    exponents = jnp.clip(jnp.ceil(jnp.log2(jnp.maximum(largest, 2.0**LOW))), LOW, HIGH)
+    exponents = jnp.clip(jnp.ceil(jnp.log2(jnp.maximum(largest, 2.0**LOW))), LOW, HIGH) - TOP
     scale = jnp.exp2(-exponents)[:, :, None]
     scaled = [(parts[kind] * scale[kind]).astype(jnp.float16) for kind in range(kinds)]
     tail = jnp.pad(exponents.transpose(1, 0, 2), ((0, 0), (0, TAIL - kinds), (0, 0)))

time: 117 us -> 117 us (level)
  no operation moved by 1% of the time
where the time goes in v10:
time: 117 us
  blocking collectives  85.3 us (73%)
  starting transfers between devices  11.8 us (10%)
  waiting for transfers between devices  11.2 us (10%)
  other arithmetic  2.59 us (2%)
  matrix products  1.84 us (2%)
  Pallas kernels  1.64 us (1%)
  local copies, waits for them, and re-layouts  1.49 us (1%)
    all_to_all x5, blocking collectives, exchange(): lax.all_to_all(value, axes, 0, 0, axis_index_groups=groups, tiled=True)  85.3 us
    ppermute x4, starting transfers between devices, shift(): return lax.ppermute(value, DP + TENSOR, pairs)  11.8 us
    ppermute x4, waiting for transfers between devices, shift(): return lax.ppermute(value, DP + TENSOR, pairs)  11.2 us
  transfers between devices with their start and end apart: 4, of which 3 were waited for; matrix products, arithmetic and copies ran while one was open for 2% of the time, Pallas kernels for 0%

profile of v10, /device:TPU:1, one launch (start us, length us, event | category | flops | bytes accessed | tf_op | source)
XLA Modules:
  0.0 116.8 jit_solution(9539809382638021257)
XLA Ops:
  0.7 1.6 %shard_map.77 = (bf16[8,3200]{1,0:T(8,128)(2,1)}, f32[16,128]{1,0:T(8,128)}) custom-call(bf16[8,640]{1,0:T(8,128)(2,1)} %input_ref.1, bf16[8,2560]{1,0:T(8,128)(2,1)} %preact_ref.1, bf16[8,2560]{1,0:T(8,128)(2,1)} %upstream_ref.1), custom_call_target="tpu_custom_call" | custom-call | tf_op jit(solution)/shard_map/pallas_call | solution.py:83
  2.3 0.9 broadcast_in_dim.8
  3.2 39.7 %all_to_all.34 = bf16[16,8,3200]{2,1,0:T(8,128)(2,1)S(1)} all-to-all(bf16[16,8,3200]{2,1,0:T(8,128)(2,1)S(1)} %broadcast_in_dim.8), channel_id=1, replica_groups={{0,48,64,112,128,176,192,240,256,304,320,368,384,432,448,496},{8,56,72,..., dimensions={0} | all-to-all | bytes 1638400 | tf_op jit(solution)/shard_map/all_to_all | solution.py:41
  42.9 3.4 %collective-permute-start.2 = (bf16[128,3200]{1,0:T(8,128)(2,1)S(1)}, bf16[128,3200]{1,0:T(8,128)(2,1)S(1)}, u32[]{:S(2)}, u32[]{:S(2)}) collective-permute-start(bf16[128,3200]{1,0:T(8,128)(2,1)S(1)} %bitcast.39), channel_id=1, source_target_pairs={{0,8},{1,25},{2,10},{3,27},{4,12},{5,29},{6,14},{7,31},{8,16},{9,1... | collective-permute-start | bytes 2457608 | tf_op jit(solution)/shard_map/ppermute | solution.py:68
  46.3 1.9 %collective-permute-start.3 = (bf16[128,3200]{1,0:T(8,128)(2,1)S(1)}, bf16[128,3200]{1,0:T(8,128)(2,1)S(1)}, u32[]{:S(2)}, u32[]{:S(2)}) collective-permute-start(bf16[128,3200]{1,0:T(8,128)(2,1)S(1)} %bitcast.40), channel_id=1, source_target_pairs={{0,24},{1,9},{2,26},{3,11},{4,28},{5,13},{6,30},{7,15},{8,0},{9,17... | collective-permute-start | bytes 2457608 | tf_op jit(solution)/shard_map/ppermute | solution.py:68
  48.3 4.6 %collective-permute-start = (bf16[64,3200]{1,0:T(8,128)(2,1)S(1)}, bf16[64,3200]{1,0:T(8,128)(2,1)S(1)}, u32[]{:S(2)}, u32[]{:S(2)}) collective-permute-start(bf16[64,3200]{1,0:T(8,128)(2,1)S(1)} %get-tuple-element.21), channel_id=1, source_target_pairs={{0,32},{1,225},{2,34},{3,227},{4,36},{5,229},{6,38},{7,231},{8,40}... | collective-permute-start | bytes 1228808 | tf_op jit(solution)/shard_map/ppermute | solution.py:68
  52.8 1.9 %collective-permute-start.1 = (bf16[64,3200]{1,0:T(8,128)(2,1)S(1)}, bf16[64,3200]{1,0:T(8,128)(2,1)S(1)}, u32[]{:S(2)}, u32[]{:S(2)}) collective-permute-start(bf16[64,3200]{1,0:T(8,128)(2,1)S(1)} %get-tuple-element.20), channel_id=1, source_target_pairs={{0,224},{1,33},{2,226},{3,35},{4,228},{5,37},{6,230},{7,39},{8,232... | collective-permute-start | bytes 1228808 | tf_op jit(solution)/shard_map/ppermute | solution.py:68
  54.8 1.3 %fusion.7 = bf16[256,2560]{1,0:T(8,128)(2,1)S(1)} fusion(bf16[256,2560]{1,0:T(8,128)(2,1)S(1)} %copy-done.1, bf16[256,2560]{1,0:T(8,128)(2,1)S(1)} %copy-done.2), kind=kLoop, calls=%fused_computation.11 | loop fusion | flops 7864320 | bytes 3932160 | tf_op jit(solution)/shard_map/convert_element_type | solution.py:31
  56.1 0.2 convolution_multiply_fusion.1
  56.3 0.5 convolution_multiply_fusion.2
  56.9 0.8 collective-permute-done
  57.7 7.7 %collective-permute-done.1 = bf16[64,3200]{1,0:T(8,128)(2,1)S(1)} collective-permute-done((bf16[64,3200]{1,0:T(8,128)(2,1)S(1)}, bf16[64,3200]{1,0:T(8,128)(2,1)S(1)}, u32[]{:S(2)}, u32[]{:S(2)}) %collective-permute-start.1) | collective-permute-done | bytes 409632 | tf_op jit(solution)/shard_map/ppermute | solution.py:68
  65.5 0.1 constant_dynamic-update-slice_fusion.1
  65.6 2.7 %collective-permute-done.3 = bf16[128,3200]{1,0:T(8,128)(2,1)S(1)} collective-permute-done((bf16[128,3200]{1,0:T(8,128)(2,1)S(1)}, bf16[128,3200]{1,0:T(8,128)(2,1)S(1)}, u32[]{:S(2)}, u32[]{:S(2)}) %collective-permute-start.3) | collective-permute-done | bytes 819232 | tf_op jit(solution)/shard_map/ppermute | solution.py:68
  68.3 0.1 constant_dynamic-update-slice_fusion
  68.4 0.7 fusion.10
  69.1 0.4 convolution_multiply_fusion
  69.7 6.1 %all_to_all.35 = f32[2,1024,128]{2,1,0:T(8,128)S(1)} all-to-all(f32[2,1024,128]{2,1,0:T(8,128)S(1)} %pad_maximum_fusion.1), channel_id=1, replica_groups=mesh['yh'=2,'z'=8,'x'=4,'yl'=4,'core'=2] {'core'}, dimensions={0} | all-to-all | bytes 2097152 | tf_op jit(solution)/shard_map/all_to_all | solution.py:41
  76.2 15.3 %all_to_all.36 = f16[4,264,128]{2,1,0:T(8,128)(2,1)S(1)} all-to-all(f16[4,264,128]{2,1,0:T(8,128)(2,1)S(1)} %fusion.17), channel_id=1, replica_groups=mesh['yh'=2,'z'=8,'x'=4,'yl'=4,'core'=2] {'yl'}, dimensions={0} | all-to-all | bytes 540672 | tf_op jit(solution)/shard_map/all_to_all | solution.py:41
  91.6 0.1 fusion.23
  91.8 0.1 reduce_sum.66
  92.0 11.9 %all_to_all.37 = f32[16,1,128]{2,1,0:T(1,128)S(1)} all-to-all(f32[16,1,128]{2,1,0:T(1,128)S(1)} %broadcast_in_dim.9), channel_id=1, replica_groups=mesh['yh'=2,'z'=8,'x'=4,'yl'=4,'core'=2] {'yh','yl','core'}, dimensions={0} | all-to-all | bytes 16384 | tf_op jit(solution)/shard_map/all_to_all | solution.py:41
  104.0 12.2 %all_to_all.38 = f32[32,1,128]{2,1,0:T(1,128)S(1)} all-to-all(f32[32,1,128]{2,1,0:T(1,128)S(1)} %broadcast_in_dim.11), channel_id=1, replica_groups=mesh['yh'=2,'z'=8,'x'=4,'yl'=4,'core'=2] {'z','x'}, dimensions={0} | all-to-all | bytes 32768 | tf_op jit(solution)/shard_map/all_to_all | solution.py:41
  116.2 0.6 multiply_reduce_fusion.2
  (36 shorter events, 0.9 us)
Async XLA Ops:
  0.6 55.4 %copy-start = (bf16[256,640]{1,0:T(8,128)(2,1)S(1)}, bf16[256,640]{1,0:T(8,128)(2,1)}, u32[]{:S(2)}) copy-start(bf16[256,640]{1,0:T(8,128)(2,1)} %param.6) | copy-start | bytes 983044
  0.6 54.1 %copy-start.1 = (bf16[256,2560]{1,0:T(8,128)(2,1)S(1)}, bf16[256,2560]{1,0:T(8,128)(2,1)}, u32[]{:S(2)}) copy-start(bf16[256,2560]{1,0:T(8,128)(2,1)} %param.7) | copy-start | bytes 3932164
  0.7 54.1 %copy-start.2 = (bf16[256,2560]{1,0:T(8,128)(2,1)S(1)}, bf16[256,2560]{1,0:T(8,128)(2,1)}, u32[]{:S(2)}) copy-start(bf16[256,2560]{1,0:T(8,128)(2,1)} %param.8) | copy-start | bytes 3932164
  42.9 22.6 %collective-permute-start.2 = (bf16[128,3200]{1,0:T(8,128)(2,1)S(1)}, bf16[128,3200]{1,0:T(8,128)(2,1)S(1)}, u32[]{:S(2)}, u32[]{:S(2)}) collective-permute-start(bf16[128,3200]{1,0:T(8,128)(2,1)S(1)} %bitcast.39), channel_id=1, source_target_pairs={{0,8},{1,25},{2,10},{3,27},{4,12},{5,29},{6,14},{7,31},{8,16},{9,1... | collective-permute-start | bytes 2457608 | tf_op jit(solution)/shard_map/ppermute | solution.py:68
  46.3 21.9 %collective-permute-start.3 = (bf16[128,3200]{1,0:T(8,128)(2,1)S(1)}, bf16[128,3200]{1,0:T(8,128)(2,1)S(1)}, u32[]{:S(2)}, u32[]{:S(2)}) collective-permute-start(bf16[128,3200]{1,0:T(8,128)(2,1)S(1)} %bitcast.40), channel_id=1, source_target_pairs={{0,24},{1,9},{2,26},{3,11},{4,28},{5,13},{6,30},{7,15},{8,0},{9,17... | collective-permute-start | bytes 2457608 | tf_op jit(solution)/shard_map/ppermute | solution.py:68
  48.3 9.4 %collective-permute-start = (bf16[64,3200]{1,0:T(8,128)(2,1)S(1)}, bf16[64,3200]{1,0:T(8,128)(2,1)S(1)}, u32[]{:S(2)}, u32[]{:S(2)}) collective-permute-start(bf16[64,3200]{1,0:T(8,128)(2,1)S(1)} %get-tuple-element.21), channel_id=1, source_target_pairs={{0,32},{1,225},{2,34},{3,227},{4,36},{5,229},{6,38},{7,231},{8,40}... | collective-permute-start | bytes 1228808 | tf_op jit(solution)/shard_map/ppermute | solution.py:68
  52.8 12.6 %collective-permute-start.1 = (bf16[64,3200]{1,0:T(8,128)(2,1)S(1)}, bf16[64,3200]{1,0:T(8,128)(2,1)S(1)}, u32[]{:S(2)}, u32[]{:S(2)}) collective-permute-start(bf16[64,3200]{1,0:T(8,128)(2,1)S(1)} %get-tuple-element.20), channel_id=1, source_target_pairs={{0,224},{1,33},{2,226},{3,35},{4,228},{5,37},{6,230},{7,39},{8,232... | collective-permute-start | bytes 1228808 | tf_op jit(solution)/shard_map/ppermute | solution.py:68
  75.9 28.0 %copy-start.3 = (f32[16,128]{1,0:T(8,128)S(1)}, f32[16,128]{1,0:T(8,128)}, u32[]{:S(2)}) copy-start(f32[16,128]{1,0:T(8,128)} %get-tuple-element.11) | copy-start | bytes 24580
  103.9 12.9 %copy-start.4 = (f32[128]{0:T(128)}, f32[128]{0:T(128)S(1)}, u32[]{:S(2)}) copy-start(f32[128]{0:T(128)S(1)} %get-tuple-element.13) | copy-start | bytes 1540

commit v11 on v8

--- a/solution.py
+++ b/solution.py
@@ -16,7 +16,7 @@
 CLASSES = 4
 LANES = 128
 TAIL = 8
-LOW, HIGH = -126.0, 30.0
+LOW, HIGH, TOP = -110.0, 30.0, 15.0
 
 inv_root_two = 0.7071067811865476
 inv_root_tau = 0.3989422804014327
@@ -68,7 +68,10 @@
     return lax.ppermute(value, DP + TENSOR, pairs)
 
 
-def valid_copies_kernel(input_ref, preact_ref, upstream_ref, out_ref, mine_ref):
+def valid_copies_kernel(input_ref, preact_ref, upstream_ref, out_ref, mine_ref, *core_refs):
+    for core, core_ref in enumerate(core_refs):
+        here = lax.axis_index("core") == core
+        core_ref[...] = jnp.full(core_ref.shape, jnp.where(here, 1.0, 0.0), jnp.float32)
     tensor = YL * CORE
     member = lax.broadcasted_iota(jnp.int32, mine_ref.shape, 0)
     mine_ref[...] = (member // tensor == lax.axis_index("yh")).astype(jnp.float32)
@@ -83,14 +86,15 @@
     rows, split = valid_input.shape
     width = split + valid_preact.shape[1]
     members = YH * Z
-    copies, mine = pl.pallas_call(
+    copies, mine, *cores = pl.pallas_call(
         valid_copies_kernel,
         out_shape=(
             jax.ShapeDtypeStruct((members, rows, width), jnp.bfloat16),
             jax.ShapeDtypeStruct((YH * YL * CORE, LANES), jnp.float32),
-        ),
+        )
+        + (jax.ShapeDtypeStruct((1, LANES), jnp.float32),) * CORE,
     )(valid_input, valid_preact, valid_upstream)
-    return exchange(copies.reshape(members * rows, width), DP, class_groups()), mine
+    return exchange(copies.reshape(members * rows, width), DP, class_groups()), mine, cores
 
 
 def neighbour_rows(own):
@@ -103,7 +107,7 @@
 def encode(parts):
     kinds, blocks, rows, lanes = parts.shape
     largest = jnp.max(jnp.abs(parts), axis=2)
-    exponents = jnp.clip(jnp.ceil(jnp.log2(jnp.maximum(largest, 2.0**LOW))), LOW, HIGH)
+    exponents = jnp.clip(jnp.ceil(jnp.log2(jnp.maximum(largest, 2.0**LOW))), LOW, HIGH) - TOP
     scale = jnp.exp2(-exponents)[:, :, None]
     scaled = [(parts[kind] * scale[kind]).astype(jnp.float16) for kind in range(kinds)]
     tail = jnp.pad(exponents.transpose(1, 0, 2), ((0, 0), (0, TAIL - kinds), (0, 0)))
@@ -121,7 +125,7 @@
 def per_device(
     train_input, train_preact, train_upstream, valid_input, valid_preact, valid_upstream
 ):
-    own, mine = class_gather(valid_input, valid_preact, valid_upstream)
+    own, mine, (is_first, is_second) = class_gather(valid_input, valid_preact, valid_upstream)
     own, train_preact, train_upstream = lax.optimization_barrier(
         (own, train_preact, train_upstream)
     )
@@ -131,10 +135,14 @@
     input_scale, grad_scale = 1.0 / math.sqrt(D), 1.0 / math.sqrt(FF)
     parts = [cross_dot(rows[:, :split], train_input) * input_scale for rows in (own, foreign)]
     parts += [cross_dot(rows[:, split:], train_grad) * grad_scale for rows in (own, foreign)]
-    pieces = jnp.stack(jnp.split(jnp.concatenate(parts), CORE, axis=1))
-    lower, upper = exchange(pieces, "core").reshape(CORE, 2, CLASSES, -1, pieces.shape[2])
-    upper = jnp.concatenate([upper[:, :2], upper[:, 3:], upper[:, 2:3]], axis=1)
-    coded = encode(lower + upper)
+    parts = jnp.concatenate(parts)
+    lower, upper = parts[:, :LANES], parts[:, LANES:]
+    sent = lower * is_second + upper * is_first
+    kept = lower * is_first + upper * is_second
+    other = lax.ppermute(sent, "core", [(0, 1), (1, 0)]).reshape(2, CLASSES, -1, LANES)
+    other = jnp.concatenate([other[:, :2], other[:, 3:], other[:, 2:3]], axis=1)
+    parts = kept.reshape(other.shape) + other
+    coded = encode(parts)
     input_kernel, grad_kernel = decode(exchange(coded, "yl"), 2)
     product = (input_kernel * grad_kernel).reshape(VAL_SEQS, -1, input_kernel.shape[1])
     sums = jnp.sum(product, axis=(1, 2)) * (1.0 / SEQ_LEN)

time: 117 us -> 116 us (level)
  blocking collectives: 85.5 us -> 79.3 us
  starting transfers between devices: 11.8 us -> 15.7 us
  waiting for transfers between devices: 11.2 us -> 12.7 us
    all_to_all x5 -> x4, blocking collectives: 85.5 us -> 79.3 us  [exchange(): lax.all_to_all(value, axes, 0, 0, axis_index_groups=groups, tiled=True)]
    ppermute x0 -> x1, starting transfers between devices: none -> 3.84 us  [per_device(): lax.ppermute(sent, 'core', [(0, 1), (1, 0)]).reshape(2, CLASSES, -1, LANES)]
    ppermute x0 -> x1, waiting for transfers between devices: none -> 1.51 us  [per_device(): lax.ppermute(sent, 'core', [(0, 1), (1, 0)]).reshape(2, CLASSES, -1, LANES)]
  transfers between devices with their start and end apart: 4 -> 5, of which waited for: 3 -> 4; matrix products, arithmetic and copies ran while one was open for 2% -> 2% of each run, Pallas kernels for 0% -> 0%
where the time goes in v11:
time: 116 us
  blocking collectives  79.3 us (68%)
  starting transfers between devices  15.7 us (14%)
  waiting for transfers between devices  12.7 us (11%)
  other arithmetic  2.63 us (2%)
  Pallas kernels  1.92 us (2%)
  matrix products  1.85 us (2%)
    all_to_all x4, blocking collectives, exchange(): lax.all_to_all(value, axes, 0, 0, axis_index_groups=groups, tiled=True)  79.3 us
    ppermute x4, starting transfers between devices, shift(): return lax.ppermute(value, DP + TENSOR, pairs)  11.8 us
    ppermute x4, waiting for transfers between devices, shift(): return lax.ppermute(value, DP + TENSOR, pairs)  11.2 us
    ppermute x1, starting transfers between devices, per_device(): lax.ppermute(sent, 'core', [(0, 1), (1, 0)]).reshape(2, CLASSES, -1, LANES)  3.84 us
  transfers between devices with their start and end apart: 5, of which 4 were waited for; matrix products, arithmetic and copies ran while one was open for 2% of the time, Pallas kernels for 0%

profile of v11, /device:TPU:1, one launch (start us, length us, event | category | flops | bytes accessed | tf_op | source)
XLA Modules:
  0.0 115.8 jit_solution(4396313035096808141)
XLA Ops:
  0.7 1.9 %shard_map.77 = (bf16[16,8,3200]{2,1,0:T(8,128)(2,1)}, f32[16,128]{1,0:T(8,128)}, f32[1,128]{1,0:T(1,128)}, f32[1,128]{1,0:T(1,128)}) custom-call(bf16[8,640]{1,0:T(8,128)(2,1)} %input_ref.1, bf16[8,2560]{1,0:T(8,128)(2,1)} %preact_ref.1, bf16[8,2560]{1,0:T(8,128)(2,1)} %upstream_ref.1), custom_call_target="tpu_custom_call" | custom-call | tf_op jit(solution)/shard_map/pallas_call | solution.py:89
  2.6 39.9 %all_to_all.29 = bf16[16,8,3200]{2,1,0:T(8,128)(2,1)S(1)} all-to-all(bf16[16,8,3200]{2,1,0:T(8,128)(2,1)} %get-tuple-element.9), channel_id=1, replica_groups={{0,48,64,112,128,176,192,240,256,304,320,368,384,432,448,496},{8,56,72,..., dimensions={0} | all-to-all | bytes 1638400 | tf_op jit(solution)/shard_map/all_to_all | solution.py:41
  42.5 3.4 %collective-permute-start.2 = (bf16[128,3200]{1,0:T(8,128)(2,1)S(1)}, bf16[128,3200]{1,0:T(8,128)(2,1)S(1)}, u32[]{:S(2)}, u32[]{:S(2)}) collective-permute-start(bf16[128,3200]{1,0:T(8,128)(2,1)S(1)} %bitcast.38), channel_id=1, source_target_pairs={{0,8},{1,25},{2,10},{3,27},{4,12},{5,29},{6,14},{7,31},{8,16},{9,1... | collective-permute-start | bytes 2457608 | tf_op jit(solution)/shard_map/ppermute | solution.py:68
  46.0 1.9 %collective-permute-start.3 = (bf16[128,3200]{1,0:T(8,128)(2,1)S(1)}, bf16[128,3200]{1,0:T(8,128)(2,1)S(1)}, u32[]{:S(2)}, u32[]{:S(2)}) collective-permute-start(bf16[128,3200]{1,0:T(8,128)(2,1)S(1)} %bitcast.39), channel_id=1, source_target_pairs={{0,24},{1,9},{2,26},{3,11},{4,28},{5,13},{6,30},{7,15},{8,0},{9,17... | collective-permute-start | bytes 2457608 | tf_op jit(solution)/shard_map/ppermute | solution.py:68
  47.9 4.6 %collective-permute-start = (bf16[64,3200]{1,0:T(8,128)(2,1)S(1)}, bf16[64,3200]{1,0:T(8,128)(2,1)S(1)}, u32[]{:S(2)}, u32[]{:S(2)}) collective-permute-start(bf16[64,3200]{1,0:T(8,128)(2,1)S(1)} %get-tuple-element.23), channel_id=1, source_target_pairs={{0,32},{1,225},{2,34},{3,227},{4,36},{5,229},{6,38},{7,231},{8,40}... | collective-permute-start | bytes 1228808 | tf_op jit(solution)/shard_map/ppermute | solution.py:68
  52.5 1.9 %collective-permute-start.1 = (bf16[64,3200]{1,0:T(8,128)(2,1)S(1)}, bf16[64,3200]{1,0:T(8,128)(2,1)S(1)}, u32[]{:S(2)}, u32[]{:S(2)}) collective-permute-start(bf16[64,3200]{1,0:T(8,128)(2,1)S(1)} %get-tuple-element.22), channel_id=1, source_target_pairs={{0,224},{1,33},{2,226},{3,35},{4,228},{5,37},{6,230},{7,39},{8,232... | collective-permute-start | bytes 1228808 | tf_op jit(solution)/shard_map/ppermute | solution.py:68
  54.4 1.3 %fusion.7 = bf16[256,2560]{1,0:T(8,128)(2,1)S(1)} fusion(bf16[256,2560]{1,0:T(8,128)(2,1)S(1)} %copy-done.1, bf16[256,2560]{1,0:T(8,128)(2,1)S(1)} %copy-done.2), kind=kLoop, calls=%fused_computation.11 | loop fusion | flops 7864320 | bytes 3932160 | tf_op jit(solution)/shard_map/convert_element_type | solution.py:31
  55.7 0.2 convolution_multiply_fusion.1
  56.0 0.5 convolution_multiply_fusion.2
  56.5 0.8 collective-permute-done
  57.4 7.7 %collective-permute-done.1 = bf16[64,3200]{1,0:T(8,128)(2,1)S(1)} collective-permute-done((bf16[64,3200]{1,0:T(8,128)(2,1)S(1)}, bf16[64,3200]{1,0:T(8,128)(2,1)S(1)}, u32[]{:S(2)}, u32[]{:S(2)}) %collective-permute-start.1) | collective-permute-done | bytes 409632 | tf_op jit(solution)/shard_map/ppermute | solution.py:68
  65.2 2.7 %collective-permute-done.3 = bf16[128,3200]{1,0:T(8,128)(2,1)S(1)} collective-permute-done((bf16[128,3200]{1,0:T(8,128)(2,1)S(1)}, bf16[128,3200]{1,0:T(8,128)(2,1)S(1)}, u32[]{:S(2)}, u32[]{:S(2)}) %collective-permute-start.3) | collective-permute-done | bytes 819232 | tf_op jit(solution)/shard_map/ppermute | solution.py:68
  68.0 0.7 fusion.10
  68.7 0.4 convolution_multiply_fusion
  69.2 0.2 copy-done.5
  69.4 0.1 multiply_add_fusion
  69.5 3.8 %collective-permute-start.4 = (f32[1024,128]{1,0:T(8,128)S(1)}, f32[1024,128]{1,0:T(8,128)S(1)}, u32[]{:S(2)}, u32[]{:S(2)}) collective-permute-start(f32[1024,128]{1,0:T(8,128)S(1)} %get-tuple-element.20), channel_id=1, source_target_pairs={{0,1},{1,0},{2,3},{3,2},{4,5},{5,4},{6,7},{7,6},{8,9},{9,8},{10,11... | collective-permute-start | bytes 1572872 | tf_op jit(solution)/shard_map/ppermute | solution.py:142
  73.4 1.5 %collective-permute-done.4 = f32[1024,128]{1,0:T(8,128)S(1)} collective-permute-done((f32[1024,128]{1,0:T(8,128)S(1)}, f32[1024,128]{1,0:T(8,128)S(1)}, u32[]{:S(2)}, u32[]{:S(2)}) %collective-permute-start.4) | collective-permute-done | bytes 524320 | tf_op jit(solution)/shard_map/ppermute | solution.py:142
  75.2 15.4 %all_to_all.30 = f16[4,264,128]{2,1,0:T(8,128)(2,1)S(1)} all-to-all(f16[4,264,128]{2,1,0:T(8,128)(2,1)S(1)} %fusion.17), channel_id=1, replica_groups=mesh['yh'=2,'z'=8,'x'=4,'yl'=4,'core'=2] {'yl'}, dimensions={0} | all-to-all | bytes 540672 | tf_op jit(solution)/shard_map/all_to_all | solution.py:41
  90.7 0.1 fusion.23
  90.9 0.1 reduce_sum.66
  91.0 11.9 %all_to_all.31 = f32[16,1,128]{2,1,0:T(1,128)S(1)} all-to-all(f32[16,1,128]{2,1,0:T(1,128)S(1)} %broadcast_in_dim.6), channel_id=1, replica_groups=mesh['yh'=2,'z'=8,'x'=4,'yl'=4,'core'=2] {'yh','yl','core'}, dimensions={0} | all-to-all | bytes 16384 | tf_op jit(solution)/shard_map/all_to_all | solution.py:41
  103.0 12.2 %all_to_all.32 = f32[32,1,128]{2,1,0:T(1,128)S(1)} all-to-all(f32[32,1,128]{2,1,0:T(1,128)S(1)} %broadcast_in_dim.8), channel_id=1, replica_groups=mesh['yh'=2,'z'=8,'x'=4,'yl'=4,'core'=2] {'z','x'}, dimensions={0} | all-to-all | bytes 32768 | tf_op jit(solution)/shard_map/all_to_all | solution.py:41
  115.2 0.6 multiply_reduce_fusion.2
  (38 shorter events, 0.9 us)
Async XLA Ops:
  0.6 55.1 %copy-start = (bf16[256,640]{1,0:T(8,128)(2,1)S(1)}, bf16[256,640]{1,0:T(8,128)(2,1)}, u32[]{:S(2)}) copy-start(bf16[256,640]{1,0:T(8,128)(2,1)} %param.6) | copy-start | bytes 983044
  0.6 53.7 %copy-start.1 = (bf16[256,2560]{1,0:T(8,128)(2,1)S(1)}, bf16[256,2560]{1,0:T(8,128)(2,1)}, u32[]{:S(2)}) copy-start(bf16[256,2560]{1,0:T(8,128)(2,1)} %param.7) | copy-start | bytes 3932164
  0.7 53.7 %copy-start.2 = (bf16[256,2560]{1,0:T(8,128)(2,1)S(1)}, bf16[256,2560]{1,0:T(8,128)(2,1)}, u32[]{:S(2)}) copy-start(bf16[256,2560]{1,0:T(8,128)(2,1)} %param.8) | copy-start | bytes 3932164
  42.5 22.6 %collective-permute-start.2 = (bf16[128,3200]{1,0:T(8,128)(2,1)S(1)}, bf16[128,3200]{1,0:T(8,128)(2,1)S(1)}, u32[]{:S(2)}, u32[]{:S(2)}) collective-permute-start(bf16[128,3200]{1,0:T(8,128)(2,1)S(1)} %bitcast.38), channel_id=1, source_target_pairs={{0,8},{1,25},{2,10},{3,27},{4,12},{5,29},{6,14},{7,31},{8,16},{9,1... | collective-permute-start | bytes 2457608 | tf_op jit(solution)/shard_map/ppermute | solution.py:68
  46.0 21.9 %collective-permute-start.3 = (bf16[128,3200]{1,0:T(8,128)(2,1)S(1)}, bf16[128,3200]{1,0:T(8,128)(2,1)S(1)}, u32[]{:S(2)}, u32[]{:S(2)}) collective-permute-start(bf16[128,3200]{1,0:T(8,128)(2,1)S(1)} %bitcast.39), channel_id=1, source_target_pairs={{0,24},{1,9},{2,26},{3,11},{4,28},{5,13},{6,30},{7,15},{8,0},{9,17... | collective-permute-start | bytes 2457608 | tf_op jit(solution)/shard_map/ppermute | solution.py:68
  47.9 9.4 %collective-permute-start = (bf16[64,3200]{1,0:T(8,128)(2,1)S(1)}, bf16[64,3200]{1,0:T(8,128)(2,1)S(1)}, u32[]{:S(2)}, u32[]{:S(2)}) collective-permute-start(bf16[64,3200]{1,0:T(8,128)(2,1)S(1)} %get-tuple-element.23), channel_id=1, source_target_pairs={{0,32},{1,225},{2,34},{3,227},{4,36},{5,229},{6,38},{7,231},{8,40}... | collective-permute-start | bytes 1228808 | tf_op jit(solution)/shard_map/ppermute | solution.py:68
  52.5 12.6 %collective-permute-start.1 = (bf16[64,3200]{1,0:T(8,128)(2,1)S(1)}, bf16[64,3200]{1,0:T(8,128)(2,1)S(1)}, u32[]{:S(2)}, u32[]{:S(2)}) collective-permute-start(bf16[64,3200]{1,0:T(8,128)(2,1)S(1)} %get-tuple-element.22), channel_id=1, source_target_pairs={{0,224},{1,33},{2,226},{3,35},{4,228},{5,37},{6,230},{7,39},{8,232... | collective-permute-start | bytes 1228808 | tf_op jit(solution)/shard_map/ppermute | solution.py:68
  68.7 0.7 copy-start.5
  68.7 0.7 copy-start.6
  69.5 5.4 %collective-permute-start.4 = (f32[1024,128]{1,0:T(8,128)S(1)}, f32[1024,128]{1,0:T(8,128)S(1)}, u32[]{:S(2)}, u32[]{:S(2)}) collective-permute-start(f32[1024,128]{1,0:T(8,128)S(1)} %get-tuple-element.20), channel_id=1, source_target_pairs={{0,1},{1,0},{2,3},{3,2},{4,5},{5,4},{6,7},{7,6},{8,9},{9,8},{10,11... | collective-permute-start | bytes 1572872 | tf_op jit(solution)/shard_map/ppermute | solution.py:142
  74.9 28.0 %copy-start.3 = (f32[16,128]{1,0:T(8,128)S(1)}, f32[16,128]{1,0:T(8,128)}, u32[]{:S(2)}) copy-start(f32[16,128]{1,0:T(8,128)} %get-tuple-element.15) | copy-start | bytes 24580
  102.9 12.9 %copy-start.4 = (f32[128]{0:T(128)}, f32[128]{0:T(128)S(1)}, u32[]{:S(2)}) copy-start(f32[128]{0:T(128)S(1)} %get-tuple-element.17) | copy-start | bytes 1540

commit v12 on v8

--- a/solution.py
+++ b/solution.py
@@ -16,7 +16,7 @@
 CLASSES = 4
 LANES = 128
 TAIL = 8
-LOW, HIGH = -126.0, 30.0
+LOW, HIGH, TOP = -110.0, 30.0, 15.0
 
 inv_root_two = 0.7071067811865476
 inv_root_tau = 0.3989422804014327
@@ -103,7 +103,7 @@
 def encode(parts):
     kinds, blocks, rows, lanes = parts.shape
     largest = jnp.max(jnp.abs(parts), axis=2)
-    exponents = jnp.clip(jnp.ceil(jnp.log2(jnp.maximum(largest, 2.0**LOW))), LOW, HIGH)
+    exponents = jnp.clip(jnp.ceil(jnp.log2(jnp.maximum(largest, 2.0**LOW))), LOW, HIGH) - TOP
     scale = jnp.exp2(-exponents)[:, :, None]
     scaled = [(parts[kind] * scale[kind]).astype(jnp.float16) for kind in range(kinds)]
     tail = jnp.pad(exponents.transpose(1, 0, 2), ((0, 0), (0, TAIL - kinds), (0, 0)))
@@ -131,8 +131,9 @@
     input_scale, grad_scale = 1.0 / math.sqrt(D), 1.0 / math.sqrt(FF)
     parts = [cross_dot(rows[:, :split], train_input) * input_scale for rows in (own, foreign)]
     parts += [cross_dot(rows[:, split:], train_grad) * grad_scale for rows in (own, foreign)]
-    pieces = jnp.stack(jnp.split(jnp.concatenate(parts), CORE, axis=1))
-    lower, upper = exchange(pieces, "core").reshape(CORE, 2, CLASSES, -1, pieces.shape[2])
+    halves = zip(*(jnp.split(part, CORE, axis=1) for part in parts))
+    pieces = jnp.concatenate([half for pieces in halves for half in pieces])
+    lower, upper = exchange(pieces, "core").reshape(CORE, 2, CLASSES, -1, pieces.shape[1])
     upper = jnp.concatenate([upper[:, :2], upper[:, 3:], upper[:, 2:3]], axis=1)
     coded = encode(lower + upper)
     input_kernel, grad_kernel = decode(exchange(coded, "yl"), 2)

time: 117 us -> 117 us (level)
  no operation moved by 1% of the time
where the time goes in v12:
time: 117 us; the launch traced here: 116 us
  blocking collectives  85.5 us (73%)
  starting transfers between devices  11.8 us (10%)
  waiting for transfers between devices  11.2 us (10%)
  other arithmetic  2.45 us (2%)
  Pallas kernels  1.92 us (2%)
  matrix products  1.86 us (2%)
    all_to_all x5, blocking collectives, exchange(): lax.all_to_all(value, axes, 0, 0, axis_index_groups=groups, tiled=True)  85.5 us
    ppermute x4, starting transfers between devices, shift(): return lax.ppermute(value, DP + TENSOR, pairs)  11.8 us
    ppermute x4, waiting for transfers between devices, shift(): return lax.ppermute(value, DP + TENSOR, pairs)  11.2 us
  transfers between devices with their start and end apart: 4, of which 3 were waited for; matrix products, arithmetic and copies ran while one was open for 2% of the time, Pallas kernels for 0%

profile of v12, /device:TPU:1, one launch (start us, length us, event | category | flops | bytes accessed | tf_op | source)
XLA Modules:
  0.0 116.3 jit_solution(903053469085630069)
XLA Ops:
  0.7 1.9 %shard_map.77 = (bf16[16,8,3200]{2,1,0:T(8,128)(2,1)}, f32[16,128]{1,0:T(8,128)}) custom-call(bf16[8,640]{1,0:T(8,128)(2,1)} %input_ref.1, bf16[8,2560]{1,0:T(8,128)(2,1)} %preact_ref.1, bf16[8,2560]{1,0:T(8,128)(2,1)} %upstream_ref.1), custom_call_target="tpu_custom_call" | custom-call | tf_op jit(solution)/shard_map/pallas_call | solution.py:86
  2.6 39.9 %all_to_all.38 = bf16[16,8,3200]{2,1,0:T(8,128)(2,1)S(1)} all-to-all(bf16[16,8,3200]{2,1,0:T(8,128)(2,1)} %get-tuple-element.7), channel_id=1, replica_groups={{0,48,64,112,128,176,192,240,256,304,320,368,384,432,448,496},{8,56,72,..., dimensions={0} | all-to-all | bytes 1638400 | tf_op jit(solution)/shard_map/all_to_all | solution.py:41
  42.5 3.4 %collective-permute-start.2 = (bf16[128,3200]{1,0:T(8,128)(2,1)S(1)}, bf16[128,3200]{1,0:T(8,128)(2,1)S(1)}, u32[]{:S(2)}, u32[]{:S(2)}) collective-permute-start(bf16[128,3200]{1,0:T(8,128)(2,1)S(1)} %bitcast.36), channel_id=1, source_target_pairs={{0,8},{1,25},{2,10},{3,27},{4,12},{5,29},{6,14},{7,31},{8,16},{9,1... | collective-permute-start | bytes 2457608 | tf_op jit(solution)/shard_map/ppermute | solution.py:68
  46.0 1.9 %collective-permute-start.3 = (bf16[128,3200]{1,0:T(8,128)(2,1)S(1)}, bf16[128,3200]{1,0:T(8,128)(2,1)S(1)}, u32[]{:S(2)}, u32[]{:S(2)}) collective-permute-start(bf16[128,3200]{1,0:T(8,128)(2,1)S(1)} %bitcast.37), channel_id=1, source_target_pairs={{0,24},{1,9},{2,26},{3,11},{4,28},{5,13},{6,30},{7,15},{8,0},{9,17... | collective-permute-start | bytes 2457608 | tf_op jit(solution)/shard_map/ppermute | solution.py:68
  47.9 4.6 %collective-permute-start = (bf16[64,3200]{1,0:T(8,128)(2,1)S(1)}, bf16[64,3200]{1,0:T(8,128)(2,1)S(1)}, u32[]{:S(2)}, u32[]{:S(2)}) collective-permute-start(bf16[64,3200]{1,0:T(8,128)(2,1)S(1)} %get-tuple-element.19), channel_id=1, source_target_pairs={{0,32},{1,225},{2,34},{3,227},{4,36},{5,229},{6,38},{7,231},{8,40}... | collective-permute-start | bytes 1228808 | tf_op jit(solution)/shard_map/ppermute | solution.py:68
  52.5 1.9 %collective-permute-start.1 = (bf16[64,3200]{1,0:T(8,128)(2,1)S(1)}, bf16[64,3200]{1,0:T(8,128)(2,1)S(1)}, u32[]{:S(2)}, u32[]{:S(2)}) collective-permute-start(bf16[64,3200]{1,0:T(8,128)(2,1)S(1)} %get-tuple-element.18), channel_id=1, source_target_pairs={{0,224},{1,33},{2,226},{3,35},{4,228},{5,37},{6,230},{7,39},{8,232... | collective-permute-start | bytes 1228808 | tf_op jit(solution)/shard_map/ppermute | solution.py:68
  54.4 0.2 convolution_multiply_fusion.1
  54.7 1.3 %fusion.7 = bf16[256,2560]{1,0:T(8,128)(2,1)S(1)} fusion(bf16[256,2560]{1,0:T(8,128)(2,1)S(1)} %copy-done.1, bf16[256,2560]{1,0:T(8,128)(2,1)S(1)} %copy-done.2), kind=kLoop, calls=%fused_computation.11 | loop fusion | flops 7864320 | bytes 3932160 | tf_op jit(solution)/shard_map/convert_element_type | solution.py:31
  56.0 0.5 convolution_multiply_fusion.2
  56.5 0.8 collective-permute-done
  57.4 7.7 %collective-permute-done.1 = bf16[64,3200]{1,0:T(8,128)(2,1)S(1)} collective-permute-done((bf16[64,3200]{1,0:T(8,128)(2,1)S(1)}, bf16[64,3200]{1,0:T(8,128)(2,1)S(1)}, u32[]{:S(2)}, u32[]{:S(2)}) %collective-permute-start.1) | collective-permute-done | bytes 409632 | tf_op jit(solution)/shard_map/ppermute | solution.py:68
  65.1 0.1 constant_dynamic-update-slice_fusion.1
  65.2 2.7 %collective-permute-done.3 = bf16[128,3200]{1,0:T(8,128)(2,1)S(1)} collective-permute-done((bf16[128,3200]{1,0:T(8,128)(2,1)S(1)}, bf16[128,3200]{1,0:T(8,128)(2,1)S(1)}, u32[]{:S(2)}, u32[]{:S(2)}) %collective-permute-start.3) | collective-permute-done | bytes 819232 | tf_op jit(solution)/shard_map/ppermute | solution.py:68
  67.9 0.1 constant_dynamic-update-slice_fusion
  68.0 0.4 convolution_multiply_fusion
  68.4 0.7 fusion.10
  69.2 6.1 %all_to_all.39 = f32[2,1024,128]{2,1,0:T(8,128)S(1)} all-to-all(f32[2,1024,128]{2,1,0:T(8,128)S(1)} %bitcast.43), channel_id=1, replica_groups=mesh['yh'=2,'z'=8,'x'=4,'yl'=4,'core'=2] {'core'}, dimensions={0} | all-to-all | bytes 2097152 | tf_op jit(solution)/shard_map/all_to_all | solution.py:41
  75.8 15.3 %all_to_all.40 = f16[4,264,128]{2,1,0:T(8,128)(2,1)S(1)} all-to-all(f16[4,264,128]{2,1,0:T(8,128)(2,1)S(1)} %fusion.17), channel_id=1, replica_groups=mesh['yh'=2,'z'=8,'x'=4,'yl'=4,'core'=2] {'yl'}, dimensions={0} | all-to-all | bytes 540672 | tf_op jit(solution)/shard_map/all_to_all | solution.py:41
  91.1 0.1 fusion.23
  91.2 0.1 reduce_sum.65
  91.3 0.1 reduce_sum.66
  91.5 11.9 %all_to_all.41 = f32[16,1,128]{2,1,0:T(1,128)S(1)} all-to-all(f32[16,1,128]{2,1,0:T(1,128)S(1)} %broadcast_in_dim.6), channel_id=1, replica_groups=mesh['yh'=2,'z'=8,'x'=4,'yl'=4,'core'=2] {'yh','yl','core'}, dimensions={0} | all-to-all | bytes 16384 | tf_op jit(solution)/shard_map/all_to_all | solution.py:41
  103.5 12.2 %all_to_all.42 = f32[32,1,128]{2,1,0:T(1,128)S(1)} all-to-all(f32[32,1,128]{2,1,0:T(1,128)S(1)} %broadcast_in_dim.8), channel_id=1, replica_groups=mesh['yh'=2,'z'=8,'x'=4,'yl'=4,'core'=2] {'z','x'}, dimensions={0} | all-to-all | bytes 32768 | tf_op jit(solution)/shard_map/all_to_all | solution.py:41
  115.7 0.6 multiply_reduce_fusion.2
  (40 shorter events, 0.7 us)
Async XLA Ops:
  0.6 53.8 %copy-start = (bf16[256,640]{1,0:T(8,128)(2,1)S(1)}, bf16[256,640]{1,0:T(8,128)(2,1)}, u32[]{:S(2)}) copy-start(bf16[256,640]{1,0:T(8,128)(2,1)} %param.6) | copy-start | bytes 983044
  0.6 54.0 %copy-start.1 = (bf16[256,2560]{1,0:T(8,128)(2,1)S(1)}, bf16[256,2560]{1,0:T(8,128)(2,1)}, u32[]{:S(2)}) copy-start(bf16[256,2560]{1,0:T(8,128)(2,1)} %param.7) | copy-start | bytes 3932164
  0.7 54.0 %copy-start.2 = (bf16[256,2560]{1,0:T(8,128)(2,1)S(1)}, bf16[256,2560]{1,0:T(8,128)(2,1)}, u32[]{:S(2)}) copy-start(bf16[256,2560]{1,0:T(8,128)(2,1)} %param.8) | copy-start | bytes 3932164
  42.5 22.6 %collective-permute-start.2 = (bf16[128,3200]{1,0:T(8,128)(2,1)S(1)}, bf16[128,3200]{1,0:T(8,128)(2,1)S(1)}, u32[]{:S(2)}, u32[]{:S(2)}) collective-permute-start(bf16[128,3200]{1,0:T(8,128)(2,1)S(1)} %bitcast.36), channel_id=1, source_target_pairs={{0,8},{1,25},{2,10},{3,27},{4,12},{5,29},{6,14},{7,31},{8,16},{9,1... | collective-permute-start | bytes 2457608 | tf_op jit(solution)/shard_map/ppermute | solution.py:68
  46.0 21.9 %collective-permute-start.3 = (bf16[128,3200]{1,0:T(8,128)(2,1)S(1)}, bf16[128,3200]{1,0:T(8,128)(2,1)S(1)}, u32[]{:S(2)}, u32[]{:S(2)}) collective-permute-start(bf16[128,3200]{1,0:T(8,128)(2,1)S(1)} %bitcast.37), channel_id=1, source_target_pairs={{0,24},{1,9},{2,26},{3,11},{4,28},{5,13},{6,30},{7,15},{8,0},{9,17... | collective-permute-start | bytes 2457608 | tf_op jit(solution)/shard_map/ppermute | solution.py:68
  47.9 9.4 %collective-permute-start = (bf16[64,3200]{1,0:T(8,128)(2,1)S(1)}, bf16[64,3200]{1,0:T(8,128)(2,1)S(1)}, u32[]{:S(2)}, u32[]{:S(2)}) collective-permute-start(bf16[64,3200]{1,0:T(8,128)(2,1)S(1)} %get-tuple-element.19), channel_id=1, source_target_pairs={{0,32},{1,225},{2,34},{3,227},{4,36},{5,229},{6,38},{7,231},{8,40}... | collective-permute-start | bytes 1228808 | tf_op jit(solution)/shard_map/ppermute | solution.py:68
  52.5 12.6 %collective-permute-start.1 = (bf16[64,3200]{1,0:T(8,128)(2,1)S(1)}, bf16[64,3200]{1,0:T(8,128)(2,1)S(1)}, u32[]{:S(2)}, u32[]{:S(2)}) collective-permute-start(bf16[64,3200]{1,0:T(8,128)(2,1)S(1)} %get-tuple-element.18), channel_id=1, source_target_pairs={{0,224},{1,33},{2,226},{3,35},{4,228},{5,37},{6,230},{7,39},{8,232... | collective-permute-start | bytes 1228808 | tf_op jit(solution)/shard_map/ppermute | solution.py:68
  75.4 28.0 %copy-start.3 = (f32[16,128]{1,0:T(8,128)S(1)}, f32[16,128]{1,0:T(8,128)}, u32[]{:S(2)}) copy-start(f32[16,128]{1,0:T(8,128)} %get-tuple-element.11) | copy-start | bytes 24580
  103.4 12.9 %copy-start.4 = (f32[128]{0:T(128)}, f32[128]{0:T(128)S(1)}, u32[]{:S(2)}) copy-start(f32[128]{0:T(128)S(1)} %get-tuple-element.13) | copy-start | bytes 1540

commit v13 on v12

--- a/solution.py
+++ b/solution.py
@@ -97,7 +97,7 @@
     half = own.shape[0] // 2
     first, second = shift(own, 0, 1), shift(own, 0, -1)
     across = [shift(own[:half], 1, 0), shift(own[half:], -1, 0)]
-    return jnp.concatenate(across + [first, second])
+    return jnp.concatenate(across), jnp.concatenate([first, second])
 
 
 def encode(parts):
@@ -125,12 +125,12 @@
     own, train_preact, train_upstream = lax.optimization_barrier(
         (own, train_preact, train_upstream)
     )
-    foreign = neighbour_rows(own)
+    blocks = (own,) + neighbour_rows(own)
     train_grad = lax.optimization_barrier(output_grad(train_preact, train_upstream))
     split = valid_input.shape[1]
     input_scale, grad_scale = 1.0 / math.sqrt(D), 1.0 / math.sqrt(FF)
-    parts = [cross_dot(rows[:, :split], train_input) * input_scale for rows in (own, foreign)]
-    parts += [cross_dot(rows[:, split:], train_grad) * grad_scale for rows in (own, foreign)]
+    parts = [cross_dot(rows[:, :split], train_input) * input_scale for rows in blocks]
+    parts += [cross_dot(rows[:, split:], train_grad) * grad_scale for rows in blocks]
     halves = zip(*(jnp.split(part, CORE, axis=1) for part in parts))
     pieces = jnp.concatenate([half for pieces in halves for half in pieces])
     lower, upper = exchange(pieces, "core").reshape(CORE, 2, CLASSES, -1, pieces.shape[1])

time: 117 us -> 118 us (level)
  waiting for transfers between devices: 11.2 us -> 7.39 us
  blocking collectives: 85.5 us -> 88.3 us
  starting transfers between devices: 11.8 us -> 13 us
    ppermute x4, waiting for transfers between devices: 11.2 us -> 7.39 us  [shift(): return lax.ppermute(value, DP + TENSOR, pairs)]
    all_to_all x5, blocking collectives: 85.5 us -> 88.3 us  [exchange(): lax.all_to_all(value, axes, 0, 0, axis_index_groups=groups, tiled=True)]
    dot_general x4 -> x6, matrix products: 1.86 us -> 2.42 us  [cross_dot(): lax.dot_general(left, right, (((1,), (1,)), ((), ())), preferred_element_...]
  transfers between devices with their start and end apart: 4 -> 4, of which waited for: 3 -> 1; matrix products, arithmetic and copies ran while one was open for 2% -> 3% of each run, Pallas kernels for 0% -> 0%
where the time goes in v13:
time: 118 us; the launch traced here: 117 us
  blocking collectives  88.3 us (75%)
  starting transfers between devices  13 us (11%)
  waiting for transfers between devices  7.39 us (6%)
  other arithmetic  2.45 us (2%)
  matrix products  2.42 us (2%)
  Pallas kernels  1.81 us (2%)
    all_to_all x5, blocking collectives, exchange(): lax.all_to_all(value, axes, 0, 0, axis_index_groups=groups, tiled=True)  88.3 us
    ppermute x4, starting transfers between devices, shift(): return lax.ppermute(value, DP + TENSOR, pairs)  13 us
    ppermute x4, waiting for transfers between devices, shift(): return lax.ppermute(value, DP + TENSOR, pairs)  7.39 us
    dot_general x6, matrix products, cross_dot(): lax.dot_general(left, right, (((1,), (1,)), ((), ())), preferred_element_...  2.42 us
  transfers between devices with their start and end apart: 4, of which 1 were waited for; matrix products, arithmetic and copies ran while one was open for 3% of the time, Pallas kernels for 0%

profile of v13, /device:TPU:1, one launch (start us, length us, event | category | flops | bytes accessed | tf_op | source)
XLA Modules:
  0.0 117.0 jit_solution(3160061230472604775)
XLA Ops:
  0.6 1.8 %shard_map.77 = (bf16[16,8,3200]{2,1,0:T(8,128)(2,1)}, f32[16,128]{1,0:T(8,128)}) custom-call(bf16[8,640]{1,0:T(8,128)(2,1)} %input_ref.1, bf16[8,2560]{1,0:T(8,128)(2,1)} %preact_ref.1, bf16[8,2560]{1,0:T(8,128)(2,1)} %upstream_ref.1), custom_call_target="tpu_custom_call" | custom-call | tf_op jit(solution)/shard_map/pallas_call | solution.py:86
  2.5 40.1 %all_to_all.38 = bf16[16,8,3200]{2,1,0:T(8,128)(2,1)S(1)} all-to-all(bf16[16,8,3200]{2,1,0:T(8,128)(2,1)} %get-tuple-element.7), channel_id=1, replica_groups={{0,48,64,112,128,176,192,240,256,304,320,368,384,432,448,496},{8,56,72,..., dimensions={0} | all-to-all | bytes 1638400 | tf_op jit(solution)/shard_map/all_to_all | solution.py:41
  42.7 2.9 %collective-permute-start.3 = (bf16[128,3200]{1,0:T(8,128)(2,1)S(1)}, bf16[128,3200]{1,0:T(8,128)(2,1)S(1)}, u32[]{:S(2)}, u32[]{:S(2)}) collective-permute-start(bf16[128,3200]{1,0:T(8,128)(2,1)S(1)} %bitcast.38), channel_id=1, source_target_pairs={{0,24},{1,9},{2,26},{3,11},{4,28},{5,13},{6,30},{7,15},{8,0},{9,17... | collective-permute-start | bytes 2457608 | tf_op jit(solution)/shard_map/ppermute | solution.py:68
  45.5 3.6 %collective-permute-start.2 = (bf16[128,3200]{1,0:T(8,128)(2,1)S(1)}, bf16[128,3200]{1,0:T(8,128)(2,1)S(1)}, u32[]{:S(2)}, u32[]{:S(2)}) collective-permute-start(bf16[128,3200]{1,0:T(8,128)(2,1)S(1)} %bitcast.39), channel_id=1, source_target_pairs={{0,8},{1,25},{2,10},{3,27},{4,12},{5,29},{6,14},{7,31},{8,16},{9,1... | collective-permute-start | bytes 2457608 | tf_op jit(solution)/shard_map/ppermute | solution.py:68
  49.2 0.2 convolution_multiply_fusion.2
  49.4 1.9 %collective-permute-start.1 = (bf16[64,3200]{1,0:T(8,128)(2,1)S(1)}, bf16[64,3200]{1,0:T(8,128)(2,1)S(1)}, u32[]{:S(2)}, u32[]{:S(2)}) collective-permute-start(bf16[64,3200]{1,0:T(8,128)(2,1)S(1)} %get-tuple-element.18), channel_id=1, source_target_pairs={{0,224},{1,33},{2,226},{3,35},{4,228},{5,37},{6,230},{7,39},{8,232... | collective-permute-start | bytes 1228808 | tf_op jit(solution)/shard_map/ppermute | solution.py:68
  51.4 4.6 %collective-permute-start = (bf16[64,3200]{1,0:T(8,128)(2,1)S(1)}, bf16[64,3200]{1,0:T(8,128)(2,1)S(1)}, u32[]{:S(2)}, u32[]{:S(2)}) collective-permute-start(bf16[64,3200]{1,0:T(8,128)(2,1)S(1)} %get-tuple-element.19), channel_id=1, source_target_pairs={{0,32},{1,225},{2,34},{3,227},{4,36},{5,229},{6,38},{7,231},{8,40}... | collective-permute-start | bytes 1228808 | tf_op jit(solution)/shard_map/ppermute | solution.py:68
  56.0 1.3 %fusion.7 = bf16[256,2560]{1,0:T(8,128)(2,1)S(1)} fusion(bf16[256,2560]{1,0:T(8,128)(2,1)S(1)} %copy-done.1, bf16[256,2560]{1,0:T(8,128)(2,1)S(1)} %copy-done.2), kind=kLoop, calls=%fused_computation.11 | loop fusion | flops 7864320 | bytes 3932160 | tf_op jit(solution)/shard_map/convert_element_type | solution.py:31
  57.3 0.5 convolution_multiply_fusion.4
  57.8 7.4 %collective-permute-done = bf16[64,3200]{1,0:T(8,128)(2,1)S(1)} collective-permute-done((bf16[64,3200]{1,0:T(8,128)(2,1)S(1)}, bf16[64,3200]{1,0:T(8,128)(2,1)S(1)}, u32[]{:S(2)}, u32[]{:S(2)}) %collective-permute-start) | collective-permute-done | bytes 409632 | tf_op jit(solution)/shard_map/ppermute | solution.py:68
  65.3 0.2 convolution_multiply_fusion.1
  65.5 0.5 convolution_multiply_fusion.3
  66.2 0.1 constant_dynamic-update-slice_fusion.2
  66.3 0.3 convolution_multiply_fusion
  66.6 0.5 fusion.10
  67.3 6.1 %all_to_all.39 = f32[2,1024,128]{2,1,0:T(8,128)S(1)} all-to-all(f32[2,1024,128]{2,1,0:T(8,128)S(1)} %bitcast.45), channel_id=1, replica_groups=mesh['yh'=2,'z'=8,'x'=4,'yl'=4,'core'=2] {'core'}, dimensions={0} | all-to-all | bytes 2097152 | tf_op jit(solution)/shard_map/all_to_all | solution.py:41
  73.7 0.1 fusion.18
  73.8 15.9 %all_to_all.40 = f16[4,264,128]{2,1,0:T(8,128)(2,1)S(1)} all-to-all(f16[4,264,128]{2,1,0:T(8,128)(2,1)S(1)} %fusion.18), channel_id=1, replica_groups=mesh['yh'=2,'z'=8,'x'=4,'yl'=4,'core'=2] {'yl'}, dimensions={0} | all-to-all | bytes 540672 | tf_op jit(solution)/shard_map/all_to_all | solution.py:41
  89.8 0.1 fusion.25
  89.9 0.1 reduce_sum.65
  89.9 0.1 reduce_sum.66
  90.1 11.9 %all_to_all.41 = f32[16,1,128]{2,1,0:T(1,128)S(1)} all-to-all(f32[16,1,128]{2,1,0:T(1,128)S(1)} %broadcast_in_dim.6), channel_id=1, replica_groups=mesh['yh'=2,'z'=8,'x'=4,'yl'=4,'core'=2] {'yh','yl','core'}, dimensions={0} | all-to-all | bytes 16384 | tf_op jit(solution)/shard_map/all_to_all | solution.py:41
  102.1 14.3 %all_to_all.42 = f32[32,1,128]{2,1,0:T(1,128)S(1)} all-to-all(f32[32,1,128]{2,1,0:T(1,128)S(1)} %broadcast_in_dim.8), channel_id=1, replica_groups=mesh['yh'=2,'z'=8,'x'=4,'yl'=4,'core'=2] {'z','x'}, dimensions={0} | all-to-all | bytes 32768 | tf_op jit(solution)/shard_map/all_to_all | solution.py:41
  116.4 0.6 multiply_reduce_fusion.2
  (46 shorter events, 0.7 us)
Async XLA Ops:
  0.6 48.5 %copy-start = (bf16[256,640]{1,0:T(8,128)(2,1)S(1)}, bf16[256,640]{1,0:T(8,128)(2,1)}, u32[]{:S(2)}) copy-start(bf16[256,640]{1,0:T(8,128)(2,1)} %param.6) | copy-start | bytes 983044
  2.5 53.5 %copy-start.1 = (bf16[256,2560]{1,0:T(8,128)(2,1)S(1)}, bf16[256,2560]{1,0:T(8,128)(2,1)}, u32[]{:S(2)}) copy-start(bf16[256,2560]{1,0:T(8,128)(2,1)} %param.7) | copy-start | bytes 3932164
  2.5 53.5 %copy-start.2 = (bf16[256,2560]{1,0:T(8,128)(2,1)S(1)}, bf16[256,2560]{1,0:T(8,128)(2,1)}, u32[]{:S(2)}) copy-start(bf16[256,2560]{1,0:T(8,128)(2,1)} %param.8) | copy-start | bytes 3932164
  42.7 23.5 %collective-permute-start.3 = (bf16[128,3200]{1,0:T(8,128)(2,1)S(1)}, bf16[128,3200]{1,0:T(8,128)(2,1)S(1)}, u32[]{:S(2)}, u32[]{:S(2)}) collective-permute-start(bf16[128,3200]{1,0:T(8,128)(2,1)S(1)} %bitcast.38), channel_id=1, source_target_pairs={{0,24},{1,9},{2,26},{3,11},{4,28},{5,13},{6,30},{7,15},{8,0},{9,17... | collective-permute-start | bytes 2457608 | tf_op jit(solution)/shard_map/ppermute | solution.py:68
  45.5 20.6 %collective-permute-start.2 = (bf16[128,3200]{1,0:T(8,128)(2,1)S(1)}, bf16[128,3200]{1,0:T(8,128)(2,1)S(1)}, u32[]{:S(2)}, u32[]{:S(2)}) collective-permute-start(bf16[128,3200]{1,0:T(8,128)(2,1)S(1)} %bitcast.39), channel_id=1, source_target_pairs={{0,8},{1,25},{2,10},{3,27},{4,12},{5,29},{6,14},{7,31},{8,16},{9,1... | collective-permute-start | bytes 2457608 | tf_op jit(solution)/shard_map/ppermute | solution.py:68
  49.4 15.8 %collective-permute-start.1 = (bf16[64,3200]{1,0:T(8,128)(2,1)S(1)}, bf16[64,3200]{1,0:T(8,128)(2,1)S(1)}, u32[]{:S(2)}, u32[]{:S(2)}) collective-permute-start(bf16[64,3200]{1,0:T(8,128)(2,1)S(1)} %get-tuple-element.18), channel_id=1, source_target_pairs={{0,224},{1,33},{2,226},{3,35},{4,228},{5,37},{6,230},{7,39},{8,232... | collective-permute-start | bytes 1228808 | tf_op jit(solution)/shard_map/ppermute | solution.py:68
  51.4 13.8 %collective-permute-start = (bf16[64,3200]{1,0:T(8,128)(2,1)S(1)}, bf16[64,3200]{1,0:T(8,128)(2,1)S(1)}, u32[]{:S(2)}, u32[]{:S(2)}) collective-permute-start(bf16[64,3200]{1,0:T(8,128)(2,1)S(1)} %get-tuple-element.19), channel_id=1, source_target_pairs={{0,32},{1,225},{2,34},{3,227},{4,36},{5,229},{6,38},{7,231},{8,40}... | collective-permute-start | bytes 1228808 | tf_op jit(solution)/shard_map/ppermute | solution.py:68
  73.5 28.5 %copy-start.3 = (f32[16,128]{1,0:T(8,128)S(1)}, f32[16,128]{1,0:T(8,128)}, u32[]{:S(2)}) copy-start(f32[16,128]{1,0:T(8,128)} %get-tuple-element.11) | copy-start | bytes 24580
  102.1 15.0 %copy-start.4 = (f32[128]{0:T(128)}, f32[128]{0:T(128)S(1)}, u32[]{:S(2)}) copy-start(f32[128]{0:T(128)S(1)} %get-tuple-element.13) | copy-start | bytes 1540

commit v14 on v12

--- a/solution.py
+++ b/solution.py
@@ -47,7 +47,12 @@
 
 def class_groups():
     return [
-        [place(yh, z, kind - 2 * z) for yh in range(YH) for z in range(Z)]
+        [
+            place(yh, (kind - 2 * x) % 4 + 4 * far, x)
+            for yh in range(YH)
+            for x in range(X)
+            for far in range(2)
+        ]
         for kind in range(CLASSES)
     ]
 
@@ -95,8 +100,8 @@
 
 def neighbour_rows(own):
     half = own.shape[0] // 2
-    first, second = shift(own, 0, 1), shift(own, 0, -1)
-    across = [shift(own[:half], 1, 0), shift(own[half:], -1, 0)]
+    first, second = shift(own, 1, 0), shift(own, -1, 0)
+    across = [shift(own[:half], 0, 1), shift(own[half:], 0, -1)]
     return jnp.concatenate(across + [first, second])
 
 

time: 117 us -> 120 us (1.026)
  waiting for transfers between devices: 11.2 us -> 12.6 us
    ppermute x4, waiting for transfers between devices: 11.2 us -> 12.6 us  [shift(): return lax.ppermute(value, DP + TENSOR, pairs)]
where the time goes in v14:
time: 120 us; the launch traced here: 119 us
  blocking collectives  86.3 us (72%)
  waiting for transfers between devices  12.6 us (10%)
  starting transfers between devices  12.3 us (10%)
  other arithmetic  2.45 us (2%)
  Pallas kernels  1.92 us (2%)
  matrix products  1.86 us (2%)
    all_to_all x5, blocking collectives, exchange(): lax.all_to_all(value, axes, 0, 0, axis_index_groups=groups, tiled=True)  86.3 us
    ppermute x4, waiting for transfers between devices, shift(): return lax.ppermute(value, DP + TENSOR, pairs)  12.6 us
    ppermute x4, starting transfers between devices, shift(): return lax.ppermute(value, DP + TENSOR, pairs)  12.3 us
  transfers between devices with their start and end apart: 4, of which 3 were waited for; matrix products, arithmetic and copies ran while one was open for 2% of the time, Pallas kernels for 0%

profile of v14, /device:TPU:1, one launch (start us, length us, event | category | flops | bytes accessed | tf_op | source)
XLA Modules:
  0.0 119.1 jit_solution(17720401861259824609)
XLA Ops:
  0.7 1.9 %shard_map.77 = (bf16[16,8,3200]{2,1,0:T(8,128)(2,1)}, f32[16,128]{1,0:T(8,128)}) custom-call(bf16[8,640]{1,0:T(8,128)(2,1)} %input_ref.1, bf16[8,2560]{1,0:T(8,128)(2,1)} %preact_ref.1, bf16[8,2560]{1,0:T(8,128)(2,1)} %upstream_ref.1), custom_call_target="tpu_custom_call" | custom-call | tf_op jit(solution)/shard_map/pallas_call | solution.py:91
  2.6 41.8 %all_to_all.38 = bf16[16,8,3200]{2,1,0:T(8,128)(2,1)S(1)} all-to-all(bf16[16,8,3200]{2,1,0:T(8,128)(2,1)} %get-tuple-element.7), channel_id=1, replica_groups={{0,128,72,200,16,144,88,216,256,384,328,456,272,400,344,472},{32,160,10..., dimensions={0} | all-to-all | bytes 1638400 | tf_op jit(solution)/shard_map/all_to_all | solution.py:41
  44.4 4.1 %collective-permute-start.2 = (bf16[128,3200]{1,0:T(8,128)(2,1)S(1)}, bf16[128,3200]{1,0:T(8,128)(2,1)S(1)}, u32[]{:S(2)}, u32[]{:S(2)}) collective-permute-start(bf16[128,3200]{1,0:T(8,128)(2,1)S(1)} %bitcast.36), channel_id=1, source_target_pairs={{0,32},{1,225},{2,34},{3,227},{4,36},{5,229},{6,38},{7,231},{8,40}... | collective-permute-start | bytes 2457608 | tf_op jit(solution)/shard_map/ppermute | solution.py:73
  48.5 1.9 %collective-permute-start.3 = (bf16[128,3200]{1,0:T(8,128)(2,1)S(1)}, bf16[128,3200]{1,0:T(8,128)(2,1)S(1)}, u32[]{:S(2)}, u32[]{:S(2)}) collective-permute-start(bf16[128,3200]{1,0:T(8,128)(2,1)S(1)} %bitcast.37), channel_id=1, source_target_pairs={{0,224},{1,33},{2,226},{3,35},{4,228},{5,37},{6,230},{7,39},{8,232... | collective-permute-start | bytes 2457608 | tf_op jit(solution)/shard_map/ppermute | solution.py:73
  50.5 4.4 %collective-permute-start = (bf16[64,3200]{1,0:T(8,128)(2,1)S(1)}, bf16[64,3200]{1,0:T(8,128)(2,1)S(1)}, u32[]{:S(2)}, u32[]{:S(2)}) collective-permute-start(bf16[64,3200]{1,0:T(8,128)(2,1)S(1)} %get-tuple-element.19), channel_id=1, source_target_pairs={{0,8},{1,25},{2,10},{3,27},{4,12},{5,29},{6,14},{7,31},{8,16},{9,1... | collective-permute-start | bytes 1228808 | tf_op jit(solution)/shard_map/ppermute | solution.py:73
  54.9 1.9 %collective-permute-start.1 = (bf16[64,3200]{1,0:T(8,128)(2,1)S(1)}, bf16[64,3200]{1,0:T(8,128)(2,1)S(1)}, u32[]{:S(2)}, u32[]{:S(2)}) collective-permute-start(bf16[64,3200]{1,0:T(8,128)(2,1)S(1)} %get-tuple-element.18), channel_id=1, source_target_pairs={{0,24},{1,9},{2,26},{3,11},{4,28},{5,13},{6,30},{7,15},{8,0},{9,17... | collective-permute-start | bytes 1228808 | tf_op jit(solution)/shard_map/ppermute | solution.py:73
  56.8 0.2 convolution_multiply_fusion.1
  57.1 1.3 %fusion.7 = bf16[256,2560]{1,0:T(8,128)(2,1)S(1)} fusion(bf16[256,2560]{1,0:T(8,128)(2,1)S(1)} %copy-done.1, bf16[256,2560]{1,0:T(8,128)(2,1)S(1)} %copy-done.2), kind=kLoop, calls=%fused_computation.11 | loop fusion | flops 7864320 | bytes 3932160 | tf_op jit(solution)/shard_map/convert_element_type | solution.py:31
  58.4 0.5 convolution_multiply_fusion.2
  58.9 0.8 collective-permute-done
  59.8 8.8 %collective-permute-done.1 = bf16[64,3200]{1,0:T(8,128)(2,1)S(1)} collective-permute-done((bf16[64,3200]{1,0:T(8,128)(2,1)S(1)}, bf16[64,3200]{1,0:T(8,128)(2,1)S(1)}, u32[]{:S(2)}, u32[]{:S(2)}) %collective-permute-start.1) | collective-permute-done | bytes 409632 | tf_op jit(solution)/shard_map/ppermute | solution.py:73
  68.6 0.1 constant_dynamic-update-slice_fusion.1
  68.7 3.0 %collective-permute-done.3 = bf16[128,3200]{1,0:T(8,128)(2,1)S(1)} collective-permute-done((bf16[128,3200]{1,0:T(8,128)(2,1)S(1)}, bf16[128,3200]{1,0:T(8,128)(2,1)S(1)}, u32[]{:S(2)}, u32[]{:S(2)}) %collective-permute-start.3) | collective-permute-done | bytes 819232 | tf_op jit(solution)/shard_map/ppermute | solution.py:73
  71.7 0.1 constant_dynamic-update-slice_fusion
  71.8 0.4 convolution_multiply_fusion
  72.2 0.7 fusion.10
  73.0 4.9 %all_to_all.39 = f32[2,1024,128]{2,1,0:T(8,128)S(1)} all-to-all(f32[2,1024,128]{2,1,0:T(8,128)S(1)} %bitcast.43), channel_id=1, replica_groups=mesh['yh'=2,'z'=8,'x'=4,'yl'=4,'core'=2] {'core'}, dimensions={0} | all-to-all | bytes 2097152 | tf_op jit(solution)/shard_map/all_to_all | solution.py:41
  78.3 15.4 %all_to_all.40 = f16[4,264,128]{2,1,0:T(8,128)(2,1)S(1)} all-to-all(f16[4,264,128]{2,1,0:T(8,128)(2,1)S(1)} %fusion.17), channel_id=1, replica_groups=mesh['yh'=2,'z'=8,'x'=4,'yl'=4,'core'=2] {'yl'}, dimensions={0} | all-to-all | bytes 540672 | tf_op jit(solution)/shard_map/all_to_all | solution.py:41
  93.8 0.1 fusion.23
  93.9 0.1 reduce_sum.65
  94.0 0.1 reduce_sum.66
  94.2 11.9 %all_to_all.41 = f32[16,1,128]{2,1,0:T(1,128)S(1)} all-to-all(f32[16,1,128]{2,1,0:T(1,128)S(1)} %broadcast_in_dim.6), channel_id=1, replica_groups=mesh['yh'=2,'z'=8,'x'=4,'yl'=4,'core'=2] {'yh','yl','core'}, dimensions={0} | all-to-all | bytes 16384 | tf_op jit(solution)/shard_map/all_to_all | solution.py:41
  106.2 12.3 %all_to_all.42 = f32[32,1,128]{2,1,0:T(1,128)S(1)} all-to-all(f32[32,1,128]{2,1,0:T(1,128)S(1)} %broadcast_in_dim.8), channel_id=1, replica_groups=mesh['yh'=2,'z'=8,'x'=4,'yl'=4,'core'=2] {'z','x'}, dimensions={0} | all-to-all | bytes 32768 | tf_op jit(solution)/shard_map/all_to_all | solution.py:41
  118.5 0.6 multiply_reduce_fusion.2
  (40 shorter events, 0.7 us)
Async XLA Ops:
  0.6 56.2 %copy-start = (bf16[256,640]{1,0:T(8,128)(2,1)S(1)}, bf16[256,640]{1,0:T(8,128)(2,1)}, u32[]{:S(2)}) copy-start(bf16[256,640]{1,0:T(8,128)(2,1)} %param.6) | copy-start | bytes 983044
  0.6 56.4 %copy-start.1 = (bf16[256,2560]{1,0:T(8,128)(2,1)S(1)}, bf16[256,2560]{1,0:T(8,128)(2,1)}, u32[]{:S(2)}) copy-start(bf16[256,2560]{1,0:T(8,128)(2,1)} %param.7) | copy-start | bytes 3932164
  0.7 56.4 %copy-start.2 = (bf16[256,2560]{1,0:T(8,128)(2,1)S(1)}, bf16[256,2560]{1,0:T(8,128)(2,1)}, u32[]{:S(2)}) copy-start(bf16[256,2560]{1,0:T(8,128)(2,1)} %param.8) | copy-start | bytes 3932164
  44.4 24.2 %collective-permute-start.2 = (bf16[128,3200]{1,0:T(8,128)(2,1)S(1)}, bf16[128,3200]{1,0:T(8,128)(2,1)S(1)}, u32[]{:S(2)}, u32[]{:S(2)}) collective-permute-start(bf16[128,3200]{1,0:T(8,128)(2,1)S(1)} %bitcast.36), channel_id=1, source_target_pairs={{0,32},{1,225},{2,34},{3,227},{4,36},{5,229},{6,38},{7,231},{8,40}... | collective-permute-start | bytes 2457608 | tf_op jit(solution)/shard_map/ppermute | solution.py:73
  48.5 23.2 %collective-permute-start.3 = (bf16[128,3200]{1,0:T(8,128)(2,1)S(1)}, bf16[128,3200]{1,0:T(8,128)(2,1)S(1)}, u32[]{:S(2)}, u32[]{:S(2)}) collective-permute-start(bf16[128,3200]{1,0:T(8,128)(2,1)S(1)} %bitcast.37), channel_id=1, source_target_pairs={{0,224},{1,33},{2,226},{3,35},{4,228},{5,37},{6,230},{7,39},{8,232... | collective-permute-start | bytes 2457608 | tf_op jit(solution)/shard_map/ppermute | solution.py:73
  50.5 9.3 %collective-permute-start = (bf16[64,3200]{1,0:T(8,128)(2,1)S(1)}, bf16[64,3200]{1,0:T(8,128)(2,1)S(1)}, u32[]{:S(2)}, u32[]{:S(2)}) collective-permute-start(bf16[64,3200]{1,0:T(8,128)(2,1)S(1)} %get-tuple-element.19), channel_id=1, source_target_pairs={{0,8},{1,25},{2,10},{3,27},{4,12},{5,29},{6,14},{7,31},{8,16},{9,1... | collective-permute-start | bytes 1228808 | tf_op jit(solution)/shard_map/ppermute | solution.py:73
  54.9 13.7 %collective-permute-start.1 = (bf16[64,3200]{1,0:T(8,128)(2,1)S(1)}, bf16[64,3200]{1,0:T(8,128)(2,1)S(1)}, u32[]{:S(2)}, u32[]{:S(2)}) collective-permute-start(bf16[64,3200]{1,0:T(8,128)(2,1)S(1)} %get-tuple-element.18), channel_id=1, source_target_pairs={{0,24},{1,9},{2,26},{3,11},{4,28},{5,13},{6,30},{7,15},{8,0},{9,17... | collective-permute-start | bytes 1228808 | tf_op jit(solution)/shard_map/ppermute | solution.py:73
  78.0 28.1 %copy-start.3 = (f32[16,128]{1,0:T(8,128)S(1)}, f32[16,128]{1,0:T(8,128)}, u32[]{:S(2)}) copy-start(f32[16,128]{1,0:T(8,128)} %get-tuple-element.11) | copy-start | bytes 24580
  106.1 13.0 %copy-start.4 = (f32[128]{0:T(128)}, f32[128]{0:T(128)S(1)}, u32[]{:S(2)}) copy-start(f32[128]{0:T(128)S(1)} %get-tuple-element.13) | copy-start | bytes 1540
